TPU v7x, 32 devices: a whole 2x2x4 slice. The times are simulated.
32 devices in a mesh: seq: 8 (over z, x), batch: 4 (over y, core).
Axes of the slice: x: 2, y: 2, z: 4, core: 2. Of those that a mesh axis runs over, the one named last changes fastest.
Arguments:
- inputs: bfloat16 [8, 4096, 768], P('batch', 'seq'), may hold values from -6 to 6
- global_inputs: bfloat16 [8, 128, 768], P('batch'), may hold values from -6 to 6
- lengths: int32 [8], P('batch'), may hold values from 2048 to 4096, as said below
- first_gain: float32 [768], replicated, may hold values from 0.5 to 1.5
- first_shift: float32 [768], replicated, may hold values from -3 to 3
- qkv_weight: bfloat16 [768, 2304], replicated, may hold values from -0.3125 to 0.3125
- out_weight: bfloat16 [768, 768], replicated, may hold values from -0.875 to 0.875
- second_gain: float32 [768], replicated, may hold values from 0.5 to 1.5
- second_shift: float32 [768], replicated, may hold values from -3 to 3
- inner_weight: bfloat16 [768, 3072], replicated, may hold values from -0.21875 to 0.21875
- inner_bias: float32 [3072], replicated, may hold values from -3 to 3
- outer_weight: bfloat16 [3072, 768], replicated, may hold values from -0.109375 to 0.109375
- output_cotangent: bfloat16 [8, 4096, 768], P('batch', 'seq'), may hold values from -6 to 6
- global_cotangent: bfloat16 [8, 128, 768], P('batch'), may hold values from -6 to 6
Outputs:
- layer_output: bfloat16 [8, 4096, 768], P('batch', 'seq')
- global_output: bfloat16 [8, 128, 768], P('batch')
- input_grad: bfloat16 [8, 4096, 768], P('batch', 'seq')
- global_input_grad: bfloat16 [8, 128, 768], P('batch')
- first_gain_grad: float32 [768], P('seq')
- first_shift_grad: float32 [768], P('seq')
- qkv_weight_grad: float32 [768, 2304], P('seq')
- out_weight_grad: float32 [768, 768], P('seq')
- second_gain_grad: float32 [768], P('seq')
- second_shift_grad: float32 [768], P('seq')
- inner_weight_grad: float32 [768, 3072], P('seq')
- inner_bias_grad: float32 [3072], P('seq')
- outer_weight_grad: float32 [3072, 768], P('seq')
Inputs may be any that keep to these rules, and one draw needn't show every extreme that they name: `lengths`: rows come 2 to a batch index; in each such group one row, drawn from the seed, has length exactly 4096, the others any length in the range.
All inputs are finite; a program needn't handle non-finite values.
Results may differ from a plain program's by a relative error of at most 0.015.
Values may be sent and summed in bfloat16 or wider, within the bound.
A program may use at most 320 MiB of HBM per device.

v0:
```python
import jax
import jax.numpy as jnp
from jax import lax
from jax.sharding import PartitionSpec as P

HEADS = 12


EPS = 1e-05
NEG = -1e30


def padded(cells, sides, width):
    for axis, dim in sides:
        count = lax.axis_size(axis)
        ends = count - 1
        head = lax.slice_in_dim(cells, 0, width, axis=dim)
        tail = lax.slice_in_dim(cells, cells.shape[dim] - width, cells.shape[dim], axis=dim)
        cells = jnp.concatenate(
            [
                lax.ppermute(tail, axis, [(i, (i + 1) % count) for i in range(ends)]),
                cells,
                lax.ppermute(head, axis, [((i + 1) % count, i) for i in range(ends)]),
            ],
            axis=dim,
        )
    return cells


def merged(part, axis, combine):
    gathered = jax.tree.map(lambda a: lax.all_gather(a, axis), part)

    def take(source):
        return jax.tree.map(lambda a: lax.dynamic_index_in_dim(a, source, 0, False), gathered)

    return lax.fori_loop(
        1, lax.axis_size(axis), lambda source, state: combine(state, take(source)), take(0)
    )


def passed_along(x, axis, by):
    devices = lax.axis_size(axis)
    pairs = [(i, i + by) for i in range(devices) if 0 <= i + by < devices]
    return lax.ppermute(x, axis, pairs)


def norm_apply(values, gain_vec, shift_vec):
    average = jnp.mean(values, axis=-1, keepdims=True)
    centred = values - average
    variance = jnp.mean(centred * centred, axis=-1, keepdims=True)
    return centred * lax.rsqrt(variance + EPS) * gain_vec + shift_vec


def gelu_apply(values):
    return jax.nn.gelu(values, approximate=False)


def mixdot(pattern, left_op, right_op):
    return jnp.einsum(pattern, left_op, right_op, preferred_element_type=jnp.float32)


def merge_stats(first_pair, second_pair):
    first_peak, first_total = first_pair
    second_peak, second_total = second_pair
    highest = jnp.maximum(first_peak, second_peak)
    return (
        highest,
        first_total * jnp.exp(first_peak - highest) + second_total * jnp.exp(second_peak - highest),
    )


def ffn_forward(residual, second_gain, second_shift, inner_weight, inner_bias, outer_weight):
    normed_second = norm_apply(residual, second_gain, second_shift).astype(jnp.bfloat16)
    inner = mixdot("rtd,df->rtf", normed_second, inner_weight) + inner_bias
    hidden = gelu_apply(inner).astype(jnp.bfloat16)
    return (residual + mixdot("rtf,fd->rtd", hidden, outer_weight), (normed_second, inner, hidden))


def ffn_backward(
    cotangent, residual, saved_acts, second_gain, second_shift, inner_weight, outer_weight
):
    normed_second, inner, hidden = saved_acts
    branch_grad = cotangent.astype(jnp.bfloat16)
    hidden_grad = mixdot("rtd,fd->rtf", branch_grad, outer_weight)
    unused_value, gelu_back = jax.vjp(gelu_apply, inner)
    inner_grad = gelu_back(hidden_grad)[0].astype(jnp.bfloat16)
    second_grad = mixdot("rtf,df->rtd", inner_grad, inner_weight)
    unused_norm, norm_back = jax.vjp(norm_apply, residual, second_gain, second_shift)
    through, gain_grad, shift_grad = norm_back(second_grad)
    outer_grad = mixdot("rtf,rtd->fd", hidden, branch_grad)
    inner_wgrad = mixdot("rtd,rtf->df", normed_second, inner_grad)
    bias_grad = jnp.sum(inner_grad.astype(jnp.float32), axis=(0, 1))
    return (cotangent + through, (gain_grad, shift_grad, inner_wgrad, bias_grad, outer_grad))


def local_scores(queries, ext_keys, global_keys, key_ok, score_scale):
    near_scores = score_scale * mixdot("rjqhd,rjkhd->rjhqk", queries, ext_keys)
    near_scores = jnp.where(key_ok[:, :, None, None, :], near_scores, NEG)
    far_scores = score_scale * mixdot("rjqhd,rghd->rjhqg", queries, global_keys)
    return (near_scores, far_scores)


def global_scores(global_queries, own_keys, global_keys, valid_rows, score_scale):
    spread = score_scale * mixdot("rghd,rthd->rhgt", global_queries, own_keys)
    spread = jnp.where(valid_rows[:, None, None, :] > 0, spread, NEG)
    among_scores = score_scale * mixdot("rghd,rkhd->rhgk", global_queries, global_keys)
    return (spread, among_scores)


def body(
    inputs,
    global_inputs,
    lengths,
    first_gain,
    first_shift,
    qkv_weight,
    out_weight,
    second_gain,
    second_shift,
    inner_weight,
    inner_bias,
    outer_weight,
    output_cotangent,
    global_cotangent,
):
    row_count, block_len, width = inputs.shape
    half_block = block_len // 2
    global_count = global_inputs.shape[1]
    head_count = HEADS
    head_size = width // head_count
    score_scale = head_size ** (-0.5)
    seq_index = lax.axis_index("seq")
    on_first = (seq_index == 0).astype(jnp.float32)
    positions = seq_index * block_len + jnp.arange(block_len, dtype=jnp.int32)
    valid_rows = (positions[None, :] < lengths[:, None]).astype(jnp.float32)
    ext_positions = seq_index * block_len - half_block + jnp.arange(2 * block_len, dtype=jnp.int32)
    ext_valid = (ext_positions[None, :] >= 0) & (ext_positions[None, :] < lengths[:, None])
    tokens = inputs.astype(jnp.float32)
    globals_in = global_inputs.astype(jnp.float32)
    normed = norm_apply(tokens, first_gain, first_shift).astype(jnp.bfloat16)
    global_normed = norm_apply(globals_in, first_gain, first_shift).astype(jnp.bfloat16)
    projected = mixdot("rtd,de->rte", normed, qkv_weight).astype(jnp.bfloat16)
    global_projected = mixdot("rgd,de->rge", global_normed, qkv_weight).astype(jnp.bfloat16)
    extended = padded(projected[:, :, width:], (("seq", 1),), half_block)
    queries = projected[:, :, :width].reshape(row_count, 2, half_block, head_count, head_size)
    ext_keys = extended[:, :, :width].reshape(row_count, 2, block_len, head_count, head_size)
    ext_values = extended[:, :, width:].reshape(row_count, 2, block_len, head_count, head_size)
    key_ok = ext_valid.reshape(row_count, 2, block_len)
    own_keys = projected[:, :, width : 2 * width].reshape(
        row_count, block_len, head_count, head_size
    )
    own_values = projected[:, :, 2 * width :].reshape(row_count, block_len, head_count, head_size)
    global_queries = global_projected[:, :, :width].reshape(
        row_count, global_count, head_count, head_size
    )
    global_keys = global_projected[:, :, width : 2 * width].reshape(
        row_count, global_count, head_count, head_size
    )
    global_values = global_projected[:, :, 2 * width :].reshape(
        row_count, global_count, head_count, head_size
    )
    near_scores, far_scores = local_scores(queries, ext_keys, global_keys, key_ok, score_scale)
    highest = jnp.maximum(jnp.max(near_scores, axis=-1), jnp.max(far_scores, axis=-1))[..., None]
    near_exp = jnp.exp(near_scores - highest)
    far_exp = jnp.exp(far_scores - highest)
    denominator = jnp.sum(near_exp, axis=-1, keepdims=True) + jnp.sum(
        far_exp, axis=-1, keepdims=True
    )
    local_lse = highest + jnp.log(denominator)
    near_weights = (near_exp / denominator).astype(jnp.bfloat16)
    far_weights = (far_exp / denominator).astype(jnp.bfloat16)
    local_mix = mixdot("rjhqk,rjkhd->rjqhd", near_weights, ext_values) + mixdot(
        "rjhqg,rghd->rjqhd", far_weights, global_values
    )
    attended = local_mix.reshape(row_count, block_len, width).astype(jnp.bfloat16)
    spread, among_scores = global_scores(
        global_queries, own_keys, global_keys, valid_rows, score_scale
    )
    part_peak = jnp.max(spread, axis=-1)
    part_total = jnp.sum(
        jnp.exp(spread - part_peak[..., None]) * valid_rows[:, None, None, :], axis=-1
    )
    merged_peak, merged_total = merged((part_peak, part_total), "seq", merge_stats)
    full_peak = jnp.maximum(merged_peak, jnp.max(among_scores, axis=-1))
    full_total = merged_total * jnp.exp(merged_peak - full_peak) + jnp.sum(
        jnp.exp(among_scores - full_peak[..., None]), axis=-1
    )
    global_lse = (full_peak + jnp.log(full_total))[..., None]
    spread_weights = jnp.exp(spread - global_lse).astype(jnp.bfloat16)
    partial_value = mixdot("rhgt,rthd->rghd", spread_weights, own_values).reshape(
        row_count, global_count, width
    )
    summed = lax.psum(partial_value, "seq")
    among_weights = jnp.exp(among_scores - global_lse).astype(jnp.bfloat16)
    among_mix = mixdot("rhgk,rkhd->rghd", among_weights, global_values).reshape(
        row_count, global_count, width
    )
    global_attended = (summed + among_mix).astype(jnp.bfloat16)
    residual = tokens + mixdot("rtd,de->rte", attended, out_weight)
    global_residual = globals_in + mixdot("rtd,de->rte", global_attended, out_weight)
    final, saved_local = ffn_forward(
        residual, second_gain, second_shift, inner_weight, inner_bias, outer_weight
    )
    global_final, saved_global = ffn_forward(
        global_residual, second_gain, second_shift, inner_weight, inner_bias, outer_weight
    )
    layer_output = (final * valid_rows[..., None]).astype(jnp.bfloat16)
    global_output = global_final.astype(jnp.bfloat16)
    cotangent = output_cotangent.astype(jnp.float32) * valid_rows[..., None]
    residual_grad, local_terms = ffn_backward(
        cotangent, residual, saved_local, second_gain, second_shift, inner_weight, outer_weight
    )
    global_residual_grad, global_terms = ffn_backward(
        global_cotangent.astype(jnp.float32),
        global_residual,
        saved_global,
        second_gain,
        second_shift,
        inner_weight,
        outer_weight,
    )
    ffn_grads = jax.tree.map(
        lambda first_term, second_term: first_term + on_first * second_term,
        local_terms,
        global_terms,
    )
    projection_grad = residual_grad.astype(jnp.bfloat16)
    global_projection_grad = global_residual_grad.astype(jnp.bfloat16)
    out_grad_sum = mixdot("rtd,rte->de", attended, projection_grad) + on_first * mixdot(
        "rtd,rte->de", global_attended, global_projection_grad
    )
    attended_grad = mixdot("rte,de->rtd", projection_grad, out_weight).astype(jnp.bfloat16)
    global_attended_grad = mixdot("rte,de->rtd", global_projection_grad, out_weight).astype(
        jnp.bfloat16
    )
    local_grad = attended_grad.reshape(row_count, 2, half_block, head_count, head_size)
    near_scores, far_scores = local_scores(queries, ext_keys, global_keys, key_ok, score_scale)
    near_probs = jnp.exp(near_scores - local_lse)
    far_probs = jnp.exp(far_scores - local_lse)
    near_dp = mixdot("rjqhd,rjkhd->rjhqk", local_grad, ext_values)
    far_dp = mixdot("rjqhd,rghd->rjhqg", local_grad, global_values)
    delta_sum = jnp.sum(near_probs * near_dp, axis=-1, keepdims=True) + jnp.sum(
        far_probs * far_dp, axis=-1, keepdims=True
    )
    near_ds = (near_probs * (near_dp - delta_sum)).astype(jnp.bfloat16)
    far_ds = (far_probs * (far_dp - delta_sum)).astype(jnp.bfloat16)
    query_grad = score_scale * (
        mixdot("rjhqk,rjkhd->rjqhd", near_ds, ext_keys)
        + mixdot("rjhqg,rghd->rjqhd", far_ds, global_keys)
    )
    ext_key_grad = score_scale * mixdot("rjhqk,rjqhd->rjkhd", near_ds, queries)
    ext_value_grad = mixdot("rjhqk,rjqhd->rjkhd", near_probs.astype(jnp.bfloat16), local_grad)
    far_key_part = score_scale * mixdot("rjhqg,rjqhd->rghd", far_ds, queries)
    far_value_part = mixdot("rjhqg,rjqhd->rghd", far_probs.astype(jnp.bfloat16), local_grad)
    ext_grad = jnp.concatenate(
        [
            ext_key_grad.reshape(row_count, 2 * block_len, width),
            ext_value_grad.reshape(row_count, 2 * block_len, width),
        ],
        axis=-1,
    )
    from_next = passed_along(ext_grad[:, :half_block].astype(jnp.bfloat16), "seq", -1).astype(
        jnp.float32
    )
    from_prev = passed_along(
        ext_grad[:, half_block + block_len :].astype(jnp.bfloat16), "seq", 1
    ).astype(jnp.float32)
    own_grad = ext_grad[:, half_block : half_block + block_len] + jnp.concatenate(
        [from_prev, from_next], axis=1
    )
    global_grad = global_attended_grad.reshape(row_count, global_count, head_count, head_size)
    spread, among_scores = global_scores(
        global_queries, own_keys, global_keys, valid_rows, score_scale
    )
    spread_probs = jnp.exp(spread - global_lse)
    among_probs = jnp.exp(among_scores - global_lse)
    spread_dp = mixdot("rghd,rthd->rhgt", global_grad, own_values)
    among_dp = mixdot("rghd,rkhd->rhgk", global_grad, global_values)
    part_delta = jnp.sum(spread_probs * spread_dp, axis=-1)
    global_delta = lax.psum(part_delta, "seq") + jnp.sum(among_probs * among_dp, axis=-1)
    spread_ds = (spread_probs * (spread_dp - global_delta[..., None])).astype(jnp.bfloat16)
    among_ds = (among_probs * (among_dp - global_delta[..., None])).astype(jnp.bfloat16)
    global_query_part = score_scale * mixdot("rhgt,rthd->rghd", spread_ds, own_keys)
    own_key_extra = score_scale * mixdot("rhgt,rghd->rthd", spread_ds, global_queries)
    own_value_extra = mixdot("rhgt,rghd->rthd", spread_probs.astype(jnp.bfloat16), global_grad)
    far_pairs = jnp.concatenate(
        [
            far_key_part.reshape(row_count, global_count, width),
            far_value_part.reshape(row_count, global_count, width),
        ],
        axis=-1,
    )
    query_summed, pairs_summed = lax.psum(
        (global_query_part.reshape(row_count, global_count, width), far_pairs), "seq"
    )
    among_query = score_scale * mixdot("rhgk,rkhd->rghd", among_ds, global_keys)
    among_key = score_scale * mixdot("rhgk,rghd->rkhd", among_ds, global_queries)
    among_value = mixdot("rhgk,rghd->rkhd", among_probs.astype(jnp.bfloat16), global_grad)
    among_pairs = jnp.concatenate(
        [
            among_key.reshape(row_count, global_count, width),
            among_value.reshape(row_count, global_count, width),
        ],
        axis=-1,
    )
    global_qkv_grad = jnp.concatenate(
        [
            query_summed + among_query.reshape(row_count, global_count, width),
            pairs_summed + among_pairs,
        ],
        axis=-1,
    ).astype(jnp.bfloat16)
    own_extra = jnp.concatenate(
        [
            own_key_extra.reshape(row_count, block_len, width),
            own_value_extra.reshape(row_count, block_len, width),
        ],
        axis=-1,
    )
    own_qkv_grad = jnp.concatenate(
        [query_grad.reshape(row_count, block_len, width), own_grad + own_extra], axis=-1
    ).astype(jnp.bfloat16)
    first_grad = mixdot("rte,de->rtd", own_qkv_grad, qkv_weight)
    global_first_grad = mixdot("rte,de->rtd", global_qkv_grad, qkv_weight)
    unused_first, first_back = jax.vjp(norm_apply, tokens, first_gain, first_shift)
    token_grad, gain_local, shift_local = first_back(first_grad)
    unused_global, global_back = jax.vjp(norm_apply, globals_in, first_gain, first_shift)
    global_token_grad, gain_global, shift_global = global_back(global_first_grad)
    input_grad = (residual_grad + token_grad).astype(jnp.bfloat16)
    global_input_grad = (global_residual_grad + global_token_grad).astype(jnp.bfloat16)
    first_gain_sum = gain_local + on_first * gain_global
    first_shift_sum = shift_local + on_first * shift_global
    qkv_grad_sum = mixdot("rtd,rte->de", normed, own_qkv_grad) + on_first * mixdot(
        "rtd,rte->de", global_normed, global_qkv_grad
    )
    all_parts = (
        lax.psum_scatter(first_gain_sum, "seq", scatter_dimension=0, tiled=True),
        lax.psum_scatter(first_shift_sum, "seq", scatter_dimension=0, tiled=True),
        lax.psum_scatter(qkv_grad_sum, "seq", scatter_dimension=0, tiled=True),
        lax.psum_scatter(out_grad_sum, "seq", scatter_dimension=0, tiled=True),
        lax.psum_scatter(ffn_grads[0], "seq", scatter_dimension=0, tiled=True),
        lax.psum_scatter(ffn_grads[1], "seq", scatter_dimension=0, tiled=True),
        lax.psum_scatter(ffn_grads[2], "seq", scatter_dimension=0, tiled=True),
        lax.psum_scatter(ffn_grads[3], "seq", scatter_dimension=0, tiled=True),
        lax.psum_scatter(ffn_grads[4], "seq", scatter_dimension=0, tiled=True),
    )
    every_grad = (
        lax.psum(all_parts[0].astype(jnp.bfloat16), "batch").astype(jnp.float32),
        lax.psum(all_parts[1].astype(jnp.bfloat16), "batch").astype(jnp.float32),
        lax.psum(all_parts[2].astype(jnp.bfloat16), "batch").astype(jnp.float32),
        lax.psum(all_parts[3].astype(jnp.bfloat16), "batch").astype(jnp.float32),
        lax.psum(all_parts[4].astype(jnp.bfloat16), "batch").astype(jnp.float32),
        lax.psum(all_parts[5].astype(jnp.bfloat16), "batch").astype(jnp.float32),
        lax.psum(all_parts[6].astype(jnp.bfloat16), "batch").astype(jnp.float32),
        lax.psum(all_parts[7].astype(jnp.bfloat16), "batch").astype(jnp.float32),
        lax.psum(all_parts[8].astype(jnp.bfloat16), "batch").astype(jnp.float32),
    )
    return (
        layer_output,
        global_output,
        input_grad,
        global_input_grad,
        every_grad[0],
        every_grad[1],
        every_grad[2],
        every_grad[3],
        every_grad[4],
        every_grad[5],
        every_grad[6],
        every_grad[7],
        every_grad[8],
    )


def solution(mesh):
    placed = (
        P("batch", "seq", None),
        P("batch", None, None),
        P("batch"),
        P(),
        P(),
        P(),
        P(),
        P(),
        P(),
        P(),
        P(),
        P(),
        P("batch", "seq", None),
        P("batch", None, None),
    )
    return jax.shard_map(
        body,
        mesh=mesh,
        in_specs=placed,
        out_specs=(
            P("batch", "seq", None),
            P("batch", None, None),
            P("batch", "seq", None),
            P("batch", None, None),
            P("seq"),
            P("seq"),
            P("seq", None),
            P("seq", None),
            P("seq"),
            P("seq"),
            P("seq", None),
            P("seq"),
            P("seq", None),
        ),
        check_vma=False,
    )
```

profile of v0, /device:TPU:0, one launch (start us, length us, event | category | flops | bytes accessed | tf_op | source)
XLA Modules:
  0.0 1345.4 jit_solution(11336812897920702606)
XLA Ops:
  18.4 6.0 collective-permute-start
  49.6 67.5 %all-gather = f32[16,12,128]{2,1,0:T(8,128)S(1)} all-gather(f32[2,12,128]{2,1,0:T(8,128)S(1)} %get-tuple-element.225), channel_id=2, replica_groups=mesh['seq'=8,'batch'=4] {'seq'}, dimensions={0}, use_global_device_ids=true | all-gather | bytes 110592 | tf_op jit(solution)/shard_map/all_gather | solution.py:31
  118.9 30.6 %all-gather.1 = f32[16,12,128]{2,1,0:T(8,128)S(1)} all-gather(f32[2,12,128]{2,1,0:T(8,128)S(1)} %multiply_reduce_fusion.2), channel_id=3, replica_groups=mesh['seq'=8,'batch'=4] {'seq'}, dimensions={0}, use_global_device_ids=true | all-gather | bytes 110592 | tf_op jit(solution)/shard_map/all_gather | solution.py:31
  150.1 9.6 while.17
  162.9 5.7 fusion.167
  184.3 5.5 bitcast_reduce_fusion
  189.8 51.1 %all-reduce.13.cloned.1.call-done = f32[2,128,768]{1,2,0:T(8,128)} async-done(((f32[2,128,768]{1,2,0:T(8,128)}), f32[2,128,768]{1,2,0:T(8,128)}) %all-reduce.13.cloned.1.call-update) | async-done | bytes 786448 | tf_op jit(solution)/shard_map/psum | solution.py:193
  250.4 7.9 multiply_convert_fusion.3
  272.6 6.1 fusion.165
  283.4 36.2 %psum.92 = f32[2,12,128]{2,1,0:T(8,128)} all-reduce(f32[2,12,128]{2,1,0:T(8,128)} %get-tuple-element.238), channel_id=1, replica_groups=mesh['seq'=8,'batch'=4] {'seq'}, use_global_device_ids=true, to_apply=%region_26.27 | all-reduce | flops 3072 | bytes 24576 | tf_op jit(solution)/shard_map/psum | solution.py:280
  320.3 6.8 multiply_convert_fusion.2
  366.2 6.2 reshape.361
  377.0 6.2 reshape.363
  383.3 15.3 %fusion.15 = (f32[2,2,12,256]{3,2,1,0:T(8,128)S(1)}, f32[2,2,12,256,512]{4,3,2,1,0:T(8,128)}) fusion(pred[2,2,512]{2,1,0:T(4,128)(4,1)S(1)} %copy-done.71, bf16[2,2,512,12,64]{2,1,4,3,0:T(2,128)(2,1)} %reshape.363, bf16[2,2,256,12,64]{2,1,4,3,0:T(2,128)(2,1)} %reshape.362), kind=kOutput, calls=%fused_computation.42 | convolution fusion | flops 824168448 | bytes 29935616 | tf_op jit(solution)/shard_map/rjqhd,rjkhd->rjhqk/dot_general | solution.py:59
  398.6 12.0 fusion.2
  417.5 12.0 fusion.74
  441.1 15.5 %fusion.88 = (u8[512,3072]{1,0:T(8,128)(4,1)S(1)}, u8[512,3072]{1,0:T(8,128)(4,1)S(1)}, f32[2,512,3072]{2,1,0:T(8,128)}) fusion(f32[3072]{0:T(1024)S(1)} %copy-done.108, bf16[768,3072]{1,0:T(8,128)(2,1)} %param.25, f32[2,512,768]{2,1,0:T(8,128)S(1)} %get-tuple-element.223, f32[768]{0:T(1024)S(1)} %copy-done.63, f32[768]{0:T(1024)S(1)} %copy-done.58, ...), kind=kOutput, calls=%fused_computation.160 | convolution fusion | flops 4876664832 | bytes 23619584 | tf_op jit(solution)/shard_map/rtd,df->rtf/dot_general | solution.py:59
  456.5 31.9 %multiply_convert_fusion.1 = (bf16[2,512,3072]{2,1,0:T(8,128)(2,1)}, f32[2,512,3072]{2,1,0:T(8,128)}) fusion(f32[2,512,3072]{2,1,0:T(8,128)} %get-tuple-element.224, f32[3072]{0:T(1024)S(1)} %copy-done.108, u8[512,3072]{1,0:T(8,128)(4,1)S(1)} %get-tuple-element.149, u8[512,3072]{1,0:T(8,128)(4,1)S(1)} %get-tuple-element.148), kind=kLoop, calls=%fused_computation.28 | loop fusion | flops 223346688 | bytes 34615296 | tf_op jit(solution)/shard_map/convert_element_type | solution.py:75
  488.5 17.5 %convert_reduce_fusion = (f32[3072]{0:T(1024)}, bf16[2,512,3072]{2,1,0:T(8,128)(2,1)}) fusion(f32[2,512,3072]{2,1,0:T(8,128)} %get-tuple-element.203, bf16[3072,768]{1,0:T(8,128)(2,1)} %param.27, bf16[2,512,768]{2,1,0:T(8,128)(2,1)} %param.28, f32[2,512]{1,0:T(2,128)S(1)} %copy-done.84, f32[2,512,3072]{2,1,0:T(8,128)} %get-tuple-element.224, f32[3072]{0:T(1024)} %param.26), kind=kOutput, calls=%fused_computation.25 | convolution fusion | flops 4887671808 | bytes 37777408 | tf_op jit(solution)/shard_map/rtd,fd->rtf/dot_general | solution.py:59
  506.0 10.7 multiply_reduce_fusion.3
  529.5 23.9 %multiply_reduce_fusion = (f32[2,2,12,256]{3,2,1,0:T(8,128)}, f32[2,2,12,256,512]{4,3,2,1,0:T(8,128)}) fusion(f32[2,2,12,256]{3,2,1,0:T(8,128)} %copy-done.55, f32[2,2,12,256,512]{4,3,2,1,0:T(8,128)} %get-tuple-element.219, pred[2,2,512]{2,1,0:T(4,128)(4,1)S(1)} %copy-done.71, bf16[2,2,512,12,64]{2,1,4,3,0:T(2,128)(2,1)} %reshape.361, ...), kind=kOutput, calls=%fused_computation.6 | convolution fusion | flops 836751360 | bytes 55150592 | tf_op jit(solution)/shard_map/rjqhd,rjkhd->rjhqk/dot_general | solution.py:59
  560.7 8.0 fusion.23
  568.8 21.9 %multiply_convert_fusion = bf16[2,2,12,256,512]{4,3,2,1,0:T(8,128)(2,1)} fusion(f32[2,2,12,256,512]{4,3,2,1,0:T(8,128)} %get-tuple-element.234, f32[2,2,12,256]{3,2,1,0:T(8,128)S(1)} %copy_add_fusion, f32[2,2,12,256]{3,2,1,0:T(8,128)S(1)} %copy-done.56, f32[2,2,12,256,512]{4,3,2,1,0:T(8,128)} %get-tuple-element.219, pred[2,2,512]{2,1,0:T(4,128)(4,1)S(1)} %copy-done.71), kind=kLoop, calls=%fused_computation.5 | loop fusion | flops 37748736 | bytes 63014912 | tf_op jit(solution)/shard_map/convert_element_type | solution.py:245
  602.9 14.0 %fusion.97 = f32[2,2,512,12,64]{2,4,3,1,0:T(8,128)} fusion(f32[2,2,12,256]{3,2,1,0:T(8,128)} %copy-done.55, f32[2,2,12,256,512]{4,3,2,1,0:T(8,128)} %get-tuple-element.219, pred[2,2,512]{2,1,0:T(4,128)(4,1)S(1)} %copy-done.71, bf16[2,2,256,12,64]{2,1,4,3,0:T(2,128)(2,1)} %reshape.371), kind=kOutput, calls=%fused_computation.169 | convolution fusion | flops 830472192 | bytes 33081344 | tf_op jit(solution)/shard_map/rjhqk,rjqhd->rjkhd/dot_general | solution.py:59
  616.9 10.5 copy.239
  627.4 9.2 reshape.374
  636.6 6.8 copy.241
  643.4 9.9 multiply_bitcast_fusion
  653.3 10.4 copy.237
  663.7 9.2 reshape.373
  672.9 6.7 copy.240
  685.3 8.0 fusion.4
  708.9 11.5 fusion.71
  731.3 32.1 %collective-permute-done.2 = bf16[2,256,1536]{2,1,0:T(8,128)(2,1)} collective-permute-done((bf16[2,256,1536]{2,1,0:T(8,128)(2,1)}, bf16[2,256,1536]{2,1,0:T(8,128)(2,1)}, u32[]{:S(2)}, u32[]{:S(2)}) %collective-permute-start.2) | collective-permute-done | bytes 1572896 | tf_op jit(solution)/shard_map/ppermute | solution.py:44
  763.4 6.3 fusion.22
  771.4 7.1 fusion.89
  783.1 7.2 fusion.18
  790.4 8.2 fusion.120
  798.7 5.1 fusion.16
  804.5 9.2 fusion.169
  813.8 5.3 fusion.17
  821.6 5.3 fusion.132
  828.2 9.6 multiply_convert_fusion.4
  852.3 83.4 %reduce-scatter.5.cloned.1.call-done = f32[96,2304]{1,0:T(8,128)} async-done(((f32[768,2304]{1,0:T(8,128)}), f32[96,2304]{1,0:T(8,128)}) %reduce-scatter.5.cloned.1.call-update) | async-done | bytes 884752 | tf_op jit(solution)/shard_map/reduce_scatter | solution.py:339
  937.7 164.4 %reduce-scatter.11.cloned.1.call-done = f32[384,768]{1,0:T(8,128)} async-done(((f32[3072,768]{1,0:T(8,128)}), f32[384,768]{1,0:T(8,128)}) %reduce-scatter.11.cloned.1.call-update) | async-done | bytes 1179664 | tf_op jit(solution)/shard_map/reduce_scatter | solution.py:345
  1104.3 164.3 %reduce-scatter.9.cloned.1.call-done = f32[96,3072]{1,0:T(8,128)} async-done(((f32[768,3072]{1,0:T(8,128)}), f32[96,3072]{1,0:T(8,128)}) %reduce-scatter.9.cloned.1.call-update) | async-done | bytes 1179664 | tf_op jit(solution)/shard_map/reduce_scatter | solution.py:343
  1274.2 36.4 %all-reduce.5 = (bf16[768]{0:T(1024)(128)(2,1)}, bf16[768]{0:T(1024)(128)(2,1)}, bf16[768]{0:T(1024)(128)(2,1)}, bf16[768]{0:T(1024)(128)(2,1)S(1)}, bf16[3072]{0:T(1024)(128)(2,1)}) all-reduce(f32[768]{0:T(1024)} %get-tuple-element.251, f32[768]{0:T(1024)} %get-tuple-element.250, ...), channel_id=4, replica_groups=mesh['seq'=8,'batch'=4] {'seq'}, use_global_device_ids=true, to_apply=%region_36.37.clone | all-reduce | flops 6144 | bytes 36864
  1315.7 6.4 all-reduce.7
  (436 shorter events, 277.5 us)
Async XLA Ops:
  7.2 233.6 %all-reduce.13.cloned.1.call-start = ((), (), s32[]{:S(2)}) async-start(), calls=%async_computation.4 | async-start | bytes 1572864 | tf_op jit(solution)/shard_map/psum | solution.py:193
  16.3 9.4 copy-start.11
  18.4 336.7 %collective-permute-start = (bf16[2,256,1536]{2,1,0:T(8,128)(2,1)}, bf16[2,256,1536]{2,1,0:T(8,128)(2,1)}, u32[]{:S(2)}, u32[]{:S(2)}) collective-permute-start(bf16[2,256,1536]{2,1,0:T(8,128)(2,1)} %get-tuple-element.211), channel_id=1, source_target_pairs={{0,4},{4,8},{8,12},{12,16},{16,20},{20,24},{24,28},{1,5},{5,9},{9,... | collective-permute-start | bytes 4718600 | tf_op jit(solution)/shard_map/ppermute | solution.py:21
  24.3 330.7 %collective-permute-start.1 = (bf16[2,256,1536]{2,1,0:T(8,128)(2,1)}, bf16[2,256,1536]{2,1,0:T(8,128)(2,1)}, u32[]{:S(2)}, u32[]{:S(2)}) collective-permute-start(bf16[2,256,1536]{2,1,0:T(8,128)(2,1)} %get-tuple-element.212), channel_id=1, source_target_pairs={{4,0},{8,4},{12,8},{16,12},{20,16},{24,20},{28,24},{5,1},{9,5},{13... | collective-permute-start | bytes 4718600 | tf_op jit(solution)/shard_map/ppermute | solution.py:23
  44.0 73.1 %copy-start.73 = (pred[2,512]{1,0:T(4,128)(4,1)}, pred[2,512]{1,0:T(4,128)(4,1)S(1)}, u32[]{:S(2)}) copy-start(pred[2,512]{1,0:T(4,128)(4,1)S(1)} %get-tuple-element.216) | copy-start | bytes 3076
  44.0 73.1 %copy-start.83 = (f32[2,512]{1,0:T(2,128)}, f32[2,512]{1,0:T(2,128)S(1)}, u32[]{:S(2)}) copy-start(f32[2,512]{1,0:T(2,128)S(1)} %get-tuple-element.217) | copy-start | bytes 12292
  49.6 69.3 %copy-start.1 = (f32[2,12,128,512]{3,2,1,0:T(8,128)}, f32[2,12,128,512]{3,2,1,0:T(8,128)S(1)}, u32[]{:S(2)}) copy-start(f32[2,12,128,512]{3,2,1,0:T(8,128)S(1)} %get-tuple-element.226) | copy-start | bytes 18874372
  168.7 609.8 %all-reduce.15.cloned.1.call-start = ((), (), s32[]{:S(2)}) async-start(), calls=%async_computation.9 | async-start | bytes 4718592 | tf_op jit(solution)/shard_map/psum | solution.py:293
  243.1 15.1 %slice-start.8 = ((s8[4718592]{0:T(1024)(128)(4,1)}), s8[4194304]{0:T(1024)(128)(4,1)S(1)}, s32[]{:S(2)}) async-start(s8[4718592]{0:T(1024)(128)(4,1)} %bitcast.314), calls=%async_computation.19 | async-start | bytes 8388608
  245.2 18.0 %copy-start.18 = (f32[2,128,768]{2,1,0:T(8,128)}, f32[2,128,768]{2,1,0:T(8,128)S(1)}, u32[]{:S(2)}) copy-start(f32[2,128,768]{2,1,0:T(8,128)S(1)} %get-tuple-element.230) | copy-start | bytes 2359300
  245.2 18.0 %copy-start.103 = (f32[2,128]{1,0:T(2,128)}, f32[2,128]{1,0:T(2,128)S(1)}, u32[]{:S(2)}) copy-start(f32[2,128]{1,0:T(2,128)S(1)} %broadcast_multiply_fusion.2) | copy-start | bytes 3076
  245.5 17.7 %copy-start.105 = (f32[2,128]{1,0:T(2,128)}, f32[2,128]{1,0:T(2,128)S(1)}, u32[]{:S(2)}) copy-start(f32[2,128]{1,0:T(2,128)S(1)} %fusion.173) | copy-start | bytes 3076
  245.5 12.7 slice-start.9
  250.3 10.7 slice-start.6
  268.6 10.1 slice-start.4
  383.2 15.3 %copy-start.72 = (f32[2,2,12,256]{3,1,2,0:T(2,128)S(1)}, f32[2,2,12,256]{3,1,2,0:T(2,128)}, u32[]{:S(2)}) copy-start(f32[2,2,12,256]{3,1,2,0:T(2,128)} %get-tuple-element.220) | copy-start | bytes 147460
  383.2 32.3 %slice-start = ((s8[6291456]{0:T(1024)(128)(4,1)}), s8[2097152]{0:T(1024)(128)(4,1)S(1)}, s32[]{:S(2)}) async-start(s8[6291456]{0:T(1024)(128)(4,1)} %bitcast.275), calls=%async_computation.11 | async-start | bytes 4194304
  398.6 17.0 %slice-start.1 = ((s8[6291456]{0:T(1024)(128)(4,1)}), s8[4194304]{0:T(1024)(128)(4,1)S(1)}, s32[]{:S(2)}) async-start(s8[6291456]{0:T(1024)(128)(4,1)} %bitcast.275), calls=%async_computation.12 | async-start | bytes 8388608
  439.9 16.6 %copy-start.7 = (f32[2,512,768]{2,1,0:T(8,128)}, f32[2,512,768]{2,1,0:T(8,128)S(1)}, u32[]{:S(2)}) copy-start(f32[2,512,768]{2,1,0:T(8,128)S(1)} %get-tuple-element.223) | copy-start | bytes 9437188
  439.9 76.8 %copy-start.76 = (f32[2,512]{1,0:T(2,128)}, f32[2,512]{1,0:T(2,128)S(1)}, u32[]{:S(2)}) copy-start(f32[2,512]{1,0:T(2,128)S(1)} %broadcast_multiply_fusion) | copy-start | bytes 12292
  441.0 15.5 %copy-start.86 = (f32[2,512]{1,0:T(2,128)}, f32[2,512]{1,0:T(2,128)S(1)}, u32[]{:S(2)}) copy-start(f32[2,512]{1,0:T(2,128)S(1)} %fusion.171) | copy-start | bytes 12292
  456.5 31.9 %copy-start.84 = (f32[2,512]{1,0:T(2,128)S(1)}, f32[2,512]{1,0:T(2,128)}, u32[]{:S(2)}) copy-start(f32[2,512]{1,0:T(2,128)} %copy-done.83) | copy-start | bytes 12292
  506.0 10.7 copy-start.99
  506.0 10.7 copy-start.8
  506.0 10.7 copy-start.87
  529.5 23.9 %copy-start.12 = (bf16[2,2,256,12,64]{2,1,4,3,0:T(2,128)(2,1)S(1)}, bf16[2,2,256,12,64]{2,1,4,3,0:T(2,128)(2,1)}, u32[]{:S(2)}) copy-start(bf16[2,2,256,12,64]{2,1,4,3,0:T(2,128)(2,1)} %reshape.371) | copy-start | bytes 4718596
  529.5 23.9 %copy-start.60 = (f32[2,2,12,256]{3,1,2,0:T(2,128)S(1)}, f32[2,2,12,256]{3,1,2,0:T(2,128)}, u32[]{:S(2)}) copy-start(f32[2,2,12,256]{3,1,2,0:T(2,128)} %copy.229) | copy-start | bytes 147460
  560.7 30.0 %slice-start.2 = ((s8[6291456]{0:T(1024)(128)(4,1)}), s8[4194304]{0:T(1024)(128)(4,1)S(1)}, s32[]{:S(2)}) async-start(s8[6291456]{0:T(1024)(128)(4,1)} %bitcast.277), calls=%async_computation.13 | async-start | bytes 8388608
  568.8 21.9 %slice-start.3 = ((s8[6291456]{0:T(1024)(128)(4,1)}), s8[2097152]{0:T(1024)(128)(4,1)S(1)}, s32[]{:S(2)}) async-start(s8[6291456]{0:T(1024)(128)(4,1)} %bitcast.277), calls=%async_computation.14 | async-start | bytes 4194304
  568.8 21.9 %copy-start.61 = (f32[2,2,12,256]{3,1,2,0:T(2,128)S(1)}, f32[2,2,12,256]{3,1,2,0:T(2,128)}, u32[]{:S(2)}) copy-start(f32[2,2,12,256]{3,1,2,0:T(2,128)} %copy.229) | copy-start | bytes 147460
  602.9 247.8 %reduce-scatter.7.cloned.1.call-start = ((), (), s32[]{:S(2)}) async-start(), calls=%async_computation.6 | async-start | bytes 2654208 | tf_op jit(solution)/shard_map/reduce_scatter | solution.py:340
  685.2 250.5 %reduce-scatter.5.cloned.1.call-start = ((), (), s32[]{:S(2)}) async-start(), calls=%async_computation.5 | async-start | bytes 7962624 | tf_op jit(solution)/shard_map/reduce_scatter | solution.py:339
  697.1 66.4 %collective-permute-start.2 = (bf16[2,256,1536]{2,1,0:T(8,128)(2,1)}, bf16[2,256,1536]{2,1,0:T(8,128)(2,1)}, u32[]{:S(2)}, u32[]{:S(2)}) collective-permute-start(bf16[2,256,1536]{2,1,0:T(8,128)(2,1)} %get-tuple-element.204), channel_id=1, source_target_pairs={{0,4},{4,8},{8,12},{12,16},{16,20},{20,24},{24,28},{1,5},{5,9},{9,... | collective-permute-start | bytes 4718600 | tf_op jit(solution)/shard_map/ppermute | solution.py:44
  699.5 63.9 %collective-permute-start.3 = (bf16[2,256,1536]{2,1,0:T(8,128)(2,1)}, bf16[2,256,1536]{2,1,0:T(8,128)(2,1)}, u32[]{:S(2)}, u32[]{:S(2)}) collective-permute-start(bf16[2,256,1536]{2,1,0:T(8,128)(2,1)} %get-tuple-element.205), channel_id=1, source_target_pairs={{4,0},{8,4},{12,8},{16,12},{20,16},{24,20},{28,24},{5,1},{9,5},{13... | collective-permute-start | bytes 4718600 | tf_op jit(solution)/shard_map/ppermute | solution.py:44
  731.3 40.1 %copy-start.14 = (bf16[2,512,768]{2,1,0:T(8,128)(2,1)S(1)}, bf16[2,512,768]{2,1,0:T(8,128)(2,1)}, u32[]{:S(2)}) copy-start(bf16[2,512,768]{2,1,0:T(8,128)(2,1)} %param.16) | copy-start | bytes 4718596
  731.3 40.1 %copy-start.48 = (bf16[2,512,768]{2,1,0:T(8,128)(2,1)S(1)}, bf16[2,512,768]{2,1,0:T(8,128)(2,1)}, u32[]{:S(2)}) copy-start(bf16[2,512,768]{2,1,0:T(8,128)(2,1)} %copy.245) | copy-start | bytes 4718596
  731.3 40.1 %copy-start.69 = (f32[768]{0:T(1024)S(1)}, f32[768]{0:T(1024)}, u32[]{:S(2)}) copy-start(f32[768]{0:T(1024)} %param.19) | copy-start | bytes 9220
  731.3 40.1 %copy-start.79 = (f32[768]{0:T(1024)S(1)}, f32[768]{0:T(1024)}, u32[]{:S(2)}) copy-start(f32[768]{0:T(1024)} %param.20) | copy-start | bytes 9220
  731.3 40.1 %copy-start.81 = (f32[2,512]{1,0:T(2,128)S(1)}, f32[2,512]{1,0:T(2,128)}, u32[]{:S(2)}) copy-start(f32[2,512]{1,0:T(2,128)} %copy-done.80) | copy-start | bytes 12292
  731.3 40.1 %copy-start.92 = (f32[2,512]{1,0:T(2,128)S(1)}, f32[2,512]{1,0:T(2,128)}, u32[]{:S(2)}) copy-start(f32[2,512]{1,0:T(2,128)} %copy-done.91) | copy-start | bytes 12292
  790.3 311.7 %reduce-scatter.11.cloned.1.call-start = ((), (), s32[]{:S(2)}) async-start(), calls=%async_computation.8 | async-start | bytes 10616832 | tf_op jit(solution)/shard_map/reduce_scatter | solution.py:345
  803.8 464.7 %reduce-scatter.9.cloned.1.call-start = ((), (), s32[]{:S(2)}) async-start(), calls=%async_computation.7 | async-start | bytes 10616832 | tf_op jit(solution)/shard_map/reduce_scatter | solution.py:343
  819.0 512.4 %all-reduce.17.cloned.1.call-start = ((), (), s32[]{:S(2)}) async-start(), calls=%async_computation.10 | async-start | bytes 3538944 | tf_op jit(solution)/shard_map/psum | solution.py:350
  828.2 9.7 copy-start.15
  828.2 9.7 copy-start.45
  828.2 9.7 copy-start.49
  828.2 9.7 copy-start.82
  852.3 418.4 %copy-start.102 = (f32[2,128]{1,0:T(2,128)S(1)}, f32[2,128]{1,0:T(2,128)}, u32[]{:S(2)}) copy-start(f32[2,128]{1,0:T(2,128)} %copy-done.100) | copy-start | bytes 3076
  (95 other events, 382.5 us)
Sparse Core Ops, SparseCore 0:
  168.8 72.0 all-reduce.12
  603.0 110.5 all-reduce.14
  717.1 86.9 reduce-scatter.6
  807.6 128.0 reduce-scatter.4
  939.6 162.4 reduce-scatter.10
  1106.0 162.5 reduce-scatter.8
  1272.5 45.7 all-reduce.16
where the time goes:
time: 1360 us; the launch traced here: 1350 us
  waiting for transfers between devices  495 us (36%)
  matrix products  295 us (22%)
  other arithmetic  177 us (13%)
  blocking collectives  177 us (13%)
  local copies, waits for them, and re-layouts  173 us (13%)
  between operations  17.1 us (1%)
    dot_general x48, matrix products, mixdot(): jnp.einsum(pattern, left_op, right_op, preferred_element_type=jnp.float32)  295 us
    reduce_scatter x1, waiting for transfers between devices, body(): lax.psum_scatter(ffn_grads[4], 'seq', scatter_dimension=0, tiled=True)  164 us
    reduce_scatter x1, waiting for transfers between devices, body(): lax.psum_scatter(ffn_grads[2], 'seq', scatter_dimension=0, tiled=True)  164 us
    all_gather x2, blocking collectives, merged(): gathered = jax.tree.map(lambda a: lax.all_gather(a, axis), part)  98.1 us
    reduce_scatter x1, waiting for transfers between devices, body(): lax.psum_scatter(qkv_grad_sum, 'seq', scatter_dimension=0, tiled=True)  83.4 us
    psum x1, waiting for transfers between devices, body(): summed = lax.psum(partial_value, 'seq')  51.1 us
    convert_element_type x2, other arithmetic, ffn_forward(): hidden = gelu_apply(inner).astype(jnp.bfloat16)  39.8 us
    unnamed x1, blocking collectives  36.4 us
  transfers between devices with their start and end apart: 11, of which 5 were waited for; matrix products, arithmetic and copies ran while one was open for 27% of the time, Pallas kernels for 0%

commit v1 on v0

v1 whole, which is shorter than its diff:
```python
import functools
import jax
import jax.numpy as jnp
from jax import lax
from jax.experimental import pallas as pl
from jax.experimental.pallas import tpu as pltpu
from jax.sharding import PartitionSpec as P

HEADS = 12
NEG = -1e30
LANES = 128
TYPE0 = 3 * HEADS

def nt(a, b):
    return lax.dot_general(a, b, (((1,), (1,)), ((), ())), preferred_element_type=jnp.float32)

def tn(a, b):
    return lax.dot_general(a, b, (((0,), (0,)), ((), ())), preferred_element_type=jnp.float32)

def nn(a, b):
    return jnp.dot(a, b, preferred_element_type=jnp.float32)


def type_marks(rows, half, lane, row):
    kind = jnp.where(row < half, TYPE0, jnp.where(row < 2 * half, TYPE0 + 1, TYPE0 + 2))
    return (lane == kind)


def attend_kernel(half, scale, tq, q_ref, k_ref, v_ref, kaug_ref, o_ref, lse_ref):
    pair = pl.program_id(1)
    rows = q_ref.shape[1]
    zero = jnp.zeros((), jnp.bfloat16)
    k, v = k_ref[0], v_ref[0]
    kaug = kaug_ref[0]
    lane_all = lax.broadcasted_iota(jnp.int32, (rows, LANES), 1)
    low_all = lane_all < LANES // 2
    one = jnp.ones((), jnp.bfloat16)
    kx, vx = [], []
    for sel in (low_all, jnp.logical_not(low_all)):
        kx.append(jnp.concatenate([jnp.where(sel, k, zero), kaug], axis=1))
        vx.append(jnp.concatenate([jnp.where(sel, v, zero), jnp.where(sel, one, zero)], axis=1))
    for start in range(0, rows, tq):
        lane = lax.broadcasted_iota(jnp.int32, (tq, LANES), 1)
        row = lax.broadcasted_iota(jnp.int32, (tq, LANES), 0) + start
        low = lane < LANES // 2
        qaug = jnp.where(type_marks(rows, half, lane, row), one, zero)
        q = (q_ref[0, start:start + tq].astype(jnp.float32) * scale).astype(jnp.bfloat16)
        qx = jnp.concatenate([q, qaug], axis=1)
        acc = None
        peaks = []
        for a in (0, 1):
            s = nt(qx, kx[a])
            peak = jnp.max(s, axis=1, keepdims=True)
            p = jnp.exp(s - peak).astype(jnp.bfloat16)
            part = nn(p, vx[a])
            acc = part if acc is None else acc + part
            peaks.append(peak)
        total = acc[:, LANES:]
        o_ref[0, start:start + tq] = (acc[:, :LANES] / total).astype(jnp.bfloat16)
        lse = jnp.where(low, peaks[0], peaks[1]) + jnp.log(total)
        first, second = lse[:, 0:1], lse[:, LANES // 2:LANES // 2 + 1]
        prev = jnp.where(pair == 0, 0.0, lse_ref[0, start:start + tq])
        head = lax.rem(lane, HEADS)
        inside = lane < 3 * HEADS
        kept = jnp.where(inside & (head == 2 * pair), first, prev)
        lse_ref[0, start:start + tq] = jnp.where(inside & (head == 2 * pair + 1), second, kept)


def attend(qkv, kaug, half, tq=320):
    row_count, rows, cols = qkv.shape
    width = cols // 3
    pairs = width // LANES
    scale = (width // HEADS) ** (-0.5)
    spec = lambda off: pl.BlockSpec((1, rows, LANES), lambda r, p: (r, 0, off + p))
    return pl.pallas_call(
        functools.partial(attend_kernel, half, scale, tq),
        grid=(row_count, pairs),
        in_specs=[spec(0), spec(pairs), spec(2 * pairs), pl.BlockSpec((1, rows, LANES), lambda r, p: (r, 0, 0))],
        out_specs=[spec(0), pl.BlockSpec((1, rows, LANES), lambda r, p: (r, 0, 0))],
        out_shape=[
            jax.ShapeDtypeStruct((row_count, rows, width), jnp.bfloat16),
            jax.ShapeDtypeStruct((row_count, rows, LANES), jnp.float32),
        ],
        compiler_params=pltpu.CompilerParams(vmem_limit_bytes=48 * 1024 * 1024),
        name="attend",
    )(qkv, qkv, qkv, kaug)


def three_parts(values, lane):
    top = values.astype(jnp.bfloat16)
    rest = values - top.astype(jnp.float32)
    mid = rest.astype(jnp.bfloat16)
    low = (rest - mid.astype(jnp.float32)).astype(jnp.bfloat16)
    zero = jnp.zeros((), jnp.bfloat16)
    return jnp.where(lane < HEADS, top, jnp.where(lane < 2 * HEADS, mid, jnp.where(lane < 3 * HEADS, low, zero)))


def attend_back_kernel(half, scale, tk, q_ref, k_ref, v_ref, g_ref, lse_ref, delta_ref, kaug_ref, dq_ref, dk_ref, dv_ref):
    pair = pl.program_id(1)
    rows = q_ref.shape[1]
    zero = jnp.zeros((), jnp.bfloat16)
    one = jnp.ones((), jnp.bfloat16)
    lane = lax.broadcasted_iota(jnp.int32, (rows, LANES), 1)
    row = lax.broadcasted_iota(jnp.int32, (rows, LANES), 0)
    low = lane < LANES // 2
    q = (q_ref[0].astype(jnp.float32) * scale).astype(jnp.bfloat16)
    g = g_ref[0]
    qaug = jnp.where(type_marks(rows, half, lane, row), one, three_parts(lse_ref[0], lane))
    gaug = three_parts(delta_ref[0], lane)
    qx = jnp.concatenate([q, qaug], axis=1)
    gx = jnp.concatenate([g, gaug], axis=1)
    sels = (low, jnp.logical_not(low))
    qh = [jnp.where(sel, q, zero) for sel in sels]
    gh = [jnp.where(sel, g, zero) for sel in sels]
    dq = None
    for start in range(0, rows, tk):
        lane_k = lax.broadcasted_iota(jnp.int32, (tk, LANES), 1)
        low_k = lane_k < LANES // 2
        head = lax.rem(lane_k, HEADS)
        inside = lane_k < 3 * HEADS
        k = k_ref[0, start:start + tk]
        v = v_ref[0, start:start + tk]
        kaug = kaug_ref[0, start:start + tk]
        dk = dv = None
        for a, sel in ((0, low_k), (1, jnp.logical_not(low_k))):
            marks = inside & (head == 2 * pair + a)
            kh = jnp.where(sel, k, zero)
            kx = jnp.concatenate([kh, jnp.where(marks, -one, kaug)], axis=1)
            vx = jnp.concatenate([jnp.where(sel, v, zero), jnp.where(marks, -one, zero)], axis=1)
            p = jnp.exp(nt(kx, qx))
            ds = (p * nt(vx, gx)).astype(jnp.bfloat16)
            part_v = nn(p.astype(jnp.bfloat16), gh[a])
            part_k = nn(ds, qh[a])
            part_q = tn(ds, kh)
            dv = part_v if dv is None else dv + part_v
            dk = part_k if dk is None else dk + part_k
            dq = part_q if dq is None else dq + part_q
        dk_ref[0, start:start + tk] = dk.astype(jnp.bfloat16)
        dv_ref[0, start:start + tk] = dv.astype(jnp.bfloat16)
    dq_ref[0] = (dq * scale).astype(jnp.bfloat16)


def attend_back(qkv, grad, lse, delta, kaug, half, tk=320):
    row_count, rows, cols = qkv.shape
    width = cols // 3
    pairs = width // LANES
    scale = (width // HEADS) ** (-0.5)
    spec = lambda off: pl.BlockSpec((1, rows, LANES), lambda r, p: (r, 0, off + p))
    whole = pl.BlockSpec((1, rows, LANES), lambda r, p: (r, 0, 0))
    out = jax.ShapeDtypeStruct((row_count, rows, width), jnp.bfloat16)
    return pl.pallas_call(
        functools.partial(attend_back_kernel, half, scale, tk),
        grid=(row_count, pairs),
        in_specs=[spec(0), spec(pairs), spec(2 * pairs), spec(0), whole, whole, whole],
        out_specs=[spec(0)] * 3,
        out_shape=[out] * 3,
        compiler_params=pltpu.CompilerParams(vmem_limit_bytes=48 * 1024 * 1024),
        name="attend_back",
    )(qkv, qkv, qkv, grad, lse, delta, kaug)


EPS = 1e-05
MESH_ID = pl.DeviceIdType.MESH


def spread_kernel(count, sizes, same, *refs):
    ins, outs = refs[:sizes], refs[sizes:2 * sizes]
    send, recv, local = refs[2 * sizes:]
    me = lax.axis_index("seq")
    barrier = pltpu.get_barrier_semaphore()
    for step in range(1, count):
        pl.semaphore_signal(
            barrier, inc=1, device_id={"seq": lax.rem(me + step, count)}, device_id_type=MESH_ID
        )
    pl.semaphore_wait(barrier, count - 1)
    own = []
    for n in range(sizes):
        copy = pltpu.make_async_copy(ins[n] if same else ins[n].at[me], outs[n].at[me], local.at[n])
        copy.start()
        own.append(copy)
    copies = []
    for step in range(1, count):
        peer = lax.rem(me + step, count)
        for n in range(sizes):
            copy = pltpu.make_async_remote_copy(
                src_ref=ins[n] if same else ins[n].at[peer],
                dst_ref=outs[n].at[me],
                send_sem=send.at[n, step],
                recv_sem=recv.at[n, step],
                device_id={"seq": peer},
                device_id_type=MESH_ID,
            )
            copy.start()
            copies.append(copy)
    for copy in own:
        copy.wait()
    for copy in copies:
        copy.wait()


def spread(arrays, count, same, collective_id):
    sizes = len(arrays)
    shapes = [(count,) + a.shape if same else a.shape for a in arrays]
    vmem = pl.BlockSpec(memory_space=pltpu.VMEM)
    return pl.pallas_call(
        functools.partial(spread_kernel, count, sizes, same),
        in_specs=[vmem] * sizes,
        out_specs=[vmem] * sizes,
        out_shape=[jax.ShapeDtypeStruct(s, a.dtype) for s, a in zip(shapes, arrays)],
        scratch_shapes=[
            pltpu.SemaphoreType.DMA((sizes, count)),
            pltpu.SemaphoreType.DMA((sizes, count)),
            pltpu.SemaphoreType.DMA((sizes,)),
        ],
        compiler_params=pltpu.CompilerParams(
            collective_id=collective_id, has_side_effects=True, vmem_limit_bytes=32 * 1024 * 1024
        ),
        name="spread",
    )(*arrays)


def norm_parts(values):
    average = jnp.mean(values, axis=-1, keepdims=True)
    centred = values - average
    variance = jnp.mean(centred * centred, axis=-1, keepdims=True)
    inv = lax.rsqrt(variance + EPS)
    return centred * inv, inv


def norm_back(grad, n, inv, gain):
    eg = grad * gain
    through = (
        eg - jnp.mean(eg, axis=-1, keepdims=True) - n * jnp.mean(eg * n, axis=-1, keepdims=True)
    ) * inv
    return through, jnp.sum(grad * n, axis=0), jnp.sum(grad, axis=0)


def split_rows(a, count):
    row_count, rows, width = a.shape
    part = rows // count
    moved = a.reshape(row_count, count, part, width).transpose(1, 0, 2, 3)
    return moved.reshape(count, row_count * part, width)


def join_rows(a, row_count):
    count, rows, width = a.shape
    part = rows // row_count
    moved = a.reshape(count, row_count, part, width).transpose(1, 0, 2, 3)
    return moved.reshape(row_count, count * part, width)


def per_head(values, width):
    lanes = values[..., :HEADS]
    return jnp.repeat(lanes, width // HEADS, axis=-1)


def head_sums(values):
    rows, width = values.shape
    lane = jnp.arange(LANES)
    head = jnp.arange(width) // (width // HEADS)
    place = ((lane[None, :] % HEADS == head[:, None]) & (lane[None, :] < 3 * HEADS)).astype(jnp.bfloat16)
    top = values.astype(jnp.bfloat16)
    rest = (values - top.astype(jnp.float32)).astype(jnp.bfloat16)
    return nn(top, place) + nn(rest, place)


def body(
    inputs,
    global_inputs,
    lengths,
    first_gain,
    first_shift,
    qkv_weight,
    out_weight,
    second_gain,
    second_shift,
    inner_weight,
    inner_bias,
    outer_weight,
    output_cotangent,
    global_cotangent,
):
    f32, bf16 = jnp.float32, jnp.bfloat16
    row_count, block_len, width = inputs.shape
    half = block_len // 2
    global_count = global_inputs.shape[1]
    rows = block_len + global_count
    inner_width = inner_weight.shape[1]
    count = lax.axis_size("seq")
    me = lax.axis_index("seq")
    after = lax.rem(me + 1, count)
    back = [(i, (i - 1) % count) for i in range(count)]
    forth = [(i, (i + 1) % count) for i in range(count)]
    token_rows = row_count * block_len
    share = global_count // count
    own_rows = row_count * share

    next_inputs = lax.ppermute(inputs[:, :half], "seq", back)
    next_cotangent = lax.ppermute(output_cotangent[:, :half], "seq", back)
    block = jnp.concatenate([inputs[:, half:], next_inputs], axis=1)
    spots = jnp.arange(half, dtype=jnp.int32)
    positions = jnp.concatenate([me * block_len + half + spots, after * block_len + spots])
    valid = positions[None, :] < lengths[:, None]

    kind = jnp.arange(LANES)[None, None, :] - TYPE0
    key_half = (jnp.arange(block_len) // half)[None, :, None]
    last = me == count - 1
    hidden_key = jnp.logical_not(valid)[:, :, None] | (last & (kind < 2) & (kind != key_half))
    token_marks = jnp.where(hidden_key & (kind >= 0) & (kind < 3), NEG, 0.0)
    global_marks = jnp.where((kind == 2) & (me != 0), NEG, 0.0)
    global_marks = jnp.broadcast_to(global_marks, (row_count, global_count, LANES))
    kaug = jnp.concatenate([token_marks, global_marks], axis=1).astype(bf16)

    states = jnp.concatenate([block, global_inputs], axis=1)
    n_first, inv_first = norm_parts(states.astype(f32))
    normed = (n_first * first_gain + first_shift).astype(bf16)
    qkv = nn(normed.reshape(row_count * rows, width), qkv_weight).astype(bf16)
    qkv = qkv.reshape(row_count, rows, 3 * width)

    mixed, lse = attend(qkv, kaug, half)
    part_mixed, part_lse = spread(
        [split_rows(mixed[:, block_len:], count), split_rows(lse[:, block_len:], count)], count, False, 0
    )
    highest = jnp.max(part_lse, axis=0)
    part_weight = jnp.exp(part_lse - highest)
    total = jnp.sum(part_weight, axis=0)
    global_lse = highest + jnp.log(total)
    global_mixed = jnp.sum(per_head(part_weight / total, width) * part_mixed.astype(f32), axis=0)

    own_globals = lax.dynamic_slice_in_dim(global_inputs, me * share, share, axis=1)
    own_global_cot = lax.dynamic_slice_in_dim(global_cotangent, me * share, share, axis=1)
    tokens = jnp.concatenate(
        [block.reshape(token_rows, width), own_globals.reshape(own_rows, width)]
    ).astype(f32)
    cot_block = jnp.concatenate([output_cotangent[:, half:], next_cotangent], axis=1)
    cot_block = jnp.where(valid[:, :, None], cot_block, 0)
    cotangent = jnp.concatenate(
        [cot_block.reshape(token_rows, width), own_global_cot.reshape(own_rows, width)]
    )
    attended = jnp.concatenate(
        [mixed[:, :block_len].reshape(token_rows, width), global_mixed.astype(bf16)]
    )
    residual = tokens + nn(attended, out_weight)
    n_second, inv_second = norm_parts(residual)
    normed_second = (n_second * second_gain + second_shift).astype(bf16)
    inner = nn(normed_second, inner_weight) + inner_bias
    bell = jnp.exp(-0.5 * inner * inner)
    cdf = 0.5 * (1.0 + lax.erf(inner * (0.5 ** 0.5)))
    hidden = (inner * cdf).astype(bf16)
    final = residual + nn(hidden, outer_weight)
    hidden_grad = nt(cotangent, outer_weight)
    slope = cdf + inner * bell * ((0.5 / jnp.pi) ** 0.5)
    inner_grad = (hidden_grad * slope).astype(bf16)
    second_grad = nt(inner_grad, inner_weight)
    through, second_gain_grad, second_shift_grad = norm_back(second_grad, n_second, inv_second, second_gain)
    residual_grad = cotangent.astype(f32) + through
    projection_grad = residual_grad.astype(bf16)
    attended_grad = nt(projection_grad, out_weight).astype(bf16)
    delta = head_sums(attended_grad.astype(f32) * attended.astype(f32))
    outer_grad = tn(hidden, cotangent)
    inner_wgrad = tn(normed_second, inner_grad)
    bias_grad = jnp.sum(inner_grad.astype(f32), axis=0)
    out_grad = tn(attended, projection_grad)

    all_grad, all_lse, all_delta = spread(
        [attended_grad[token_rows:], global_lse, delta[token_rows:]], count, True, 1
    )
    block_grad = jnp.concatenate(
        [attended_grad[:token_rows].reshape(row_count, block_len, width), join_rows(all_grad, row_count)], axis=1
    )
    block_lse = jnp.concatenate([lse[:, :block_len], join_rows(all_lse, row_count)], axis=1)
    block_delta = jnp.concatenate(
        [delta[:token_rows].reshape(row_count, block_len, LANES), join_rows(all_delta, row_count)], axis=1
    )
    dqkv = jnp.concatenate(attend_back(qkv, block_grad, block_lse, block_delta, kaug, half, rows), axis=-1)
    (part_dqkv,) = spread([split_rows(dqkv[:, block_len:], count)], count, False, 2)
    global_dqkv = jnp.sum(part_dqkv.astype(f32), axis=0).astype(bf16)
    qkv_grad = jnp.concatenate([dqkv[:, :block_len].reshape(token_rows, 3 * width), global_dqkv])

    first_grad = nt(qkv_grad, qkv_weight)
    n_tokens, inv_tokens = norm_parts(tokens)
    through, first_gain_grad, first_shift_grad = norm_back(first_grad, n_tokens, inv_tokens, first_gain)
    input_grad = (residual_grad + through).astype(bf16)
    normed_tokens = (n_tokens * first_gain + first_shift).astype(bf16)
    qkv_wgrad = tn(normed_tokens, qkv_grad)

    layer = final[:token_rows].reshape(row_count, block_len, width)
    layer = jnp.where(valid[:, :, None], layer, 0.0).astype(bf16)
    grad_block = input_grad[:token_rows].reshape(row_count, block_len, width)
    layer_output = jnp.concatenate([lax.ppermute(layer[:, half:], "seq", forth), layer[:, :half]], axis=1)
    input_out = jnp.concatenate(
        [lax.ppermute(grad_block[:, half:], "seq", forth), grad_block[:, :half]], axis=1
    )
    global_final, global_grad = spread(
        [final[token_rows:].astype(bf16), input_grad[token_rows:]], count, True, 3
    )

    def shares(a):
        return a.reshape(count, a.shape[0] // count, -1)

    strips = inner_width // width
    inner_part = inner_wgrad.reshape(count, width // count, strips, width).transpose(0, 2, 1, 3)
    qkv_part = qkv_wgrad.reshape(count, width // count, 3, width).transpose(0, 2, 1, 3)
    small = jnp.concatenate(
        [
            shares(first_gain_grad),
            shares(first_shift_grad),
            shares(second_gain_grad),
            shares(second_shift_grad),
            shares(bias_grad),
        ],
        axis=1,
    )
    small = small.reshape(count, 1, -1)
    stacked = jnp.concatenate(
        [
            inner_part.reshape(count, -1, width).astype(bf16),
            shares(outer_grad).astype(bf16),
            shares(out_grad).astype(bf16),
            qkv_part.reshape(count, -1, width).astype(bf16),
        ],
        axis=1,
    )
    stacked = lax.psum_scatter(stacked, "seq", scatter_dimension=0, tiled=True)
    stacked = lax.psum(stacked, "batch")[0].astype(f32)
    small = lax.psum_scatter(small, "seq", scatter_dimension=0, tiled=True)
    small = lax.psum(small, "batch").reshape(-1)
    part = width // count
    first_rows = strips * part
    outer_rows = inner_width // count
    inner_out = stacked[:first_rows].reshape(strips, part, width).transpose(1, 0, 2).reshape(part, inner_width)
    at = first_rows + outer_rows
    outer_out = stacked[first_rows:at]
    out_out = stacked[at:at + part]
    qkv_out = stacked[at + part:].reshape(3, part, width).transpose(1, 0, 2).reshape(part, 3 * width)
    return (
        layer_output,
        join_rows(global_final, row_count),
        input_out,
        join_rows(global_grad, row_count),
        small[:part],
        small[part:2 * part],
        qkv_out,
        out_out,
        small[2 * part:3 * part],
        small[3 * part:4 * part],
        inner_out,
        small[4 * part:],
        outer_out,
    )


def solution(mesh):
    rows = P("batch", "seq", None)
    globals_at = P("batch", None, None)
    return jax.shard_map(
        body,
        mesh=mesh,
        in_specs=(rows, globals_at, P("batch")) + (P(),) * 9 + (rows, globals_at),
        out_specs=(
            rows,
            globals_at,
            rows,
            globals_at,
            P("seq"),
            P("seq"),
            P("seq", None),
            P("seq", None),
            P("seq"),
            P("seq"),
            P("seq", None),
            P("seq"),
            P("seq", None),
        ),
        check_vma=False,
    )
```

time: 1360 us -> 691 us (0.51)
  waiting for transfers between devices: 495 us -> 243 us
  matrix products: 295 us -> 97.8 us
  Pallas kernels: 0 us -> 131 us
  blocking collectives: 177 us -> 47.5 us
  other arithmetic: 177 us -> 49 us
  local copies, waits for them, and re-layouts: 173 us -> 82.1 us
    dot_general x48 -> x14, matrix products: 295 us -> 97.8 us  [the longest x4 36.1 us: nt(): lax.dot_general(a, b, (((1,), (1,)), ((), ())), preferred_element_type=jn...]
    reduce_scatter x4 -> x1, waiting for transfers between devices: 412 us -> 237 us  [body(): stacked = lax.psum_scatter(stacked, 'seq', scatter_dimension=0, tiled=True)]
    pallas_call x0 -> x6, Pallas kernels: none -> 131 us  [the longest x4 69.8 us: spread(): pl.pallas_call(functools.partial(spread_kernel, count, sizes, same), in_s...]
    all_gather x2 -> x0, blocking collectives: 98.1 us -> none  [merged(): gathered = jax.tree.map(lambda a: lax.all_gather(a, axis), part)]
    convert_element_type x24 -> x5, other arithmetic: 104 us -> 6.42 us  [the longest x1 1.87 us: body(): stacked = lax.psum(stacked, 'batch')[0].astype(f32)]
    reshape x18 -> x13, local copies, waits for them, and re-layouts: 78.9 us -> 5.6 us  [the longest x1 2.68 us: per_head(): return jnp.repeat(lanes, width // HEADS, axis=-1)]
    psum x3 -> x1, waiting for transfers between devices: 51.1 us -> 0.01 us  [body(): stacked = lax.psum(stacked, 'batch')[0].astype(f32)]
    psum x2 -> x1, blocking collectives: 42.5 us -> 5.63 us  [body(): small = lax.psum(small, 'batch').reshape(-1)]
  transfers between devices with their start and end apart: 11 -> 6, of which waited for: 5 -> 2; matrix products, arithmetic and copies ran while one was open for 27% -> 11% of each run, Pallas kernels for 0% -> 8%
where the time goes in v1:
time: 691 us; the launch traced here: 680 us
  waiting for transfers between devices  243 us (35%)
  Pallas kernels  131 us (19%)
  matrix products  97.8 us (14%)
  local copies, waits for them, and re-layouts  82.1 us (12%)
  other arithmetic  49 us (7%)
  blocking collectives  47.5 us (7%)
  between operations  15.4 us (2%)
  starting transfers between devices  14.9 us (2%)
    reduce_scatter x1, waiting for transfers between devices, body(): stacked = lax.psum_scatter(stacked, 'seq', scatter_dimension=0, tiled=True)  237 us
    pallas_call x4, Pallas kernels, spread(): pl.pallas_call(functools.partial(spread_kernel, count, sizes, same), in_s...  69.8 us
    unnamed x1, blocking collectives  41.9 us
    dot_general x4, matrix products, nt(): lax.dot_general(a, b, (((1,), (1,)), ((), ())), preferred_element_type=jn...  36.1 us
    pallas_call x1, Pallas kernels, attend_back(): pl.pallas_call(functools.partial(attend_back_kernel, half, scale, tk), gr...  33.7 us
    dot_general x4, matrix products, tn(): lax.dot_general(a, b, (((0,), (0,)), ((), ())), preferred_element_type=jn...  32.1 us
    dot_general x6, matrix products, nn(): return jnp.dot(a, b, preferred_element_type=jnp.float32)  29.5 us
    pallas_call x1, Pallas kernels, attend(): pl.pallas_call(functools.partial(attend_kernel, half, scale, tq), grid=(r...  27.9 us
  transfers between devices with their start and end apart: 6, of which 2 were waited for; matrix products, arithmetic and copies ran while one was open for 11% of the time, Pallas kernels for 8%

profile of v1, /device:TPU:0, one launch (start us, length us, event | category | flops | bytes accessed | tf_op | source)
XLA Modules:
  0.0 680.4 jit_solution(15032094215011543500)
XLA Ops:
  7.3 2.8 fusion.58
  10.0 6.0 collective-permute-start
  21.6 1.4 constant_dynamic-slice_fusion.1
  28.8 5.5 collective-permute-done
  34.3 1.8 fusion.52
  36.1 2.1 multiply_reduce_fusion
  39.5 1.8 maximum_convert_fusion
  42.1 6.5 convolution_convert_fusion
  48.6 27.9 %attend.1 = (bf16[2,640,768]{2,1,0:T(8,128)(2,1)S(1)}, f32[2,640,128]{2,1,0:T(8,128)S(1)}) custom-call(bf16[2,640,2304]{2,1,0:T(8,128)(2,1)} %bitcast.112, bf16[2,640,2304]{2,1,0:T(8,128)(2,1)} %bitcast.113, bf16[2,640,2304]{2,1,0:T(8,128)(2,1)} %bitcast.114, bf16[2,640,128]{2,1,0:T(8,128)(2,1)S(1)} %copy-done.2), custom_call_target="tpu_custom_call" | custom-call | tf_op jit(solution)/shard_map/attend/pallas_call | solution.py:75
  77.9 12.1 %spread.4 = (bf16[8,32,768]{2,1,0:T(8,128)(2,1)S(1)}, f32[8,32,128]{2,1,0:T(8,128)S(1)}) custom-call(bf16[8,32,768]{2,1,0:T(8,128)(2,1)S(1)} %bitcast.105, f32[8,32,128]{2,1,0:T(8,128)S(1)} %bitcast.106), custom_call_target="tpu_custom_call" | custom-call | tf_op jit(solution)/shard_map/spread/pallas_call | solution.py:205
  93.9 1.9 broadcast_in_dim.46
  95.8 2.7 reshape.424
  98.5 1.5 multiply_reduce_fusion.6
  100.0 1.6 pad_maximum_fusion.8
  101.7 1.6 fusion.59
  106.7 10.4 %multiply_convert_fusion = (bf16[1056,3072]{1,0:T(8,128)(2,1)}, f32[1056,3072]{1,0:T(8,128)}) fusion(f32[3072]{0:T(1024)S(1)} %copy-done.43, bf16[768,3072]{1,0:T(8,128)(2,1)S(1)} %bitcast.168, f32[1056,768]{1,0:T(8,128)S(1)} %get-tuple-element.62, f32[768]{0:T(1024)S(1)} %copy-done.44, f32[768]{0:T(1024)S(1)} %copy-done.34, f32[1056]{0:T(1024)S(1)} %add_rsqrt_fusion.1, ...), kind=kOutput, calls=%fused_computation.9 | convolution fusion | flops 5006352384 | bytes 27453696 | tf_op jit(solution)/shard_map/dot_general | solution.py:21
  117.1 15.3 %convert_reduce_fusion = (f32[3072]{0:T(1024)}, bf16[1056,3072]{1,0:T(8,128)(2,1)}) fusion(f32[1056,3072]{1,0:T(8,128)} %get-tuple-element.64, bf16[3072,768]{1,0:T(8,128)(2,1)} %param.25, bf16[32,768]{1,0:T(8,128)(2,1)S(1)} %bitcast.159, bf16[1024,768]{1,0:T(8,128)(2,1)S(1)} %bitcast_select_fusion), kind=kOutput, calls=%fused_computation.8 | convolution fusion | flops 5025002496 | bytes 25817088 | tf_op jit(solution)/shard_map/dot_general | solution.py:15
  132.4 10.8 %multiply_reduce_fusion.1 = (f32[768]{0:T(1024)}, f32[1056]{0:T(1024)S(1)}, f32[1056]{0:T(1024)S(1)}, f32[768]{0:T(1024)}, f32[1056,768]{1,0:T(8,128)S(1)}) fusion(f32[1056,768]{1,0:T(8,128)S(1)} %get-tuple-element.62, f32[1056]{0:T(1024)S(1)} %add_rsqrt_fusion.1, f32[1056]{0:T(1024)S(1)} %broadcast_multiply_fusion.5, f32[768]{0:T(1024)S(1)} %copy-done.34, ...), kind=kOutput, calls=%fused_computation.43 | convolution fusion | flops 4990128128 | bytes 17720832 | tf_op jit(solution)/shard_map/dot_general | solution.py:15
  143.2 11.2 %convolution_convert_fusion.2 = bf16[768,3072]{1,0:T(8,128)(2,1)} fusion(bf16[1056,3072]{1,0:T(8,128)(2,1)} %get-tuple-element.68, f32[1056,768]{1,0:T(8,128)S(1)} %get-tuple-element.62, f32[768]{0:T(1024)S(1)} %copy-done.44, f32[768]{0:T(1024)S(1)} %copy-done.34, f32[1056]{0:T(1024)S(1)} %add_rsqrt_fusion.1, f32[1056]{0:T(1024)S(1)} %broadcast_multiply_fusion.5), kind=kOutput, calls=%fused_computation.14 | convolution fusion | flops 4989247488 | bytes 14465280 | tf_op jit(solution)/shard_map/dot_general | solution.py:18
  154.4 1.9 multiply_add_fusion
  156.3 2.8 convolution_convert_fusion.5
  159.1 1.5 convolution_convert_fusion.4
  162.6 17.5 %spread.5 = (bf16[8,32,768]{2,1,0:T(8,128)(2,1)S(1)}, f32[8,32,128]{2,1,0:T(8,128)S(1)}, f32[8,32,128]{2,1,0:T(8,128)S(1)}) custom-call(bf16[32,768]{1,0:T(8,128)(2,1)S(1)} %slice.166.refs_0_, f32[32,128]{1,0:T(8,128)S(1)} %log_add_fusion.refs_1_, f32[32,128]{1,0:T(8,128)S(1)} %slice.167.refs_2_), custom_call_target="tpu_custom_call" | custom-call | tf_op jit(solution)/shard_map/spread/pallas_call | solution.py:205
  181.6 33.7 %attend_back.1 = (bf16[2,640,768]{2,1,0:T(8,128)(2,1)S(1)}, bf16[2,640,768]{2,1,0:T(8,128)(2,1)S(1)}, bf16[2,640,768]{2,1,0:T(8,128)(2,1)}) custom-call(bf16[2,640,2304]{2,1,0:T(8,128)(2,1)} %bitcast.115, bf16[2,640,2304]{2,1,0:T(8,128)(2,1)} %bitcast.116, bf16[2,640,2304]{2,1,0:T(8,128)(2,1)} %bitcast.117, bf16[2,640,768]{2,1,0:T(8,128)(2,1)} %pad_maximum_fusion.4.g_ref, ...), custom_call_target="tpu_custom_call" | custom-call | tf_op jit(solution)/shard_map/attend_back/pallas_call | solution.py:151
  218.1 2.7 slice.169
  222.2 8.5 %convolution_convert_fusion.1 = bf16[3072,768]{1,0:T(8,128)(2,1)} fusion(bf16[1056,3072]{1,0:T(8,128)(2,1)S(1)} %bitcast.170, bf16[32,768]{1,0:T(8,128)(2,1)S(1)} %bitcast.161, bf16[1024,768]{1,0:T(8,128)(2,1)S(1)} %bitcast_select_fusion), kind=kOutput, calls=%fused_computation.13 | convolution fusion | flops 4988436480 | bytes 12828672 | tf_op jit(solution)/shard_map/dot_general | solution.py:18
  230.6 9.9 %convert_element_type.140 = bf16[8,96,4,768]{3,2,1,0:T(4,128)(2,1)} reshape(bf16[768,3072]{1,0:T(8,128)(2,1)} %convolution_convert_fusion.2) | data formatting | bytes 9437184 | tf_op jit(solution)/shard_map/convert_element_type | solution.py:417
  240.6 5.4 copy.72
  246.1 23.9 %spread.6 = bf16[8,32,2304]{2,1,0:T(8,128)(2,1)S(1)} custom-call(bf16[8,32,2304]{2,1,0:T(8,128)(2,1)S(1)} %bitcast.104), custom_call_target="tpu_custom_call" | custom-call | tf_op jit(solution)/shard_map/spread/pallas_call | solution.py:205
  271.1 2.1 reduce_sum.173
  273.2 9.7 %convolution_convert_fusion.3 = bf16[768,2304]{1,0:T(8,128)(2,1)} fusion(bf16[32,2304]{1,0:T(8,128)(2,1)} %reduce_sum.173, bf16[1024,2304]{1,0:T(8,128)(2,1)} %bitcast.132, f32[768]{0:T(1024)} %param.18, f32[1056]{0:T(1024)S(1)} %add_rsqrt_fusion, f32[1056]{0:T(1024)S(1)} %broadcast_multiply_fusion.1, f32[768]{0:T(1024)} %param.17, ...), kind=kOutput, calls=%fused_computation.15 | convolution fusion | flops 3755925504 | bytes 10041600 | tf_op jit(solution)/shard_map/dot_general | solution.py:18
  282.9 5.8 copy.73
  288.7 8.9 %convert_element_type.149 = bf16[8,96,3,768]{1,0,3,2:T(8,128)(2,1)} reshape(bf16[768,2304]{0,1:T(8,128)(2,1)} %copy.73) | data formatting | bytes 7077888 | tf_op jit(solution)/shard_map/convert_element_type | solution.py:420
  297.6 6.7 copy.74
  304.4 12.2 %pad_maximum_fusion = bf16[8,1152,768]{2,1,0:T(8,128)(2,1)} fusion(bf16[8,288,768]{2,1,0:T(8,128)(2,1)} %bitcast.127, bf16[8,96,768]{2,1,0:T(8,128)(2,1)} %bitcast.145, bf16[8,384,768]{2,1,0:T(8,128)(2,1)} %bitcast.131, bf16[8,384,768]{2,1,0:T(8,128)(2,1)} %bitcast.124), kind=kLoop, calls=%fused_computation.2 | loop fusion | flops 56623104 | bytes 28311552 | tf_op jit(solution)/shard_map/concatenate | solution.py:415
  316.6 9.5 %convolution_add_fusion.1 = bf16[1056,768]{1,0:T(8,128)(2,1)S(1)} fusion(f32[1056,768]{1,0:T(8,128)} %copy-done.12, bf16[1056,3072]{1,0:T(8,128)(2,1)} %get-tuple-element.63, bf16[3072,768]{1,0:T(8,128)(2,1)} %param.25), kind=kOutput, calls=%fused_computation.20 | convolution fusion | flops 4984455168 | bytes 16072704 | tf_op jit(solution)/shard_map/dot_general | solution.py:21
  327.9 4.4 collective-permute-start.1
  332.3 8.6 %fusion.20 = (f32[768]{0:T(1024)}, f32[1056]{0:T(1024)S(1)}, f32[1056]{0:T(1024)S(1)}, f32[768]{0:T(1024)}, f32[1056,768]{1,0:T(8,128)S(1)}) fusion(f32[1056]{0:T(1024)S(1)} %add_rsqrt_fusion, f32[1056]{0:T(1024)S(1)} %broadcast_multiply_fusion.1, bf16[32,768]{1,0:T(8,128)(2,1)S(1)} %bitcast.152, bf16[1024,768]{1,0:T(8,128)(2,1)S(1)} %bitcast.122, ...), kind=kOutput, calls=%fused_computation.39 | convolution fusion | flops 3757396480 | bytes 13297152 | tf_op jit(solution)/shard_map/dot_general | solution.py:15
  340.9 1.7 fusion.19
  345.2 3.9 collective-permute-start.3
  349.0 237.0 %reduce-scatter.2.cloned.1.call-done = bf16[1,1152,768]{2,1,0:T(8,128)(2,1)} async-done(((bf16[8,1152,768]{2,1,0:T(8,128)(2,1)}), bf16[1,1152,768]{2,1,0:T(8,128)(2,1)}) %reduce-scatter.2.cloned.1.call-update) | async-done | bytes 1769488 | tf_op jit(solution)/shard_map/reduce_scatter | solution.py:424
  592.1 16.3 %spread.7 = (bf16[8,32,768]{2,1,0:T(8,128)(2,1)S(1)}, bf16[8,32,768]{2,1,0:T(8,128)(2,1)S(1)}) custom-call(bf16[32,768]{1,0:T(8,128)(2,1)S(1)} %copy-done.8, bf16[32,768]{1,0:T(8,128)(2,1)S(1)} %copy-done.9), custom_call_target="tpu_custom_call" | custom-call | tf_op jit(solution)/shard_map/spread/pallas_call | solution.py:205
  610.0 1.4 concatenate.71
  611.4 41.9 %all-reduce = f32[8,1,768]{2,1,0:T(1,128)} all-reduce(f32[8,1,768]{2,1,0:T(1,128)} %bitcast.163), channel_id=2, replica_groups=mesh['seq'=8,'batch'=4] {'seq'}, use_global_device_ids=true, to_apply=%region_19.20.clone | all-reduce | flops 6144 | bytes 49152
  654.6 5.6 psum.14
  661.5 2.6 pad_maximum_fusion.9
  664.1 2.4 pad_maximum_fusion.11
  666.5 1.9 convert_element_type.152
  (206 shorter events, 49.8 us)
Async XLA Ops:
  7.2 34.9 %copy-start = (bf16[768,2304]{1,0:T(8,128)(2,1)S(1)}, bf16[768,2304]{1,0:T(8,128)(2,1)}, u32[]{:S(2)}) copy-start(bf16[768,2304]{1,0:T(8,128)(2,1)} %param.19) | copy-start | bytes 10616836
  7.2 14.4 %copy-start.41 = (s32[2]{0:T(128)S(1)}, s32[2]{0:T(128)}, u32[]{:S(2)}) copy-start(s32[2]{0:T(128)} %param.16) | copy-start | bytes 28
  7.2 578.8 %reduce-scatter.2.cloned.1.call-start = ((), (), s32[]{:S(2)}) async-start(), calls=%async_computation.1 | async-start | bytes 15925248 | tf_op jit(solution)/shard_map/reduce_scatter | solution.py:424
  7.2 8.8 %copy-start.23 = (bf16[2,512,768]{2,1,0:T(8,128)(2,1)S(1)}, bf16[2,512,768]{2,1,0:T(8,128)(2,1)}, u32[]{:S(2)}) copy-start(bf16[2,512,768]{2,1,0:T(8,128)(2,1)} %param.26) | copy-start | bytes 4718596
  10.0 24.2 %collective-permute-start = (bf16[2,256,768]{2,1,0:T(8,128)(2,1)}, bf16[2,256,768]{2,1,0:T(8,128)(2,1)}, u32[]{:S(2)}, u32[]{:S(2)}) collective-permute-start(bf16[2,256,768]{2,1,0:T(8,128)(2,1)} %get-tuple-element.56), channel_id=1, source_target_pairs={{0,28},{4,0},{8,4},{12,8},{16,12},{20,16},{24,20},{28,24},{1,29},{... | collective-permute-start | bytes 2359304 | tf_op jit(solution)/shard_map/ppermute | solution.py:298
  17.3 87.0 %collective-permute-start.2 = (bf16[2,256,768]{2,1,0:T(8,128)(2,1)}, bf16[2,256,768]{2,1,0:T(8,128)(2,1)}, u32[]{:S(2)}, u32[]{:S(2)}) collective-permute-start(bf16[2,256,768]{2,1,0:T(8,128)(2,1)} %get-tuple-element.52), channel_id=1, source_target_pairs={{0,28},{4,0},{8,4},{12,8},{16,12},{20,16},{24,20},{28,24},{1,29},{... | collective-permute-start | bytes 2359304 | tf_op jit(solution)/shard_map/ppermute | solution.py:299
  39.5 1.8 copy-start.31
  39.5 1.8 copy-start.40
  42.1 6.5 copy-start.2
  76.5 13.5 %copy-start.4 = (f32[2,640,128]{2,1,0:T(8,128)}, f32[2,640,128]{2,1,0:T(8,128)S(1)}, u32[]{:S(2)}) copy-start(f32[2,640,128]{2,1,0:T(8,128)S(1)} %get-tuple-element.26) | copy-start | bytes 1966084
  98.5 3.1 copy-start.24
  98.5 3.1 copy-start.25
  98.5 3.1 copy-start.42
  100.0 6.6 slice-start.1
  101.6 119.1 %copy-start.10 = (bf16[2,512,768]{2,1,0:T(8,128)(2,1)}, bf16[2,512,768]{2,1,0:T(8,128)(2,1)S(1)}, u32[]{:S(2)}) copy-start(bf16[2,512,768]{2,1,0:T(8,128)(2,1)S(1)} %pad_maximum_fusion.8) | copy-start | bytes 4718596
  101.7 1.7 copy-start.5
  101.7 4.9 slice-start.2
  103.3 51.1 %copy-start.12 = (f32[1056,768]{1,0:T(8,128)}, f32[1056,768]{1,0:T(8,128)S(1)}, u32[]{:S(2)}) copy-start(f32[1056,768]{1,0:T(8,128)S(1)} %get-tuple-element.62) | copy-start | bytes 9732100
  103.3 1.8 copy-start.19
  103.7 2.6 copy-start.35
  104.2 2.4 copy-start.34
  104.2 2.4 copy-start.43
  104.2 2.4 copy-start.44
  106.7 10.5 %copy-start.27 = (bf16[2,16,768]{2,1,0:T(8,128)(2,1)S(1)}, bf16[2,16,768]{2,1,0:T(8,128)(2,1)}, u32[]{:S(2)}) copy-start(bf16[2,16,768]{2,1,0:T(8,128)(2,1)} %constant_dynamic-slice_fusion.1) | copy-start | bytes 147460
  156.3 2.8 copy-start.13
  159.1 1.5 copy-start.46
  159.1 1.5 copy-start.47
  162.5 17.6 %slice-start = ((bf16[1056,768]{1,0:T(8,128)(2,1)}), bf16[1024,768]{1,0:T(8,128)(2,1)S(1)}, s32[]{:S(2)}) async-start(bf16[1056,768]{1,0:T(8,128)(2,1)} %copy-done.17), calls=%async_computation.3 | async-start | bytes 3145728 | tf_op jit(solution)/shard_map/slice | solution.py:369
  215.3 1.5 copy-start.21
  217.0 4.5 slice-start.3
  218.1 4.1 slice-start.4
  240.6 5.4 copy-start.18
  316.5 349.9 %all-reduce.3.cloned.1.call-start = ((), (), s32[]{:S(2)}) async-start(), calls=%async_computation.2 | async-start | bytes 3538944 | tf_op jit(solution)/shard_map/psum | solution.py:425
  316.6 9.7 %copy-start.33 = (pred[2,512]{1,0:T(4,128)(4,1)S(1)}, pred[2,512]{1,0:T(4,128)(4,1)}, u32[]{:S(2)}) copy-start(pred[2,512]{1,0:T(4,128)(4,1)} %get-tuple-element.48) | copy-start | bytes 3076
  326.1 1.8 copy-start.22
  326.2 6.1 copy-start.11
  326.2 6.1 copy-start.26
  326.2 6.1 copy-start.28
  326.2 6.0 copy-start.32
  327.9 13.0 %copy-start.14 = (f32[1056,768]{1,0:T(8,128)S(1)}, f32[1056,768]{1,0:T(8,128)}, u32[]{:S(2)}) copy-start(f32[1056,768]{1,0:T(8,128)} %copy-done.13) | copy-start | bytes 9732100
  327.9 333.6 %collective-permute-start.1 = (bf16[2,256,768]{2,1,0:T(8,128)(2,1)}, bf16[2,256,768]{2,1,0:T(8,128)(2,1)}, u32[]{:S(2)}, u32[]{:S(2)}) collective-permute-start(bf16[2,256,768]{2,1,0:T(8,128)(2,1)} %get-tuple-element.53), channel_id=1, source_target_pairs={{0,4},{4,8},{8,12},{12,16},{16,20},{20,24},{24,28},{28,0},{1,5},{5... | collective-permute-start | bytes 2359304 | tf_op jit(solution)/shard_map/ppermute | solution.py:390
  343.9 242.2 %copy-start.45 = (u32[32]{0:T(128)S(1)}, u32[32]{0:T(128)}, u32[]{:S(2)}) copy-start(u32[32]{0:T(128)} %constant.116) | copy-start | bytes 388
  343.9 245.6 %copy-start.38 = (f32[768]{0:T(1024)S(1)}, f32[768]{0:T(1024)}, u32[]{:S(2)}) copy-start(f32[768]{0:T(1024)} %get-tuple-element.37) | copy-start | bytes 9220
  343.9 245.7 %copy-start.36 = (f32[768]{0:T(1024)S(1)}, f32[768]{0:T(1024)}, u32[]{:S(2)}) copy-start(f32[768]{0:T(1024)} %get-tuple-element.43) | copy-start | bytes 9220
  343.9 245.7 %copy-start.39 = (f32[768]{0:T(1024)S(1)}, f32[768]{0:T(1024)}, u32[]{:S(2)}) copy-start(f32[768]{0:T(1024)} %get-tuple-element.39) | copy-start | bytes 9220
  345.2 318.9 %collective-permute-start.3 = (bf16[2,256,768]{2,1,0:T(8,128)(2,1)}, bf16[2,256,768]{2,1,0:T(8,128)(2,1)}, u32[]{:S(2)}, u32[]{:S(2)}) collective-permute-start(bf16[2,256,768]{2,1,0:T(8,128)(2,1)} %get-tuple-element.49), channel_id=1, source_target_pairs={{0,4},{4,8},{8,12},{12,16},{16,20},{20,24},{24,28},{28,0},{1,5},{5... | collective-permute-start | bytes 2359304 | tf_op jit(solution)/shard_map/ppermute | solution.py:392
  660.3 3.8 copy-start.20
  666.5 3.7 copy-start.15
  (11 other events, 10.9 us)
Sparse Core Ops, SparseCore 0:
  316.7 269.3 reduce-scatter.1
  588.4 45.1 all-reduce.2

commit v2 on v1

--- a/solution.py
+++ b/solution.py
@@ -1,4 +1,6 @@
 import functools
+import math
+
 import jax
 import jax.numpy as jnp
 from jax import lax
@@ -95,8 +97,13 @@
     return jnp.where(lane < HEADS, top, jnp.where(lane < 2 * HEADS, mid, jnp.where(lane < 3 * HEADS, low, zero)))
 
 
-def attend_back_kernel(half, scale, tk, q_ref, k_ref, v_ref, g_ref, lse_ref, delta_ref, kaug_ref, dq_ref, dk_ref, dv_ref):
-    pair = pl.program_id(1)
+def attend_back_step(half, scale, tk, q_ref, k_ref, v_ref, g_ref, lse_ref, delta_ref, *refs):
+    attend_back_kernel(
+        half, scale, tk, pl.program_id(1), q_ref, k_ref, v_ref, g_ref[0], lse_ref[0], delta_ref[0], *refs
+    )
+
+
+def attend_back_kernel(half, scale, tk, pair, q_ref, k_ref, v_ref, g, lse, delta, kaug_ref, dq_ref, dk_ref, dv_ref):
     rows = q_ref.shape[1]
     zero = jnp.zeros((), jnp.bfloat16)
     one = jnp.ones((), jnp.bfloat16)
@@ -104,9 +111,8 @@
     row = lax.broadcasted_iota(jnp.int32, (rows, LANES), 0)
     low = lane < LANES // 2
     q = (q_ref[0].astype(jnp.float32) * scale).astype(jnp.bfloat16)
-    g = g_ref[0]
-    qaug = jnp.where(type_marks(rows, half, lane, row), one, three_parts(lse_ref[0], lane))
-    gaug = three_parts(delta_ref[0], lane)
+    qaug = jnp.where(type_marks(rows, half, lane, row), one, three_parts(lse, lane))
+    gaug = three_parts(delta, lane)
     qx = jnp.concatenate([q, qaug], axis=1)
     gx = jnp.concatenate([g, gaug], axis=1)
     sels = (low, jnp.logical_not(low))
@@ -149,7 +155,7 @@
     whole = pl.BlockSpec((1, rows, LANES), lambda r, p: (r, 0, 0))
     out = jax.ShapeDtypeStruct((row_count, rows, width), jnp.bfloat16)
     return pl.pallas_call(
-        functools.partial(attend_back_kernel, half, scale, tk),
+        functools.partial(attend_back_step, half, scale, tk),
         grid=(row_count, pairs),
         in_specs=[spec(0), spec(pairs), spec(2 * pairs), spec(0), whole, whole, whole],
         out_specs=[spec(0)] * 3,
@@ -219,6 +225,994 @@
     )(*arrays)
 
 
+SEQ_BITS = (("z1", 4), ("z0", 2), ("x", 1))
+BATCH_BITS = (("y", 2), ("c", 1))
+
+
+class Place:
+    def __init__(self):
+        self.spot, self.step = {}, {}
+        for name, bits in (("seq", SEQ_BITS), ("batch", BATCH_BITS)):
+            index = lax.axis_index(name)
+            for axis, weight in bits:
+                bit = lax.rem(lax.div(index, weight), 2)
+                self.spot[axis] = bit
+                self.step[axis] = {name: index + weight * (1 - 2 * bit)}
+
+    def __getitem__(self, axis):
+        return self.spot[axis]
+
+    def partner(self, axis):
+        return self.step[axis]
+
+    def greet(self, others=()):
+        barrier = pltpu.get_barrier_semaphore()
+        peers = list(self.step.values()) + list(others)
+        for to in peers:
+            pl.semaphore_signal(barrier, inc=1, device_id=to, device_id_type=MESH_ID)
+        pl.semaphore_wait(barrier, len(peers))
+
+
+def remote(src, dst, send, recv, to):
+    return pltpu.make_async_remote_copy(
+        src_ref=src, dst_ref=dst, send_sem=send, recv_sem=recv, device_id=to, device_id_type=MESH_ID
+    )
+
+
+class Halve:
+    def __init__(self, place, own, lanes, order, bufs, send, recv, first, stages=None):
+        self.place, self.own, self.order = place, own, order
+        self.lanes = pl.ds(*lanes)
+        self.half = own.shape[3] // 2
+        stages = range(len(order)) if stages is None else stages
+        self.bufs = dict(zip(stages, bufs))
+        self.copies = {
+            n: remote(
+                own.at[self.region(n, False)], self.bufs[n], send.at[first + n], recv.at[first + n], place.partner(order[n])
+            )
+            for n in stages
+        }
+
+    @staticmethod
+    def buffers(rows, width, order, stages=None, dtype=jnp.bfloat16):
+        shapes = []
+        for n in range(len(order)) if stages is None else stages:
+            left = [axis for axis, _ in SEQ_BITS if axis not in order[:n + 1]]
+            shapes.append((2,) * len(left) + (rows // 2 if "y" in order[:n + 1] else rows, width))
+        return [pltpu.VMEM(shape, dtype) for shape in shapes]
+
+    def region(self, n, mine, free=(), piece=None):
+        free = list(free)
+        at = []
+        for axis, _ in SEQ_BITS:
+            if axis in self.order[:n]:
+                at.append(self.place[axis])
+            elif axis == self.order[n]:
+                at.append(self.place[axis] if mine else 1 - self.place[axis])
+            else:
+                at.append(free.pop(0) if free else slice(None))
+        first, count = 0, self.own.shape[3]
+        if "y" in self.order[:n + 1]:
+            y = self.place["y"]
+            y = y if mine or self.order[n] != "y" else 1 - y
+            first, count = y * self.half, self.half
+        if piece is not None:
+            first, count = first + piece[0], piece[1]
+        rows = pl.ds(pl.multiple_of(first, 16), count)
+        return (*at, rows, self.lanes)
+
+    def start(self, n):
+        self.copies[n].start()
+
+    def finish(self, n):
+        self.copies[n].wait_recv()
+        buf = self.bufs[n]
+        dims = len(buf.shape) - 2
+        count = buf.shape[-2]
+        piece = math.gcd(count, 48)
+        pieces = count // piece
+
+        def add(i, carry):
+            block, row = lax.div(i, pieces), lax.rem(i, pieces) * piece
+            free = [lax.rem(lax.div(block, 2 ** (dims - 1 - d)), 2) for d in range(dims)]
+            at = self.region(n, True, free, (row, piece))
+            more = buf[(*free, pl.ds(pl.multiple_of(row, 16), piece), slice(None))]
+            self.own[at] = (self.own[at].astype(jnp.float32) + more.astype(jnp.float32)).astype(self.own.dtype)
+            return carry
+
+        lax.fori_loop(0, 2 ** dims * pieces, add, 0)
+
+
+class Gather:
+    order = ("z1", "z0", "x")
+
+    def __init__(self, place, buf, send, recv):
+        self.copies = []
+        for n, axis in enumerate(self.order):
+            at = tuple(slice(None) if other in self.order[:n] else place[other] for other, _ in SEQ_BITS)
+            self.copies.append(remote(buf.at[at], buf.at[at], send.at[n], recv.at[n], place.partner(axis)))
+
+    def stage(self, n):
+        if n > 0:
+            self.copies[n - 1].wait_recv()
+        if n < 3:
+            self.copies[n].start()
+
+    def finish(self):
+        for copy in self.copies:
+            copy.wait_send()
+
+
+PARTS = (
+    ((0, 256), ("x", "y", "z0", "z1")),
+    ((256, 256), ("y", "x", "z0", "z1")),
+    ((512, 256), ("z0", "z1", "x", "y")),
+)
+
+
+class Fold:
+    EARLY, LATE = (0, 1), (2, 3)
+
+    def __init__(self, place, pieces, refs, source=None, stages=(0, 1, 2, 3)):
+        self.place = place
+        c, y = place["c"], place["y"]
+        if stages == self.LATE:
+            self.own, self.done, send, recv, *bufs = refs
+            self.got = local = None
+        elif source is None:
+            self.own, self.done, *refs = refs
+        else:
+            self.own, self.done = source.at[:, :, :, c], None
+        if stages != self.LATE:
+            self.got, send, recv, local, *bufs = refs
+        own, got, done = self.own, self.got, self.done
+        rows = own.shape[3]
+        half = rows // 2
+        self.mine = pl.ds(pl.multiple_of(y * half, 16), half)
+        at, self.keep, self.core = 0, [], []
+        if stages == self.LATE:
+            pieces = ()
+        if source is not None:
+            self.core.append(remote(source.at[:, :, :, 1 - c], got, send.at[0], recv.at[0], place.partner("c")))
+            pieces = ()
+        for n, (take, count) in enumerate(pieces):
+            spot = pl.ds(at, count)
+            self.keep.append(pltpu.make_async_copy(take(c), own.at[:, :, :, spot], local.at[n]))
+            self.core.append(
+                remote(take(1 - c), got.at[:, :, :, spot], send.at[n], recv.at[n], place.partner("c"))
+            )
+            at += count
+        first = len(self.core)
+        self.parts = []
+        for n, (lanes, order) in enumerate(PARTS):
+            own_bufs = bufs[len(stages) * n:len(stages) * (n + 1)]
+            self.parts.append(Halve(place, own, lanes, order, own_bufs, send, recv, first + 4 * n, stages))
+        first += 12
+        if done is None:
+            return
+        self.across = remote(
+            done.at[c, self.mine], done.at[c, self.mine], send.at[first], recv.at[first], place.partner("y")
+        )
+        self.back = remote(done.at[c], done.at[c], send.at[first + 1], recv.at[first + 1], place.partner("c"))
+
+    @staticmethod
+    def scratch(rows, width, pieces, sourced=False, stages=(0, 1, 2, 3)):
+        vmem = lambda *shape: pltpu.VMEM(shape, jnp.bfloat16)
+        refs = [] if sourced else [vmem(2, 2, 2, rows, width), vmem(2, rows, width)]
+        if stages != Fold.LATE:
+            refs.append(vmem(2, 2, 2, rows, width))
+        refs += [
+            pltpu.SemaphoreType.DMA((pieces + 14,)),
+            pltpu.SemaphoreType.DMA((pieces + 14,)),
+        ]
+        if stages != Fold.LATE:
+            refs.append(pltpu.SemaphoreType.DMA((pieces,)))
+        for (_, count), order in PARTS:
+            refs += Halve.buffers(rows, count, order, stages)
+        return refs
+
+    def stage(self, n):
+        if n == 0:
+            for copy in self.keep + self.core:
+                copy.start()
+        elif n == 1:
+            for copy in self.keep:
+                copy.wait()
+            for copy in self.core:
+                copy.wait_recv()
+
+            piece = math.gcd(self.got.shape[3], 48)
+            pieces = self.got.shape[3] // piece
+
+            def add(i, carry):
+                block = lax.div(i, pieces)
+                rows = pl.ds(pl.multiple_of(lax.rem(i, pieces) * piece, 16), piece)
+                at = (*(lax.rem(lax.div(block, w), 2) for _, w in SEQ_BITS), rows)
+                total = self.own[at].astype(jnp.float32) + self.got[at].astype(jnp.float32)
+                self.own[at] = total.astype(jnp.bfloat16)
+                return carry
+
+            lax.fori_loop(0, 8 * pieces, add, 0)
+            for part in self.parts:
+                part.start(0)
+        elif n < 5:
+            for part in self.parts:
+                part.finish(n - 2)
+                part.start(n - 1)
+        elif n == 5:
+            for part in self.parts:
+                part.finish(3)
+            at = tuple(self.place[axis] for axis, _ in SEQ_BITS)
+            self.done[self.place["c"], self.mine] = self.own[(*at, self.mine)]
+            self.across.start()
+        elif n == 6:
+            self.across.wait_recv()
+            self.back.start()
+        else:
+            self.back.wait_recv()
+
+    def held(self):
+        z1, z0, x = (self.place[axis] for axis, _ in SEQ_BITS)
+        a, b, c = (lanes[1] for lanes, _ in PARTS)
+        return (slice(None), slice(None), x, self.mine, pl.ds(0, a + b)), (
+            z1, z0, slice(None), slice(None), pl.ds(a + b, c)
+        )
+
+    def resume(self, ab, last):
+        first, second = self.held()
+        self.own[first] = ab[...]
+        self.own[second] = last[...]
+        for part in self.parts:
+            part.start(2)
+
+    def finish(self):
+        for copy in self.core + [self.across, self.back]:
+            copy.wait_send()
+        for part in self.parts:
+            for copy in part.copies.values():
+                copy.wait_send()
+
+
+class Sum:
+    order = ("c", "x", "y", "z0", "z1")
+
+    def __init__(self, place, value, got, send, recv):
+        self.value, self.got = value, got
+        self.copies = [
+            remote(value.at[n], got.at[n], send.at[n], recv.at[n], place.partner(axis))
+            for n, axis in enumerate(self.order)
+        ]
+
+    def stage(self, n):
+        if n > 0:
+            self.copies[n - 1].wait_recv()
+            self.value[n] = self.value[n - 1] + self.got[n - 1]
+        if n < 5:
+            self.copies[n].start()
+
+    def finish(self):
+        for copy in self.copies:
+            copy.wait_send()
+
+
+def share_views(a, count):
+    *lead, rows, width = a.shape
+    return a.reshape(*lead, 2, 2, 2, rows // count, width)
+
+
+def half_views(a, count):
+    *lead, rows, width = a.shape
+    return a.reshape(*lead, 2, 2, 2, 2, rows // (2 * count), width)
+
+
+def write_big(first, second, inner_o, outer_o):
+    width = outer_o.shape[1]
+    part = inner_o.shape[0]
+    half = outer_o.shape[0] // 2
+    strips = inner_o.shape[1] // width // 2
+    for c in range(2):
+        for j in range(strips):
+            inner_o[:, pl.ds((c * strips + j) * width, width)] = first.done[c, pl.ds(j * part, part)].astype(jnp.float32)
+        outer_o[pl.ds(c * half, half)] = second.done[c].astype(jnp.float32)
+
+
+def begin(copies):
+    for copy in copies:
+        copy.start()
+
+
+def sum_rows(values):
+    rows, width = values.shape
+    return jnp.sum(values.reshape(rows // 8, 8, width), axis=0)
+
+
+def ticks(plan, folds, step):
+    for t, todo in plan.items():
+
+        @pl.when(step == t)
+        def _():
+            for f, n in todo:
+                folds[f].stage(n)
+
+
+REAR_TICKS = {
+    0: ((0, 0),),
+    2: ((0, 1),),
+    3: ((3, 4),),
+    5: ((3, 5),),
+    6: ((0, 2),),
+    7: ((3, 6),),
+    8: ((3, 7),),
+    10: ((0, 3),),
+    13: ((0, 4),),
+    14: ((1, 0),),
+    15: ((0, 5),),
+    16: ((1, 1), (2, 0)),
+    17: ((0, 6),),
+    18: ((2, 1), (0, 7)),
+    19: ((1, 2),),
+    20: ((2, 2),),
+}
+REAR_END = (
+    (5, 1), (4, 1), (1, 3), (5, 2), (4, 2), (2, 3), (5, 3), (1, 4), (4, 3), (5, 4), (2, 4), (5, 5), (1, 5), (2, 5), (1, 6),
+    (2, 6), (1, 7), (2, 7),
+)
+SPREAD_TICKS = {15: 0, 17: 1, 20: 2}
+
+
+def rear_kernel(
+    half, scale, pairs, fold_refs,
+    q_ref, k_ref, v_ref, g_ref, lse_ref, delta_ref, kaug_ref,
+    x_ref, res_ref, gg_ref, glse_ref, gdelta_ref, gx_ref, gres_ref, normed_ref, globals_ref, weight_ref, gain_ref,
+    vectors_ref, outer_ab_ref, outer_c_ref, inner, out,
+    igrad_o, ggrad_o, inner_o, outer_o, out_o, qkv_o, small_o,
+    dqkv, gfirst, sums, qkv_src, grads, ggrad, value, got,
+    send, recv, local, *scratch,
+):
+    step = pl.program_id(0)
+    place = Place()
+    me = lax.axis_index("seq")
+    count = lax.axis_size("seq")
+    row_count, rows, cols = dqkv.shape
+    block_len = 2 * half
+    width = cols // 3
+    share = gx_ref.shape[1]
+    attn = row_count * pairs
+    strips = inner.shape[0] // 2
+    part_rows = inner.shape[4]
+    half_part = part_rows // 2
+    sources = (
+        [(lambda c, j=j: inner.at[c * strips + j], part_rows) for j in range(strips)],
+        [(lambda c: out.at[:, :, :, c], half_part), (lambda c: qkv_src.at[0, :, :, :, c], half_part)],
+        [(lambda c, j=j: qkv_src.at[j, :, :, :, c], half_part) for j in (1, 2)],
+    )
+    folds, at = [], 0
+    for pieces, size in zip(sources, fold_refs[:3]):
+        folds.append(Fold(place, pieces, scratch[at:at + size]))
+        at += size
+    folds.append(Fold(place, (), scratch[at:at + fold_refs[3]], None, Fold.LATE))
+    at += fold_refs[3]
+    spread = Halve(place, gfirst, (0, width), ("x", "z0", "z1"), scratch[at:], send.at[0], recv.at[0], 0)
+    gather = Gather(place, ggrad, send.at[row_count], recv.at[row_count])
+    small = Sum(place, value, got, send.at[row_count + 1], recv.at[row_count + 1])
+    following = {"seq": lax.rem(me + 1, count)}
+    before = {"seq": lax.rem(me + count - 1, count)}
+    home = [
+        remote(
+            grads.at[1, r], igrad_o.at[r, pl.ds(0, half)], send.at[row_count + 2, r], recv.at[row_count + 2, r], following
+        )
+        for r in range(row_count)
+    ]
+    keep = [
+        pltpu.make_async_copy(grads.at[0, r], igrad_o.at[r, pl.ds(half, half)], local.at[r]) for r in range(row_count)
+    ]
+
+    @pl.when(step == 0)
+    def _():
+        place.greet([following, before])
+        sums[...] = jnp.zeros_like(sums)
+        folds[3].resume(outer_ab_ref, outer_c_ref)
+
+    ticks(REAR_TICKS, folds, step)
+
+    @pl.when(step < attn)
+    def _():
+        r, p = lax.div(step, pairs), lax.rem(step, pairs)
+        spots = [pl.ds(pl.multiple_of(j * width + p * LANES, LANES), LANES) for j in range(3)]
+        lane = pl.ds(pl.multiple_of(p * LANES, LANES), LANES)
+        wide = lambda a, b: jnp.concatenate([a, b.reshape(rows - block_len, LANES)], axis=0)
+        attend_back_kernel(
+            half, scale, 320, p, q_ref, k_ref, v_ref, wide(g_ref[...], gg_ref[:, :, :, r, :, lane]),
+            wide(lse_ref[0], glse_ref[:, :, :, r]), wide(delta_ref[...], gdelta_ref[:, :, :, r]), kaug_ref,
+            *(dqkv.at[pl.ds(r, 1), :, spot] for spot in spots),
+        )
+
+    strip_at = step - (attn + 1)
+
+    @pl.when((strip_at >= 0) & (strip_at < 3))
+    def _():
+        strip = pl.ds(pl.multiple_of(strip_at * width, width), width)
+        total = tn(normed_ref[0], dqkv[0, :, strip])
+        for r in range(1, row_count):
+            total = total + tn(normed_ref[r], dqkv[r, :, strip])
+        qkv_src[strip_at] = total.astype(jnp.bfloat16).reshape(qkv_src.shape[1:])
+
+    for t, n in SPREAD_TICKS.items():
+
+        @pl.when(step == t)
+        def _():
+            spread.finish(n)
+            if n < 2:
+                spread.start(n + 1)
+
+    gain = gain_ref[...]
+
+    def stats(x):
+        centred = x - jnp.mean(x, axis=-1, keepdims=True)
+        inv = lax.rsqrt(jnp.mean(centred * centred, axis=-1, keepdims=True) + EPS)
+        return centred * inv, inv
+
+    def add_sums(first, n):
+        sums[0] += sum_rows(first * n)
+        sums[1] += sum_rows(first)
+
+    def through(first, n, inv):
+        eg = first * gain
+        return (eg - jnp.mean(eg, axis=-1, keepdims=True) - n * jnp.mean(eg * n, axis=-1, keepdims=True)) * inv
+
+    @pl.when(step == attn)
+    def _():
+        own = pl.ds(block_len, rows - block_len)
+        partial = jnp.concatenate([dqkv[r, own] for r in range(row_count)], axis=0)
+        first = nt(partial, weight_ref[...])
+        n, _ = stats(globals_ref[...].astype(jnp.float32).reshape(first.shape))
+        add_sums(first, n)
+        first = first.astype(jnp.bfloat16).reshape(row_count, 2, 2, 2, share, width)
+        for r in range(row_count):
+            gfirst[:, :, :, pl.ds(r * share, share)] = first[r]
+        spread.start(0)
+
+    tiles = attn + 4
+    tile = step - tiles
+
+    @pl.when((tile >= 0) & (tile < 2 * row_count))
+    def _():
+        r, h = lax.rem(tile, row_count), 1 - lax.div(tile, row_count)
+        spot = pl.ds(pl.multiple_of(h * half, half), half)
+        first = nt(dqkv[r, spot], weight_ref[...])
+        n, inv = stats(x_ref[...].astype(jnp.float32))
+        add_sums(first, n)
+        grads[h, r] = (res_ref[...] + through(first, n, inv)).astype(jnp.bfloat16)
+
+    for r in range(row_count):
+
+        @pl.when(tile == r)
+        def _():
+            home[r].start()
+
+        @pl.when(tile == row_count + r)
+        def _():
+            keep[r].start()
+
+    after = tiles + 2 * row_count
+
+    @pl.when(step == after)
+    def _():
+        lines = [jnp.sum(sums[n], axis=0, keepdims=True) for n in range(2)]
+        value[0] = jnp.concatenate(lines + [vectors_ref[...]])
+        small.stage(0)
+        own_rows = row_count * share
+        at = tuple(place[axis] for axis, _ in SEQ_BITS)
+        n, inv = stats(gx_ref[...].astype(jnp.float32).reshape(own_rows, width))
+        grad = gres_ref[...].reshape(own_rows, width) + through(gfirst[at].astype(jnp.float32), n, inv)
+        ggrad[at] = grad.astype(jnp.bfloat16).reshape(row_count, share, width)
+        gather.stage(0)
+
+    @pl.when(step == after + 1)
+    def _():
+        write_big(folds[0], folds[3], inner_o, outer_o)
+        leave = pltpu.make_async_copy(ggrad, ggrad_o, local.at[row_count])
+        movers = folds + [gather, small]
+        for f, n in REAR_END:
+            movers[f].stage(n)
+            if (f, n) == (4, 3):
+                leave.start()
+        small_o[...] = value[5]
+        f32 = jnp.float32
+        for c in range(2):
+            spot = pl.ds(c * half_part, half_part)
+            first, second = pl.ds(0, half_part), pl.ds(half_part, half_part)
+            out_o[spot] = folds[1].done[c, first].astype(f32)
+            for j, (fold, lines) in enumerate(((folds[1], second), (folds[2], first), (folds[2], second))):
+                qkv_o[spot, pl.ds(j * width, width)] = fold.done[c, lines].astype(f32)
+        for fold in folds:
+            fold.finish()
+        gather.finish()
+        small.finish()
+        for copy in spread.copies.values():
+            copy.wait_send()
+        for copy in keep + home + [leave]:
+            copy.wait()
+
+
+def rear(
+    qkv, grad, lse, delta, kaug, tokens, res_grad, global_grad, global_lse, global_delta, own_globals, own_res, normed,
+    globals_in, weight, gain, vectors, outer_ab, outer_c, inner, out, half, count,
+):
+    row_count, rows, cols = qkv.shape
+    width = cols // 3
+    pairs = width // LANES
+    block_len = 2 * half
+    global_count = rows - block_len
+    share = global_count // count
+    part = width // count
+    scale = (width // HEADS) ** (-0.5)
+    attn = row_count * pairs
+    f32, bf16 = jnp.float32, jnp.bfloat16
+    row_of = lambda t: jnp.minimum(t, attn - 1) // pairs
+    pair_of = lambda t: jnp.minimum(t, attn - 1) % pairs
+    spec = lambda off: pl.BlockSpec((1, rows, LANES), lambda t: (row_of(t), 0, off + pair_of(t)))
+    whole = pl.BlockSpec((1, rows, LANES), lambda t: (row_of(t), 0, 0))
+
+    def tile_of(t):
+        n = jnp.clip(t - attn - 4, 0, 2 * row_count - 1)
+        return n % row_count * 2 + 1 - n // row_count, 0
+
+    fixed = lambda a: pl.BlockSpec(a.shape, lambda t: (0,) * a.ndim, pipeline_mode=pl.Buffered(1))
+    tile = pl.BlockSpec((half, width), tile_of)
+    hbm = pl.BlockSpec(memory_space=pl.ANY)
+    outs = [
+        jax.ShapeDtypeStruct((row_count, block_len, width), bf16),
+        jax.ShapeDtypeStruct((2, 2, 2, row_count, share, width), bf16),
+        jax.ShapeDtypeStruct((part, 4 * width), f32),
+        jax.ShapeDtypeStruct((4 * part, width), f32),
+        jax.ShapeDtypeStruct((part, width), f32),
+        jax.ShapeDtypeStruct((part, 3 * width), f32),
+        jax.ShapeDtypeStruct((8, width), f32),
+    ]
+    folds, sizes = [], []
+    for size, pieces in ((2 * part, 2), (part, 2), (part, 2)):
+        refs = Fold.scratch(size, width, pieces)
+        folds += refs
+        sizes.append(len(refs))
+    refs = Fold.scratch(2 * part, width, 0, False, Fold.LATE)
+    folds += refs
+    sizes.append(len(refs))
+    vmem = pltpu.VMEM
+    kinds = 4 + row_count
+    fixeds = (
+        global_grad, global_lse, global_delta, own_globals, own_res, normed, globals_in, weight, gain, vectors,
+        outer_ab, outer_c,
+    )
+    return pl.pallas_call(
+        functools.partial(rear_kernel, half, scale, pairs, tuple(sizes)),
+        grid=(attn + 4 + 2 * row_count + 2,),
+        in_specs=[spec(0), spec(pairs), spec(2 * pairs)]
+        + [pl.BlockSpec((block_len, LANES), lambda t: (row_of(t), pair_of(t)))]
+        + [pl.BlockSpec((1, block_len, LANES), lambda t: (row_of(t), 0, 0))]
+        + [pl.BlockSpec((block_len, LANES), lambda t: (row_of(t), 0)), whole]
+        + [tile, tile]
+        + [fixed(a) for a in fixeds]
+        + [hbm] * 2,
+        out_specs=[hbm] * 2 + [pl.BlockSpec(memory_space=pltpu.VMEM)] * 5,
+        out_shape=outs,
+        scratch_shapes=[
+            vmem((row_count, rows, cols), bf16),
+            vmem((2, 2, 2, row_count * share, width), bf16),
+            vmem((2, 8, width), f32),
+            vmem((3, 2, 2, 2, 2, part // 2, width), bf16),
+            vmem((2, row_count, half, width), bf16),
+            vmem((2, 2, 2, row_count, share, width), bf16),
+            vmem((6, 8, width), f32),
+            vmem((5, 8, width), f32),
+            pltpu.SemaphoreType.DMA((kinds, 5)),
+            pltpu.SemaphoreType.DMA((kinds, 5)),
+            pltpu.SemaphoreType.DMA((1 + row_count,)),
+        ]
+        + folds
+        + Halve.buffers(row_count * share, width, ("x", "z0", "z1")),
+        compiler_params=pltpu.CompilerParams(
+            collective_id=9, has_side_effects=True, vmem_limit_bytes=64 * 1024 * 1024
+        ),
+        name="rear",
+    )(
+        qkv, qkv, qkv, grad, lse, delta, kaug, tokens, res_grad, *fixeds,
+        share_views(inner, count), half_views(out, count),
+    )
+
+
+def cdf_bell(v):
+    bell = jnp.exp(-0.5 * v * v)
+    t = 1.0 / (1.0 + (0.3275911 * 0.5 ** 0.5) * jnp.abs(v))
+    poly = t * (
+        0.127414796 + t * (-0.142248368 + t * (0.7107068705 + t * (-0.7265760135 + t * 0.5307027145)))
+    )
+    tail = poly * bell
+    return jnp.where(v < 0, tail, 1.0 - tail), bell
+
+
+MID_TICKS = {9: 0, 11: 1, 14: 2}
+MID_GATHERS = {6: (0, 1), 8: (0, 2), 10: (0, 3), 11: (1, 1), 12: (1, 2), 13: (1, 3)}
+
+
+def mid_kernel(
+    half, fold_refs,
+    lengths, x_ref, mixed_ref, cot_ref, gx_ref, gcot_ref, out_w, inner_w, outer_w, bias_ref, gain_ref, shift_ref, heads_ref,
+    mixed_all, lse_all,
+    layer_o, res_o, grad_o, delta_o, gres_o, gout_o, ggrad_o, glse_o, gdelta_o, inner_o, outer_ab_o, outer_c_o, out_o,
+    vectors_o,
+    hidden, slope, normed, cot, att, proj, residual, outer_src, sums, bias_sums, layers,
+    gout, ggrad, glse, gdelta, part_mixed, part_lse, send, recv, local, *scratch,
+):
+    f32, bf16 = jnp.float32, jnp.bfloat16
+    step = pl.program_id(0)
+    place = Place()
+    me = lax.axis_index("seq")
+    count = lax.axis_size("seq")
+    row_count, share = gx_ref.shape[:2]
+    block_len = 2 * half
+    tokens = row_count * block_len
+    own_rows = row_count * share
+    width = gx_ref.shape[2]
+    strips = inner_w.shape[1] // width
+    tiles = 2 * row_count
+    fold = Fold(place, None, scratch, outer_src, Fold.EARLY)
+    following = {"seq": lax.rem(me + 1, count)}
+    at = tuple(place[axis] for axis, _ in SEQ_BITS)
+
+    def parts(m, to, r, n):
+        rows = pl.ds(pl.multiple_of(block_len + share * to, 16), share)
+        return (
+            (mixed_all.at[r, rows], part_mixed.at[m, r]) if n == 0 else (lse_all.at[r, rows], part_lse.at[m, r])
+        )
+
+    part_copies, part_own = [], []
+    for r in range(row_count):
+        for n in range(2):
+            src, dst = parts(me, me, r, n)
+            part_own.append(pltpu.make_async_copy(src, dst, local.at[2 * r + n]))
+            for other in range(1, count):
+                to = lax.rem(me + other, count)
+                src, dst = parts(me, to, r, n)
+                part_copies.append(remote(src, dst, send.at[2 * r + n, other], recv.at[2 * r + n, other], {"seq": to}))
+    base = 2 * row_count
+    gathers = [
+        Gather(place, buf, send.at[base + n], recv.at[base + n]) for n, buf in enumerate((gout, ggrad, glse, gdelta))
+    ]
+    leaves = [
+        pltpu.make_async_copy(buf, o, local.at[base + n])
+        for n, (buf, o) in enumerate(((gout, gout_o), (ggrad, ggrad_o), (glse, glse_o), (gdelta, gdelta_o)))
+    ]
+    base += 4
+    home = [
+        remote(layers.at[1, r], layer_o.at[r, pl.ds(0, half)], send.at[base, r], recv.at[base, r], following)
+        for r in range(row_count)
+    ]
+    keep = [
+        pltpu.make_async_copy(layers.at[0, r], layer_o.at[r, pl.ds(half, half)], local.at[base + r]) for r in range(row_count)
+    ]
+    gain, shift = gain_ref[...], shift_ref[...]
+
+    @pl.when(step == 0)
+    def _():
+        place.greet([{"seq": lax.rem(me + other, count)} for other in range(1, count)])
+        begin(part_own + part_copies)
+        sums[...] = jnp.zeros_like(sums)
+        bias_sums[...] = jnp.zeros_like(bias_sums)
+
+    def stats(values):
+        centred = values - jnp.mean(values, axis=-1, keepdims=True)
+        inv = lax.rsqrt(jnp.mean(centred * centred, axis=-1, keepdims=True) + EPS)
+        return centred * inv, inv
+
+    def forward(x, attended, rows):
+        att[rows] = attended
+        total = x.astype(f32) + nn(attended, out_w[...])
+        residual[rows] = total
+        n, _ = stats(total)
+        second = (n * gain + shift).astype(bf16)
+        normed[rows] = second
+
+        def run(j, total):
+            strip = pl.ds(pl.multiple_of(j * width, width), width)
+            inner = nn(second, inner_w[:, strip]) + bias_ref[:, strip]
+            cdf, bell = cdf_bell(inner)
+            active = (inner * cdf).astype(bf16)
+            hidden[rows, strip] = active
+            slope[rows, strip] = (cdf + inner * bell * ((0.5 / math.pi) ** 0.5)).astype(bf16)
+            return total + nn(active, outer_w[strip, :])
+
+        return lax.fori_loop(0, strips, run, total)
+
+    def backward(cotangent, rows):
+        def run(j, total):
+            strip = pl.ds(pl.multiple_of(j * width, width), width)
+            grad = (nt(cotangent, outer_w[strip, :]) * slope[rows, strip].astype(f32)).astype(bf16)
+            slope[rows, strip] = grad
+            bias_sums[j] += sum_rows(grad.astype(f32))
+            return total + nt(grad, inner_w[:, strip])
+
+        second_grad = lax.fori_loop(0, strips, run, jnp.zeros(cotangent.shape, f32))
+        n, inv = stats(residual[rows])
+        eg = second_grad * gain
+        through = (eg - jnp.mean(eg, axis=-1, keepdims=True) - n * jnp.mean(eg * n, axis=-1, keepdims=True)) * inv
+        sums[0] += sum_rows(second_grad * n)
+        sums[1] += sum_rows(second_grad)
+        res = cotangent.astype(f32) + through
+        projected = res.astype(bf16)
+        proj[rows] = projected
+        grad = nt(projected, out_w[...]).astype(bf16)
+        product = grad.astype(f32) * att[rows].astype(f32)
+        top = product.astype(bf16)
+        rest = (product - top.astype(f32)).astype(bf16)
+        return res, grad, nn(top, heads_ref[...]) + nn(rest, heads_ref[...])
+
+    @pl.when(step < tiles)
+    def _():
+        r, h = lax.rem(step, row_count), 1 - lax.div(step, row_count)
+        rows = pl.ds(pl.multiple_of((2 * r + h) * half, half), half)
+        owner = lax.rem(me + h, count)
+        spot = owner * block_len + (1 - h) * half + lax.broadcasted_iota(jnp.int32, (half, width), 0)
+        valid = spot < lengths[r]
+        cot[rows] = jnp.where(valid, cot_ref[...].astype(f32), 0.0).astype(bf16)
+        final = forward(x_ref[...], mixed_ref[0], rows)
+        layers[h, r] = jnp.where(valid, final, 0.0).astype(bf16)
+
+    back = step - (tiles + 2 + strips)
+
+    @pl.when((back >= 0) & (back < tiles))
+    def _():
+        r, h = lax.rem(back, row_count), 1 - lax.div(back, row_count)
+        rows = pl.ds(pl.multiple_of((2 * r + h) * half, half), half)
+        res, grad, delta = backward(cot[rows], rows)
+        res_o[...] = res
+        grad_o[...] = grad
+        delta_o[...] = delta
+
+    for r in range(row_count):
+
+        @pl.when(step == r)
+        def _():
+            home[r].start()
+
+        @pl.when(step == row_count + r)
+        def _():
+            keep[r].start()
+
+    last = pl.ds(tokens, own_rows)
+
+    @pl.when(step == tiles)
+    def _():
+        for copy in part_own:
+            copy.wait()
+        for copy in part_copies:
+            copy.wait_recv()
+        peak = jnp.max(part_lse[...], axis=0)
+        shares = jnp.exp(part_lse[...] - peak)
+        total = jnp.sum(shares, axis=0)
+        lse = peak + jnp.log(total)
+        glse[at] = lse
+        shares = (shares / total).reshape(count * own_rows, LANES)
+        lane = lax.broadcasted_iota(jnp.int32, shares.shape, 1)
+        shares = jnp.where(lane < HEADS, shares, 0.0)
+        top = shares.astype(bf16)
+        rest = (shares - top.astype(f32)).astype(bf16)
+        wide = nt(top, heads_ref[...]) + nt(rest, heads_ref[...])
+        mixed = wide * part_mixed[...].reshape(count * own_rows, width).astype(f32)
+        mixed = jnp.sum(mixed.reshape(count, own_rows, width), axis=0).astype(bf16)
+        cot[last] = gcot_ref[...].reshape(own_rows, width)
+        final = forward(gx_ref[...].reshape(own_rows, width), mixed, last)
+        gout[at] = final.astype(bf16).reshape(row_count, share, width)
+        gathers[0].stage(0)
+
+    strip_at = step - (tiles + 1)
+
+    @pl.when((strip_at >= 0) & (strip_at < strips))
+    def _():
+        strip = pl.ds(pl.multiple_of(strip_at * width, width), width)
+        grad = tn(hidden[:, strip], cot[...]).astype(bf16)
+        outer_src[lax.div(strip_at, 2), lax.rem(strip_at, 2)] = grad.reshape(outer_src.shape[2:])
+
+    for t, (kind, n) in MID_GATHERS.items():
+
+        @pl.when(step == t)
+        def _():
+            chosen = range(1, 4) if kind else range(1)
+            for g in chosen:
+                gathers[g].stage(n)
+                if n == 3:
+                    leaves[g].start()
+
+    for t, n in MID_TICKS.items():
+
+        @pl.when(step == t)
+        def _():
+            fold.stage(n)
+
+    after = 2 * tiles + 1 + strips
+
+    @pl.when(step == tiles + 1 + strips)
+    def _():
+        res, grad, delta = backward(cot[last], last)
+        gres_o[...] = res.reshape(row_count, share, width)
+        ggrad[at] = grad.reshape(row_count, share, width)
+        gdelta[at] = delta.reshape(row_count, share, LANES)
+        for gather in gathers[1:]:
+            gather.stage(0)
+
+    inner_at = step - (after + 1)
+
+    @pl.when((inner_at >= 0) & (inner_at < strips))
+    def _():
+        strip = pl.ds(pl.multiple_of(inner_at * width, width), width)
+        inner_o[0] = tn(normed[...], slope[:, strip]).astype(bf16)
+
+    @pl.when(step == after + 1 + strips)
+    def _():
+        out_o[...] = tn(att[...], proj[...]).astype(bf16)
+        lines = [jnp.sum(sums[n], axis=0, keepdims=True) for n in range(2)]
+        lines += [jnp.sum(bias_sums[n], axis=0, keepdims=True) for n in range(strips)]
+        vectors_o[...] = jnp.concatenate(lines)
+        for part in fold.parts:
+            part.finish(1)
+        first, second = fold.held()
+        outer_ab_o[...] = fold.own[first]
+        outer_c_o[...] = fold.own[second]
+        for copy in fold.core:
+            copy.wait_send()
+        for part in fold.parts:
+            for copy in part.copies.values():
+                copy.wait_send()
+        for gather in gathers:
+            gather.finish()
+        for copy in part_copies:
+            copy.wait_send()
+        for copy in keep + home + leaves:
+            copy.wait()
+
+
+def mid(
+    lengths, tokens, mixed, lse, cotangent, own_globals, own_cot, out_weight, inner_weight, outer_weight, bias, gain, shift,
+    half, count,
+):
+    f32, bf16 = jnp.float32, jnp.bfloat16
+    row_count, rows, width = mixed.shape
+    block_len = 2 * half
+    share = (rows - block_len) // count
+    own_rows = row_count * share
+    inner_width = inner_weight.shape[1]
+    strips = inner_width // width
+    part = width // count
+    tiles = 2 * row_count
+    total = row_count * block_len + own_rows
+    lane, head = jnp.arange(LANES), jnp.arange(width) // (width // HEADS)
+    heads = ((lane[None, :] % HEADS == head[:, None]) & (lane[None, :] < 3 * HEADS)).astype(bf16)
+
+    def tile_at(first):
+        def place(t):
+            n = jnp.clip(t - first, 0, tiles - 1)
+            return n % row_count, 1 - n // row_count
+
+        return place
+
+    forward_at, back_at = tile_at(0), tile_at(tiles + 2 + strips)
+
+    def flat(where, cols):
+        def index(t):
+            r, h = where(t)
+            return 2 * r + h, 0
+
+        return pl.BlockSpec((half, cols), index)
+
+    fixed = lambda a: pl.BlockSpec(a.shape, lambda t: (0,) * a.ndim, pipeline_mode=pl.Buffered(1))
+    whole = lambda *shape: pl.BlockSpec(shape, lambda t: (0,) * len(shape))
+    hbm = pl.BlockSpec(memory_space=pl.ANY)
+    fixeds = (own_globals, own_cot, out_weight, inner_weight, outer_weight, bias[None], gain[None], shift[None], heads)
+    shared = (2, 2, 2, row_count, share)
+    after = 2 * tiles + 2 + strips
+    of = jax.ShapeDtypeStruct
+    outs = [
+        of((row_count, block_len, width), bf16),
+        of((row_count * block_len, width), f32),
+        of((row_count * block_len, width), bf16),
+        of((row_count * block_len, LANES), f32),
+        of((row_count, share, width), f32),
+        of((*shared, width), bf16),
+        of((*shared, width), bf16),
+        of((*shared, LANES), f32),
+        of((*shared, LANES), f32),
+        of((strips, width, width), bf16),
+        of((2, 2, strips * part // 4, 512), bf16),
+        of((2, strips * part // 2, 256), bf16),
+        of((width, width), bf16),
+        of((2 + strips, width), f32),
+    ]
+    vmem = pltpu.VMEM
+    fold = Fold.scratch(strips * part // 2, width, 1, True, Fold.EARLY)
+    kinds = 2 * row_count + 5
+    return pl.pallas_call(
+        functools.partial(mid_kernel, half, len(fold)),
+        grid=(after + strips + 1,),
+        in_specs=[
+            pl.BlockSpec(memory_space=pltpu.SMEM),
+            flat(forward_at, width),
+            pl.BlockSpec((1, half, width), lambda t: (*forward_at(t), 0)),
+            flat(forward_at, width),
+        ]
+        + [fixed(a) for a in fixeds]
+        + [hbm] * 2,
+        out_specs=[
+            hbm,
+            flat(back_at, width),
+            flat(back_at, width),
+            flat(back_at, LANES),
+            whole(row_count, share, width),
+            hbm,
+            hbm,
+            hbm,
+            hbm,
+            pl.BlockSpec((1, width, width), lambda t: (jnp.clip(t - after, 0, strips - 1), 0, 0)),
+            whole(*outs[10].shape),
+            whole(*outs[11].shape),
+            whole(width, width),
+            whole(2 + strips, width),
+        ],
+        out_shape=outs,
+        scratch_shapes=[
+            vmem((total, inner_width), bf16),
+            vmem((total, inner_width), bf16),
+            vmem((total, width), bf16),
+            vmem((total, width), bf16),
+            vmem((total, width), bf16),
+            vmem((total, width), bf16),
+            vmem((total, width), f32),
+            vmem((2, 2, 2, 2, strips * part // 2, width), bf16),
+            vmem((2, 8, width), f32),
+            vmem((strips, 8, width), f32),
+            vmem((2, row_count, half, width), bf16),
+            vmem((*shared, width), bf16),
+            vmem((*shared, width), bf16),
+            vmem((*shared, LANES), f32),
+            vmem((*shared, LANES), f32),
+            vmem((count, row_count, share, width), bf16),
+            vmem((count, row_count, share, LANES), f32),
+            pltpu.SemaphoreType.DMA((kinds, count)),
+            pltpu.SemaphoreType.DMA((kinds, count)),
+            pltpu.SemaphoreType.DMA((kinds + row_count,)),
+        ]
+        + fold,
+        compiler_params=pltpu.CompilerParams(
+            collective_id=10, has_side_effects=True, vmem_limit_bytes=64 * 1024 * 1024
+        ),
+        name="mid",
+    )(lengths, tokens, mixed, cotangent, *fixeds, mixed, lse)
+
+
+def wgrad_kernel(a_ref, b_ref, o_ref):
+    o_ref[...] = tn(a_ref[...], b_ref[...]).astype(o_ref.dtype).reshape(o_ref.shape)
+
+
+def wgrad(a, b, strip):
+    rows, a_cols = a.shape
+    b_cols = b.shape[1]
+    split_a = a_cols > b_cols
+    strips = max(a_cols, b_cols) // strip
+    fixed = lambda n: (0, 0)
+    moving = lambda n: (0, n)
+    return pl.pallas_call(
+        wgrad_kernel,
+        grid=(strips,),
+        in_specs=[
+            pl.BlockSpec((rows, strip), moving if split_a else fixed),
+            pl.BlockSpec((rows, strip), fixed if split_a else moving),
+        ],
+        out_specs=pl.BlockSpec((1, strip, strip), lambda n: (n, 0, 0)),
+        out_shape=jax.ShapeDtypeStruct((strips, strip, strip), jnp.bfloat16),
+        compiler_params=pltpu.CompilerParams(vmem_limit_bytes=40 * 1024 * 1024),
+        name="wgrad",
+    )(a, b)
+
+
 def norm_parts(values):
     average = jnp.mean(values, axis=-1, keepdims=True)
     centred = values - average
@@ -262,6 +1256,11 @@
     top = values.astype(jnp.bfloat16)
     rest = (values - top.astype(jnp.float32)).astype(jnp.bfloat16)
     return nn(top, place) + nn(rest, place)
+
+
+def reduce_share(a):
+    a = lax.psum_scatter(a, "seq", scatter_dimension=0, tiled=True)
+    return lax.psum(a.astype(jnp.bfloat16), "batch").astype(jnp.float32)
 
 
 def body(
@@ -318,6 +1317,31 @@
     qkv = qkv.reshape(row_count, rows, 3 * width)
 
     mixed, lse = attend(qkv, kaug, half)
+    own_globals = lax.dynamic_slice_in_dim(global_inputs, me * share, share, axis=1)
+    own_global_cot = lax.dynamic_slice_in_dim(global_cotangent, me * share, share, axis=1)
+    tokens_in = block.reshape(token_rows, width)
+    cot_block = jnp.concatenate([output_cotangent[:, half:], next_cotangent], axis=1)
+    if count == 8 and lax.axis_size("batch") == 4:
+        (
+            layer_output, residual_grad, block_grad, block_delta, own_res, global_out, global_grad, global_lse, global_delta,
+            inner_wgrad, outer_ab, outer_c, out_grad, vectors,
+        ) = mid(
+            lengths, tokens_in, mixed, lse, cot_block.reshape(token_rows, width), own_globals, own_global_cot, out_weight,
+            inner_weight, outer_weight, inner_bias, second_gain, second_shift, half, count,
+        )
+        input_out, global_grad, inner_out, outer_out, out_out, qkv_out, small = rear(
+            qkv, block_grad, lse, block_delta, kaug, tokens_in, residual_grad, global_grad, global_lse, global_delta,
+            own_globals, own_res, normed, global_inputs, qkv_weight, first_gain[None], vectors, outer_ab, outer_c, inner_wgrad,
+            out_grad, half, count,
+        )
+        cut = lambda a: lax.dynamic_slice_in_dim(a, me * (a.shape[0] // count), a.shape[0] // count)
+        vectors_out = [cut(small[n]) for n in range(4)] + [cut(small[4:].reshape(-1))]
+        joined = lambda a: join_rows(a.reshape(count, own_rows, width), row_count)
+        return (
+            layer_output, joined(global_out), input_out, joined(global_grad), vectors_out[0], vectors_out[1], qkv_out,
+            out_out, vectors_out[2], vectors_out[3], inner_out, vectors_out[4], outer_out,
+        )
+
     part_mixed, part_lse = spread(
         [split_rows(mixed[:, block_len:], count), split_rows(lse[:, block_len:], count)], count, False, 0
     )
@@ -327,12 +1351,7 @@
     global_lse = highest + jnp.log(total)
     global_mixed = jnp.sum(per_head(part_weight / total, width) * part_mixed.astype(f32), axis=0)
 
-    own_globals = lax.dynamic_slice_in_dim(global_inputs, me * share, share, axis=1)
-    own_global_cot = lax.dynamic_slice_in_dim(global_cotangent, me * share, share, axis=1)
-    tokens = jnp.concatenate(
-        [block.reshape(token_rows, width), own_globals.reshape(own_rows, width)]
-    ).astype(f32)
-    cot_block = jnp.concatenate([output_cotangent[:, half:], next_cotangent], axis=1)
+    tokens = jnp.concatenate([tokens_in, own_globals.reshape(own_rows, width)]).astype(f32)
     cot_block = jnp.where(valid[:, :, None], cot_block, 0)
     cotangent = jnp.concatenate(
         [cot_block.reshape(token_rows, width), own_global_cot.reshape(own_rows, width)]
@@ -357,10 +1376,10 @@
     projection_grad = residual_grad.astype(bf16)
     attended_grad = nt(projection_grad, out_weight).astype(bf16)
     delta = head_sums(attended_grad.astype(f32) * attended.astype(f32))
-    outer_grad = tn(hidden, cotangent)
-    inner_wgrad = tn(normed_second, inner_grad)
+    outer_grad = wgrad(hidden, cotangent, width)
+    inner_wgrad = wgrad(normed_second, inner_grad, width)
     bias_grad = jnp.sum(inner_grad.astype(f32), axis=0)
-    out_grad = tn(attended, projection_grad)
+    out_grad = wgrad(attended, projection_grad, width)
 
     all_grad, all_lse, all_delta = spread(
         [attended_grad[token_rows:], global_lse, delta[token_rows:]], count, True, 1
@@ -372,6 +1391,11 @@
     block_delta = jnp.concatenate(
         [delta[:token_rows].reshape(row_count, block_len, LANES), join_rows(all_delta, row_count)], axis=1
     )
+    layer = final[:token_rows].reshape(row_count, block_len, width)
+    layer = jnp.where(valid[:, :, None], layer, 0.0).astype(bf16)
+    layer_output = jnp.concatenate([lax.ppermute(layer[:, half:], "seq", forth), layer[:, :half]], axis=1)
+    own_out = final[token_rows:].astype(bf16)
+    part = width // count
     dqkv = jnp.concatenate(attend_back(qkv, block_grad, block_lse, block_delta, kaug, half, rows), axis=-1)
     (part_dqkv,) = spread([split_rows(dqkv[:, block_len:], count)], count, False, 2)
     global_dqkv = jnp.sum(part_dqkv.astype(f32), axis=0).astype(bf16)
@@ -382,25 +1406,17 @@
     through, first_gain_grad, first_shift_grad = norm_back(first_grad, n_tokens, inv_tokens, first_gain)
     input_grad = (residual_grad + through).astype(bf16)
     normed_tokens = (n_tokens * first_gain + first_shift).astype(bf16)
-    qkv_wgrad = tn(normed_tokens, qkv_grad)
-
-    layer = final[:token_rows].reshape(row_count, block_len, width)
-    layer = jnp.where(valid[:, :, None], layer, 0.0).astype(bf16)
+    qkv_wgrad = wgrad(normed_tokens, qkv_grad, width)
+
     grad_block = input_grad[:token_rows].reshape(row_count, block_len, width)
-    layer_output = jnp.concatenate([lax.ppermute(layer[:, half:], "seq", forth), layer[:, :half]], axis=1)
     input_out = jnp.concatenate(
         [lax.ppermute(grad_block[:, half:], "seq", forth), grad_block[:, :half]], axis=1
     )
-    global_final, global_grad = spread(
-        [final[token_rows:].astype(bf16), input_grad[token_rows:]], count, True, 3
-    )
+    global_final, global_grad = spread([own_out, input_grad[token_rows:]], count, True, 3)
 
     def shares(a):
-        return a.reshape(count, a.shape[0] // count, -1)
-
-    strips = inner_width // width
-    inner_part = inner_wgrad.reshape(count, width // count, strips, width).transpose(0, 2, 1, 3)
-    qkv_part = qkv_wgrad.reshape(count, width // count, 3, width).transpose(0, 2, 1, 3)
+        return a.reshape(count, a.shape[0] // count)
+
     small = jnp.concatenate(
         [
             shares(first_gain_grad),
@@ -411,28 +1427,11 @@
         ],
         axis=1,
     )
-    small = small.reshape(count, 1, -1)
-    stacked = jnp.concatenate(
-        [
-            inner_part.reshape(count, -1, width).astype(bf16),
-            shares(outer_grad).astype(bf16),
-            shares(out_grad).astype(bf16),
-            qkv_part.reshape(count, -1, width).astype(bf16),
-        ],
-        axis=1,
-    )
-    stacked = lax.psum_scatter(stacked, "seq", scatter_dimension=0, tiled=True)
-    stacked = lax.psum(stacked, "batch")[0].astype(f32)
-    small = lax.psum_scatter(small, "seq", scatter_dimension=0, tiled=True)
-    small = lax.psum(small, "batch").reshape(-1)
-    part = width // count
-    first_rows = strips * part
-    outer_rows = inner_width // count
-    inner_out = stacked[:first_rows].reshape(strips, part, width).transpose(1, 0, 2).reshape(part, inner_width)
-    at = first_rows + outer_rows
-    outer_out = stacked[first_rows:at]
-    out_out = stacked[at:at + part]
-    qkv_out = stacked[at + part:].reshape(3, part, width).transpose(1, 0, 2).reshape(part, 3 * width)
+    inner_out = reduce_share(inner_wgrad.transpose(1, 0, 2).reshape(width, -1))
+    outer_out = reduce_share(outer_grad.reshape(inner_width, width))
+    out_out = reduce_share(out_grad[0])
+    qkv_out = reduce_share(qkv_wgrad.transpose(1, 0, 2).reshape(width, -1))
+    small = reduce_share(small)[0]
     return (
         layer_output,
         join_rows(global_final, row_count),

time: 691 us -> 308 us (0.45); the launches traced: 680 us -> 308 us
  waiting for transfers between devices: 243 us -> 12 us
  Pallas kernels: 131 us -> 246 us
  matrix products: 97.8 us -> 6.54 us
  local copies, waits for them, and re-layouts: 82.1 us -> 25.7 us
  blocking collectives: 47.5 us -> 0 us
  other arithmetic: 49 us -> 10.4 us
  between operations: 15.4 us -> 0.94 us
  starting transfers between devices: 14.9 us -> 6.51 us
    reduce_scatter x1 -> x0, waiting for transfers between devices: 237 us -> none  [body(): stacked = lax.psum_scatter(stacked, 'seq', scatter_dimension=0, tiled=True)]
    pallas_call x5 -> x2, Pallas kernels: 103 us -> 218 us  [the longest x1 119 us: rear(): pl.pallas_call(functools.partial(rear_kernel, half, scale, pairs, tuple(s...]
    dot_general x8 -> x0, matrix products: 68.3 us -> none  [the longest x4 36.1 us: nt(): lax.dot_general(a, b, (((1,), (1,)), ((), ())), preferred_element_type=jn...]
    unnamed x1 -> x0, blocking collectives: 41.9 us -> none
    convert_element_type x5 -> x0, local copies, waits for them, and re-layouts: 36.8 us -> none  [the longest x3 21.4 us: body(): qkv_part.reshape(count, -1, width).astype(bf16)]
    dot_general x6 -> x1, matrix products: 29.5 us -> 6.54 us  [nn(): return jnp.dot(a, b, preferred_element_type=jnp.float32)]
    concatenate x6 -> x0, other arithmetic: 18.6 us -> none  [the longest x1 12.2 us: body(): jnp.concatenate([inner_part.reshape(count, -1, width).astype(bf16), share...]
    slice x23 -> x2, local copies, waits for them, and re-layouts: 13.9 us -> 1.69 us  [the longest x1 0.95 us: body(): small[n]]
  transfers between devices with their start and end apart: 6 -> 2, of which waited for: 2 -> 1; matrix products, arithmetic and copies ran while one was open for 11% -> 5% of each run, Pallas kernels for 8% -> 9%
where the time goes in v2:
time: 308 us
  Pallas kernels  246 us (80%)
  local copies, waits for them, and re-layouts  25.7 us (8%)
  waiting for transfers between devices  12 us (4%)
  other arithmetic  10.4 us (3%)
  matrix products  6.54 us (2%)
  starting transfers between devices  6.51 us (2%)
    pallas_call x1, Pallas kernels, rear(): pl.pallas_call(functools.partial(rear_kernel, half, scale, pairs, tuple(s...  119 us
    pallas_call x1, Pallas kernels, mid(): pl.pallas_call(functools.partial(mid_kernel, half, len(fold)), grid=(afte...  98.6 us
    pallas_call x1, Pallas kernels, attend(): pl.pallas_call(functools.partial(attend_kernel, half, scale, tq), grid=(r...  27.9 us
    ppermute x1, waiting for transfers between devices, body(): next_inputs = lax.ppermute(inputs[:, :half], 'seq', back)  12 us
    unnamed x46, local copies, waits for them, and re-layouts  10.7 us
    dot_general x1, matrix products, nn(): return jnp.dot(a, b, preferred_element_type=jnp.float32)  6.54 us
  transfers between devices with their start and end apart: 2, of which 1 were waited for; matrix products, arithmetic and copies ran while one was open for 5% of the time, Pallas kernels for 9%

profile of v2, /device:TPU:0, one launch (start us, length us, event | category | flops | bytes accessed | tf_op | source)
XLA Modules:
  0.0 307.6 jit_solution(1081730210454311743)
XLA Ops:
  0.7 0.0 copy-start.15
  0.7 0.0 copy-start.5
  0.7 0.0 copy-start.19
  0.7 2.5 fusion.16
  3.2 6.0 %collective-permute-start = (bf16[2,256,768]{2,1,0:T(8,128)(2,1)}, bf16[2,256,768]{2,1,0:T(8,128)(2,1)S(1)}, u32[]{:S(2)}, u32[]{:S(2)}) collective-permute-start(bf16[2,256,768]{2,1,0:T(8,128)(2,1)} %get-tuple-element.62), channel_id=1, source_target_pairs={{0,28},{4,0},{8,4},{12,8},{16,12},{20,16},{24,20},{28,24},{1,29},{... | collective-permute-start | bytes 2359304 | tf_op jit(solution)/shard_map/ppermute | solution.py:1297
  9.2 0.0 copy-done.7
  9.2 1.0 fusion.15
  10.2 0.5 collective-permute-start.1
  10.8 0.6 broadcast_in_dim.51.gain_ref
  11.4 0.6 broadcast_in_dim.52.shift_ref
  12.0 0.6 broadcast_in_dim.53.gain_ref
  12.6 0.1 compare_and_fusion
  12.7 1.4 constant_dynamic-slice_fusion.4
  14.2 0.1 compare_not_fusion
  14.3 0.2 select_convert_fusion
  14.5 0.0 copy-start.1
  14.6 0.8 and_convert_fusion.heads_ref
  15.4 12.0 %collective-permute-done = bf16[2,256,768]{2,1,0:T(8,128)(2,1)S(1)} collective-permute-done((bf16[2,256,768]{2,1,0:T(8,128)(2,1)}, bf16[2,256,768]{2,1,0:T(8,128)(2,1)S(1)}, u32[]{:S(2)}, u32[]{:S(2)}) %collective-permute-start) | collective-permute-done | bytes 786464 | tf_op jit(solution)/shard_map/ppermute | solution.py:1297
  27.4 0.3 convert_reduce_fusion
  27.8 0.9 multiply_reduce_fusion
  28.7 0.0 copy-start.6
  28.7 1.1 fusion.3
  29.8 0.9 copy-done.6
  30.7 6.5 %convolution_convert_fusion = bf16[1280,2304]{1,0:T(8,128)(2,1)} fusion(bf16[1280,768]{1,0:T(8,128)(2,1)S(1)} %fusion.3, bf16[768,2304]{1,0:T(8,128)(2,1)S(1)} %copy-done.6), kind=kOutput, calls=%fused_computation | convolution fusion | flops 4532797440 | bytes 11403264 | tf_op jit(solution)/shard_map/dot_general | solution.py:23
  37.3 27.9 %attend.1 = (bf16[2,640,768]{2,1,0:T(8,128)(2,1)S(1)}, f32[2,640,128]{2,1,0:T(8,128)S(1)}) custom-call(bf16[2,640,2304]{2,1,0:T(8,128)(2,1)} %bitcast.34, bf16[2,640,2304]{2,1,0:T(8,128)(2,1)} %bitcast.35, bf16[2,640,2304]{2,1,0:T(8,128)(2,1)} %bitcast.36, bf16[2,640,128]{2,1,0:T(8,128)(2,1)S(1)} %pad_maximum_fusion.3.kaug_ref), custom_call_target="tpu_custom_call" | custom-call | tf_op jit(solution)/shard_map/attend/pallas_call | solution.py:77
  65.2 1.3 copy-done
  66.5 0.9 copy-done.2
  67.4 1.2 pad_maximum_fusion.1
  68.6 0.0 collective-permute-done.1
  68.6 2.4 pad_maximum_fusion.2
  71.0 98.6 %mid.1 = (bf16[2,512,768]{2,1,0:T(8,128)(2,1)}, f32[1024,768]{1,0:T(8,128)}, bf16[1024,768]{1,0:T(8,128)(2,1)}, f32[1024,128]{1,0:T(8,128)}, f32[2,16,768]{2,1,0...) custom-call(s32[2]{0:T(128)} %lengths.1, ...), custom_call_target="tpu_custom_call" | custom-call | tf_op jit(solution)/shard_map/mid/pallas_call | solution.py:1133
  169.6 3.1 %add_convert_fusion.normed_ref = bf16[2,640,768]{2,1,0:T(8,128)(2,1)} fusion(f32[768]{0:T(1024)} %param.18, f32[768]{0:T(1024)} %param.17, f32[2,640]{1,0:T(2,128)} %copy-done.14, f32[2,640]{1,0:T(2,128)} %copy-done.13, bf16[2,128,768]{2,1,0:T(8,128)(2,1)} %globals_ref.1, bf16[2,256,768]{2,1,0:T(8,128)(2,1)} %copy-done.4, bf16[2,256,768]{2,1,0:T(8,128)(2,1)} %copy-done.3), kind=kLoop, calls=%fused_computation.6 | loop fusion | flops 10813440 | bytes 3948544 | tf_op jit(solution)/shard_map/convert_element_type | solution.py:1315
  172.8 119.0 %rear.1 = (bf16[2,512,768]{2,1,0:T(8,128)(2,1)}, bf16[2,2,2,2,16,768]{5,4,3,2,1,0:T(8,128)(2,1)}, f32[96,3072]{1,0:T(8,128)}, f32[384,768]{1,0:T(8,128)}, f32[96...) custom-call(bf16[2,640,2304]{2,1,0:T(8,128)(2,1)} %bitcast.37, bf16[2,640,2304]{2,1,0:T(8,128)(2,1)} %bitcast.38, ...), custom_call_target="tpu_custom_call" | custom-call | tf_op jit(solution)/shard_map/rear/pallas_call | solution.py:787
  291.8 1.0 fusion.17
  292.7 0.7 slice.35
  293.5 1.8 copy.27
  295.2 1.8 copy.28
  297.1 0.6 fusion.10
  297.7 0.6 fusion.11
  298.2 0.6 fusion.12
  298.8 0.6 fusion.13
  299.4 0.7 dynamic_slice.39
  300.1 2.7 copy.35
  302.8 1.1 copy.36
  303.9 0.9 copy.37
  304.8 0.7 copy.38
  305.5 1.0 copy.39
  306.6 1.0 copy.40
  (48 shorter events, 0.2 us)
Async XLA Ops:
  0.6 8.5 %copy-start.7 = (bf16[2,512,768]{2,1,0:T(8,128)(2,1)S(1)}, bf16[2,512,768]{2,1,0:T(8,128)(2,1)}, u32[]{:S(2)}) copy-start(bf16[2,512,768]{2,1,0:T(8,128)(2,1)} %param.26) | copy-start | bytes 4718596
  0.7 10.1 %copy-start.17 = (f32[768]{0:T(1024)S(1)}, f32[768]{0:T(1024)}, u32[]{:S(2)}) copy-start(f32[768]{0:T(1024)} %param.21) | copy-start | bytes 9220
  0.7 10.7 %copy-start.18 = (f32[768]{0:T(1024)S(1)}, f32[768]{0:T(1024)}, u32[]{:S(2)}) copy-start(f32[768]{0:T(1024)} %param.22) | copy-start | bytes 9220
  0.7 11.3 %copy-start.15 = (f32[768]{0:T(1024)S(1)}, f32[768]{0:T(1024)}, u32[]{:S(2)}) copy-start(f32[768]{0:T(1024)} %param.17) | copy-start | bytes 9220
  0.7 12.1 %copy-start.5 = (bf16[2,128,768]{2,1,0:T(8,128)(2,1)S(1)}, bf16[2,128,768]{2,1,0:T(8,128)(2,1)}, u32[]{:S(2)}) copy-start(bf16[2,128,768]{2,1,0:T(8,128)(2,1)} %globals_ref.1) | copy-start | bytes 1179652
  0.7 13.5 %copy-start.19 = (s32[2]{0:T(128)S(1)}, s32[2]{0:T(128)}, u32[]{:S(2)}) copy-start(s32[2]{0:T(128)} %lengths.1) | copy-start | bytes 28
  3.2 62.0 %copy-start.3 = (bf16[2,256,768]{2,1,0:T(8,128)(2,1)}, bf16[2,256,768]{2,1,0:T(8,128)(2,1)S(1)}, u32[]{:S(2)}) copy-start(bf16[2,256,768]{2,1,0:T(8,128)(2,1)S(1)} %get-tuple-element.61) | copy-start | bytes 2359300
  3.2 24.2 %collective-permute-start = (bf16[2,256,768]{2,1,0:T(8,128)(2,1)}, bf16[2,256,768]{2,1,0:T(8,128)(2,1)S(1)}, u32[]{:S(2)}, u32[]{:S(2)}) collective-permute-start(bf16[2,256,768]{2,1,0:T(8,128)(2,1)} %get-tuple-element.62), channel_id=1, source_target_pairs={{0,28},{4,0},{8,4},{12,8},{16,12},{20,16},{24,20},{28,24},{1,29},{... | collective-permute-start | bytes 2359304 | tf_op jit(solution)/shard_map/ppermute | solution.py:1297
  10.2 18.6 %copy-start.16 = (f32[768]{0:T(1024)S(1)}, f32[768]{0:T(1024)}, u32[]{:S(2)}) copy-start(f32[768]{0:T(1024)} %param.18) | copy-start | bytes 9220
  10.2 58.5 %collective-permute-start.1 = (bf16[2,256,768]{2,1,0:T(8,128)(2,1)}, bf16[2,256,768]{2,1,0:T(8,128)(2,1)}, u32[]{:S(2)}, u32[]{:S(2)}) collective-permute-start(bf16[2,256,768]{2,1,0:T(8,128)(2,1)} %get-tuple-element.60), channel_id=1, source_target_pairs={{0,28},{4,0},{8,4},{12,8},{16,12},{20,16},{24,20},{28,24},{1,29},{... | collective-permute-start | bytes 2359304 | tf_op jit(solution)/shard_map/ppermute | solution.py:1298
  14.5 22.7 %copy-start.1 = (bf16[2,640,128]{2,1,0:T(8,128)(2,1)}, bf16[2,640,128]{2,1,0:T(8,128)(2,1)S(1)}, u32[]{:S(2)}) copy-start(bf16[2,640,128]{2,1,0:T(8,128)(2,1)S(1)} %pad_maximum_fusion.3.kaug_ref) | copy-start | bytes 983044
  27.4 37.7 %copy-start.4 = (bf16[2,256,768]{2,1,0:T(8,128)(2,1)}, bf16[2,256,768]{2,1,0:T(8,128)(2,1)S(1)}, u32[]{:S(2)}) copy-start(bf16[2,256,768]{2,1,0:T(8,128)(2,1)S(1)} %collective-permute-done) | copy-start | bytes 2359300
  27.8 9.5 %copy-start.13 = (f32[2,640]{1,0:T(2,128)}, f32[2,640]{1,0:T(2,128)S(1)}, u32[]{:S(2)}) copy-start(f32[2,640]{1,0:T(2,128)S(1)} %broadcast_multiply_fusion) | copy-start | bytes 15364
  28.7 8.6 %copy-start.14 = (f32[2,640]{1,0:T(2,128)}, f32[2,640]{1,0:T(2,128)S(1)}, u32[]{:S(2)}) copy-start(f32[2,640]{1,0:T(2,128)S(1)} %add_rsqrt_fusion) | copy-start | bytes 15364
  28.7 2.0 copy-start.6
  65.2 1.3 copy-start
  66.5 0.9 copy-start.2
  291.8 11.0 %copy-start.8 = (bf16[2,512,768]{2,1,0:T(8,128)(2,1)S(1)}, bf16[2,512,768]{2,1,0:T(8,128)(2,1)}, u32[]{:S(2)}) copy-start(bf16[2,512,768]{2,1,0:T(8,128)(2,1)} %get-tuple-element.88) | copy-start | bytes 4718596
  295.2 8.7 %copy-start.11 = (f32[96,2304]{1,0:T(8,128)S(1)}, f32[96,2304]{1,0:T(8,128)}, u32[]{:S(2)}) copy-start(f32[96,2304]{1,0:T(8,128)} %get-tuple-element.92) | copy-start | bytes 2654212
  300.1 4.8 %copy-start.12 = (f32[96,768]{1,0:T(8,128)S(1)}, f32[96,768]{1,0:T(8,128)}, u32[]{:S(2)}) copy-start(f32[96,768]{1,0:T(8,128)} %get-tuple-element.93) | copy-start | bytes 884740
  302.8 2.8 copy-start.10
  302.8 3.8 %copy-start.9 = (f32[384,768]{1,0:T(8,128)S(1)}, f32[384,768]{1,0:T(8,128)}, u32[]{:S(2)}) copy-start(f32[384,768]{1,0:T(8,128)} %get-tuple-element.98) | copy-start | bytes 3538948

commit v3 on v2

--- a/solution.py
+++ b/solution.py
@@ -28,8 +28,11 @@
     return (lane == kind)
 
 
-def attend_kernel(half, scale, tq, q_ref, k_ref, v_ref, kaug_ref, o_ref, lse_ref):
-    pair = pl.program_id(1)
+def attend_step(half, scale, tq, *refs):
+    attend_kernel(half, scale, tq, pl.program_id(1), *refs)
+
+
+def attend_kernel(half, scale, tq, pair, q_ref, k_ref, v_ref, kaug_ref, o_ref, lse_ref):
     rows = q_ref.shape[1]
     zero = jnp.zeros((), jnp.bfloat16)
     k, v = k_ref[0], v_ref[0]
@@ -75,7 +78,7 @@
     scale = (width // HEADS) ** (-0.5)
     spec = lambda off: pl.BlockSpec((1, rows, LANES), lambda r, p: (r, 0, off + p))
     return pl.pallas_call(
-        functools.partial(attend_kernel, half, scale, tq),
+        functools.partial(attend_step, half, scale, tq),
         grid=(row_count, pairs),
         in_specs=[spec(0), spec(pairs), spec(2 * pairs), pl.BlockSpec((1, rows, LANES), lambda r, p: (r, 0, 0))],
         out_specs=[spec(0), pl.BlockSpec((1, rows, LANES), lambda r, p: (r, 0, 0))],
@@ -266,12 +269,14 @@
         self.half = own.shape[3] // 2
         stages = range(len(order)) if stages is None else stages
         self.bufs = dict(zip(stages, bufs))
-        self.copies = {
-            n: remote(
-                own.at[self.region(n, False)], self.bufs[n], send.at[first + n], recv.at[first + n], place.partner(order[n])
-            )
-            for n in stages
-        }
+        self.send, self.recv, self.first = send, recv, first
+
+    def copy(self, n):
+        at = self.first + n
+        return remote(
+            self.own.at[self.region(n, False)], self.bufs[n], self.send.at[at], self.recv.at[at],
+            self.place.partner(self.order[n]),
+        )
 
     @staticmethod
     def buffers(rows, width, order, stages=None, dtype=jnp.bfloat16):
@@ -302,10 +307,14 @@
         return (*at, rows, self.lanes)
 
     def start(self, n):
-        self.copies[n].start()
+        self.copy(n).start()
+
+    def sent(self):
+        for n in self.bufs:
+            self.copy(n).wait_send()
 
     def finish(self, n):
-        self.copies[n].wait_recv()
+        self.copy(n).wait_recv()
         buf = self.bufs[n]
         dims = len(buf.shape) - 2
         count = buf.shape[-2]
@@ -316,8 +325,7 @@
             block, row = lax.div(i, pieces), lax.rem(i, pieces) * piece
             free = [lax.rem(lax.div(block, 2 ** (dims - 1 - d)), 2) for d in range(dims)]
             at = self.region(n, True, free, (row, piece))
-            more = buf[(*free, pl.ds(pl.multiple_of(row, 16), piece), slice(None))]
-            self.own[at] = (self.own[at].astype(jnp.float32) + more.astype(jnp.float32)).astype(self.own.dtype)
+            self.own[at] = self.own[at] + buf[(*free, pl.ds(pl.multiple_of(row, 16), piece), slice(None))]
             return carry
 
         lax.fori_loop(0, 2 ** dims * pieces, add, 0)
@@ -327,20 +335,23 @@
     order = ("z1", "z0", "x")
 
     def __init__(self, place, buf, send, recv):
-        self.copies = []
-        for n, axis in enumerate(self.order):
-            at = tuple(slice(None) if other in self.order[:n] else place[other] for other, _ in SEQ_BITS)
-            self.copies.append(remote(buf.at[at], buf.at[at], send.at[n], recv.at[n], place.partner(axis)))
+        self.place, self.buf, self.send, self.recv = place, buf, send, recv
+
+    def copy(self, n):
+        done = self.order[:n]
+        at = (slice(None), *(slice(None) if axis in done else self.place[axis] for axis, _ in SEQ_BITS))
+        block = self.buf.at[at]
+        return remote(block, block, self.send.at[n], self.recv.at[n], self.place.partner(self.order[n]))
 
     def stage(self, n):
         if n > 0:
-            self.copies[n - 1].wait_recv()
+            self.copy(n - 1).wait_recv()
         if n < 3:
-            self.copies[n].start()
+            self.copy(n).start()
 
     def finish(self):
-        for copy in self.copies:
-            copy.wait_send()
+        for n in range(3):
+            self.copy(n).wait_send()
 
 
 PARTS = (
@@ -369,31 +380,44 @@
         rows = own.shape[3]
         half = rows // 2
         self.mine = pl.ds(pl.multiple_of(y * half, 16), half)
-        at, self.keep, self.core = 0, [], []
-        if stages == self.LATE:
-            pieces = ()
-        if source is not None:
-            self.core.append(remote(source.at[:, :, :, 1 - c], got, send.at[0], recv.at[0], place.partner("c")))
-            pieces = ()
-        for n, (take, count) in enumerate(pieces):
-            spot = pl.ds(at, count)
-            self.keep.append(pltpu.make_async_copy(take(c), own.at[:, :, :, spot], local.at[n]))
-            self.core.append(
-                remote(take(1 - c), got.at[:, :, :, spot], send.at[n], recv.at[n], place.partner("c"))
-            )
-            at += count
-        first = len(self.core)
+        self.pieces, self.source, self.done = pieces, source, done
+        self.sems = send, recv, local
+        first = 1 if source is not None else len(pieces)
+        self.first = first + 12
         self.parts = []
         for n, (lanes, order) in enumerate(PARTS):
             own_bufs = bufs[len(stages) * n:len(stages) * (n + 1)]
             self.parts.append(Halve(place, own, lanes, order, own_bufs, send, recv, first + 4 * n, stages))
-        first += 12
-        if done is None:
-            return
-        self.across = remote(
-            done.at[c, self.mine], done.at[c, self.mine], send.at[first], recv.at[first], place.partner("y")
-        )
-        self.back = remote(done.at[c], done.at[c], send.at[first + 1], recv.at[first + 1], place.partner("c"))
+
+    def keep(self):
+        at, copies = 0, []
+        if self.source is None:
+            for n, (take, count) in enumerate(self.pieces):
+                spot = self.own.at[:, :, :, pl.ds(at, count)]
+                copies.append(pltpu.make_async_copy(take(self.place["c"]), spot, self.sems[2].at[n]))
+                at += count
+        return copies
+
+    def core(self):
+        send, recv, _ = self.sems
+        to, c = self.place.partner("c"), 1 - self.place["c"]
+        if self.source is not None:
+            return [remote(self.source.at[:, :, :, c], self.got, send.at[0], recv.at[0], to)]
+        at, copies = 0, []
+        for n, (take, count) in enumerate(self.pieces):
+            copies.append(remote(take(c), self.got.at[:, :, :, pl.ds(at, count)], send.at[n], recv.at[n], to))
+            at += count
+        return copies
+
+    def across(self):
+        send, recv, _ = self.sems
+        spot = self.done.at[self.place["c"], self.mine]
+        return remote(spot, spot, send.at[self.first], recv.at[self.first], self.place.partner("y"))
+
+    def back(self):
+        send, recv, _ = self.sems
+        spot = self.done.at[self.place["c"]]
+        return remote(spot, spot, send.at[self.first + 1], recv.at[self.first + 1], self.place.partner("c"))
 
     @staticmethod
     def scratch(rows, width, pieces, sourced=False, stages=(0, 1, 2, 3)):
@@ -413,12 +437,12 @@
 
     def stage(self, n):
         if n == 0:
-            for copy in self.keep + self.core:
+            for copy in self.keep() + self.core():
                 copy.start()
         elif n == 1:
-            for copy in self.keep:
+            for copy in self.keep():
                 copy.wait()
-            for copy in self.core:
+            for copy in self.core():
                 copy.wait_recv()
 
             piece = math.gcd(self.got.shape[3], 48)
@@ -428,8 +452,7 @@
                 block = lax.div(i, pieces)
                 rows = pl.ds(pl.multiple_of(lax.rem(i, pieces) * piece, 16), piece)
                 at = (*(lax.rem(lax.div(block, w), 2) for _, w in SEQ_BITS), rows)
-                total = self.own[at].astype(jnp.float32) + self.got[at].astype(jnp.float32)
-                self.own[at] = total.astype(jnp.bfloat16)
+                self.own[at] = self.own[at] + self.got[at]
                 return carry
 
             lax.fori_loop(0, 8 * pieces, add, 0)
@@ -444,12 +467,12 @@
                 part.finish(3)
             at = tuple(self.place[axis] for axis, _ in SEQ_BITS)
             self.done[self.place["c"], self.mine] = self.own[(*at, self.mine)]
-            self.across.start()
+            self.across().start()
         elif n == 6:
-            self.across.wait_recv()
-            self.back.start()
+            self.across().wait_recv()
+            self.back().start()
         else:
-            self.back.wait_recv()
+            self.back().wait_recv()
 
     def held(self):
         z1, z0, x = (self.place[axis] for axis, _ in SEQ_BITS)
@@ -458,41 +481,40 @@
             z1, z0, slice(None), slice(None), pl.ds(a + b, c)
         )
 
-    def resume(self, ab, last):
-        first, second = self.held()
-        self.own[first] = ab[...]
-        self.own[second] = last[...]
+    def resume(self):
         for part in self.parts:
             part.start(2)
 
     def finish(self):
-        for copy in self.core + [self.across, self.back]:
+        copies = self.core()
+        if self.done is not None:
+            copies = copies + [self.across(), self.back()]
+        for copy in copies:
             copy.wait_send()
         for part in self.parts:
-            for copy in part.copies.values():
-                copy.wait_send()
+            part.sent()
 
 
 class Sum:
     order = ("c", "x", "y", "z0", "z1")
 
     def __init__(self, place, value, got, send, recv):
-        self.value, self.got = value, got
-        self.copies = [
-            remote(value.at[n], got.at[n], send.at[n], recv.at[n], place.partner(axis))
-            for n, axis in enumerate(self.order)
-        ]
+        self.place, self.value, self.got, self.send, self.recv = place, value, got, send, recv
+
+    def copy(self, n):
+        to = self.place.partner(self.order[n])
+        return remote(self.value.at[n], self.got.at[n], self.send.at[n], self.recv.at[n], to)
 
     def stage(self, n):
         if n > 0:
-            self.copies[n - 1].wait_recv()
+            self.copy(n - 1).wait_recv()
             self.value[n] = self.value[n - 1] + self.got[n - 1]
         if n < 5:
-            self.copies[n].start()
+            self.copy(n).start()
 
     def finish(self):
-        for copy in self.copies:
-            copy.wait_send()
+        for n in range(5):
+            self.copy(n).wait_send()
 
 
 def share_views(a, count):
@@ -505,15 +527,65 @@
     return a.reshape(*lead, 2, 2, 2, 2, rows // (2 * count), width)
 
 
-def write_big(first, second, inner_o, outer_o):
+def fetch(sources, targets, sems, first=0):
+    return [pltpu.make_async_copy(s, t, sems.at[first + n]) for n, (s, t) in enumerate(zip(sources, targets))]
+
+
+def finish_kernel(
+    inner, late, keys, outer, small, layer, igrad, gout, ggrad,
+    inner_o, outer_o, out_o, qkv_o, fg_o, fs_o, sg_o, ss_o, bias_o, layer_o, igrad_o, gout_o, ggrad_o, sems,
+):
+    f32 = jnp.float32
+    me = lax.axis_index("seq")
+    copies = fetch((layer, igrad, gout, ggrad), (layer_o, igrad_o, gout_o, ggrad_o), sems)
+    begin(copies)
     width = outer_o.shape[1]
     part = inner_o.shape[0]
-    half = outer_o.shape[0] // 2
-    strips = inner_o.shape[1] // width // 2
+    strips = inner.shape[1] // part
+    half = outer.shape[1]
     for c in range(2):
         for j in range(strips):
-            inner_o[:, pl.ds((c * strips + j) * width, width)] = first.done[c, pl.ds(j * part, part)].astype(jnp.float32)
-        outer_o[pl.ds(c * half, half)] = second.done[c].astype(jnp.float32)
+            inner_o[:, pl.ds((c * strips + j) * width, width)] = inner[c, pl.ds(j * part, part)].astype(f32)
+        outer_o[pl.ds(c * half, half)] = outer[c].astype(f32)
+        spot = pl.ds(c * part // 2, part // 2)
+        first, second = pl.ds(0, part // 2), pl.ds(part // 2, part // 2)
+        out_o[spot] = late[c, first].astype(f32)
+        for j, (ref, lines) in enumerate(((late, second), (keys, first), (keys, second))):
+            qkv_o[spot, pl.ds(j * width, width)] = ref[c, lines].astype(f32)
+    values = small[...]
+    turned = pltpu.roll(values, lax.rem(width - part * me, width), 1)
+    for n, ref in enumerate((fg_o, fs_o, sg_o, ss_o)):
+        ref[...] = turned[n:n + 1, :part]
+    wide = bias_o.shape[1]
+    per = width // wide
+    row = small[pl.ds(4 + lax.div(me, per), 1)]
+    spots = [row[:, n * wide:(n + 1) * wide] for n in range(per)]
+    chosen = spots[0]
+    for n in range(1, per):
+        chosen = jnp.where(lax.rem(me, per) == n, spots[n], chosen)
+    bias_o[...] = chosen
+    for copy in copies:
+        copy.wait()
+
+
+def finish(inner, late, keys, outer, small, layer, igrad, gout, ggrad):
+    width = small.shape[1]
+    part = late.shape[1]
+    bias = 2 * outer.shape[1]
+    vmem, hbm = pl.BlockSpec(memory_space=pltpu.VMEM), pl.BlockSpec(memory_space=pl.ANY)
+    shapes = [(part, 2 * inner.shape[1] // part * width), (bias, width), (part, width), (part, 3 * width)]
+    shapes += [(1, part)] * 4 + [(1, bias)]
+    moved = [layer, igrad, gout, ggrad]
+    return pl.pallas_call(
+        finish_kernel,
+        in_specs=[vmem] * 9,
+        out_specs=[vmem] * 9 + [hbm] * 4,
+        out_shape=[jax.ShapeDtypeStruct(s, jnp.float32) for s in shapes]
+        + [jax.ShapeDtypeStruct(a.shape, a.dtype) for a in moved],
+        scratch_shapes=[pltpu.SemaphoreType.DMA((4,))],
+        compiler_params=pltpu.CompilerParams(vmem_limit_bytes=60 * 1024 * 1024),
+        name="finish",
+    )(inner, late, keys, outer, small, *moved)
 
 
 def begin(copies):
@@ -535,6 +607,8 @@
                 folds[f].stage(n)
 
 
+TILE_AT = ((6, 0, 1), (7, 0, 0), (15, 1, 1), (19, 1, 0))
+GLOBALS_AT, STRIPS_AT, OWN_AT = 14, 16, 20
 REAR_TICKS = {
     0: ((0, 0),),
     2: ((0, 1),),
@@ -543,29 +617,27 @@
     6: ((0, 2),),
     7: ((3, 6),),
     8: ((3, 7),),
-    10: ((0, 3),),
-    13: ((0, 4),),
-    14: ((1, 0),),
-    15: ((0, 5),),
-    16: ((1, 1), (2, 0)),
-    17: ((0, 6),),
-    18: ((2, 1), (0, 7)),
-    19: ((1, 2),),
-    20: ((2, 2),),
+    11: ((0, 3),),
+    14: ((0, 4),),
+    16: ((0, 5),),
+    17: ((1, 0),),
+    18: ((0, 6),),
+    19: ((1, 1), (2, 0), (0, 7)),
 }
 REAR_END = (
-    (5, 1), (4, 1), (1, 3), (5, 2), (4, 2), (2, 3), (5, 3), (1, 4), (4, 3), (5, 4), (2, 4), (5, 5), (1, 5), (2, 5), (1, 6),
+    (2, 1), (5, 1), (1, 2), (4, 1), (2, 2), (1, 3), (5, 2), (4, 2), (2, 3), (5, 3), (1, 4), (4, 3), (5, 4), (2, 4), (5, 5), (1, 5), (2, 5), (1, 6),
     (2, 6), (1, 7), (2, 7),
 )
-SPREAD_TICKS = {15: 0, 17: 1, 20: 2}
+SPREAD_TICKS = {17: 0, 18: 1, 20: 2}
 
 
 def rear_kernel(
     half, scale, pairs, fold_refs,
     q_ref, k_ref, v_ref, g_ref, lse_ref, delta_ref, kaug_ref,
-    x_ref, res_ref, gg_ref, glse_ref, gdelta_ref, gx_ref, gres_ref, normed_ref, globals_ref, weight_ref, gain_ref,
-    vectors_ref, outer_ab_ref, outer_c_ref, inner, out,
-    igrad_o, ggrad_o, inner_o, outer_o, out_o, qkv_o, small_o,
+    x_ref, next_x_ref, res_ref, gg_in, glse_in, gdelta_in, outer_ab, outer_c, gres_in, globals_in, weight_in, gain_in, vectors_in,
+    normed_in, inner, out,
+    igrad_o, ggrad_o, inner_o, late_o, keys_o, outer_o, small_o,
+    gg_ref, glse_ref, gdelta_ref, gres_ref, globals_ref, weight_ref, gain_ref, vectors_ref, normed_ref,
     dqkv, gfirst, sums, qkv_src, grads, ggrad, value, got,
     send, recv, local, *scratch,
 ):
@@ -576,7 +648,7 @@
     row_count, rows, cols = dqkv.shape
     block_len = 2 * half
     width = cols // 3
-    share = gx_ref.shape[1]
+    share = gres_ref.shape[1]
     attn = row_count * pairs
     strips = inner.shape[0] // 2
     part_rows = inner.shape[4]
@@ -597,37 +669,68 @@
     small = Sum(place, value, got, send.at[row_count + 1], recv.at[row_count + 1])
     following = {"seq": lax.rem(me + 1, count)}
     before = {"seq": lax.rem(me + count - 1, count)}
-    home = [
-        remote(
-            grads.at[1, r], igrad_o.at[r, pl.ds(0, half)], send.at[row_count + 2, r], recv.at[row_count + 2, r], following
-        )
-        for r in range(row_count)
-    ]
-    keep = [
-        pltpu.make_async_copy(grads.at[0, r], igrad_o.at[r, pl.ds(half, half)], local.at[r]) for r in range(row_count)
-    ]
+    held = folds[3].held()
+    early = lambda: fetch(
+        (gg_in, glse_in, gdelta_in, outer_ab, outer_c),
+        (gg_ref, glse_ref, gdelta_ref, folds[3].own.at[held[0]], folds[3].own.at[held[1]]), local,
+    )
+    later = lambda: fetch(
+        (gres_in, globals_in, weight_in, gain_in, vectors_in),
+        (gres_ref, globals_ref, weight_ref, gain_ref.at[0], vectors_ref), local, 5,
+    )
+    latest = lambda: fetch((normed_in,), (normed_ref,), local, 11)
+
+    def home(r):
+        sems = send.at[row_count + 2, r], recv.at[row_count + 2, r]
+        return remote(grads.at[1, r], igrad_o.at[r, pl.ds(0, half)], *sems, following)
+
+    def keep(r):
+        return pltpu.make_async_copy(grads.at[0, r], igrad_o.at[r, pl.ds(half, half)], local.at[12 + r])
 
     @pl.when(step == 0)
     def _():
+        begin(early() + later() + latest())
         place.greet([following, before])
         sums[...] = jnp.zeros_like(sums)
-        folds[3].resume(outer_ab_ref, outer_c_ref)
+        for copy in early():
+            copy.wait()
+        folds[3].resume()
 
     ticks(REAR_TICKS, folds, step)
 
-    @pl.when(step < attn)
-    def _():
-        r, p = lax.div(step, pairs), lax.rem(step, pairs)
+    @pl.when((step < pairs) | ((step >= pairs + 2) & (step < attn + 2)))
+    def _():
+        r = jnp.where(step < pairs, 0, 1)
+        p = step - r * (pairs + 2)
         spots = [pl.ds(pl.multiple_of(j * width + p * LANES, LANES), LANES) for j in range(3)]
         lane = pl.ds(pl.multiple_of(p * LANES, LANES), LANES)
         wide = lambda a, b: jnp.concatenate([a, b.reshape(rows - block_len, LANES)], axis=0)
         attend_back_kernel(
-            half, scale, 320, p, q_ref, k_ref, v_ref, wide(g_ref[...], gg_ref[:, :, :, r, :, lane]),
-            wide(lse_ref[0], glse_ref[:, :, :, r]), wide(delta_ref[...], gdelta_ref[:, :, :, r]), kaug_ref,
+            half, scale, 320, p, q_ref, k_ref, v_ref, wide(g_ref[...], gg_ref[r, :, :, :, :, lane]),
+            wide(lse_ref[0], glse_ref[r]), wide(delta_ref[...], gdelta_ref[r]), kaug_ref,
             *(dqkv.at[pl.ds(r, 1), :, spot] for spot in spots),
         )
 
-    strip_at = step - (attn + 1)
+    for t, n in SPREAD_TICKS.items():
+
+        @pl.when(step == t)
+        def _():
+            spread.finish(n)
+            if n < 2:
+                spread.start(n + 1)
+
+    @pl.when(step == TILE_AT[0][0])
+    def _():
+        for copy in later():
+            copy.wait()
+
+    @pl.when(step == STRIPS_AT)
+    def _():
+        for copy in latest():
+            copy.wait()
+
+
+    strip_at = step - STRIPS_AT
 
     @pl.when((strip_at >= 0) & (strip_at < 3))
     def _():
@@ -637,16 +740,6 @@
             total = total + tn(normed_ref[r], dqkv[r, :, strip])
         qkv_src[strip_at] = total.astype(jnp.bfloat16).reshape(qkv_src.shape[1:])
 
-    for t, n in SPREAD_TICKS.items():
-
-        @pl.when(step == t)
-        def _():
-            spread.finish(n)
-            if n < 2:
-                spread.start(n + 1)
-
-    gain = gain_ref[...]
-
     def stats(x):
         centred = x - jnp.mean(x, axis=-1, keepdims=True)
         inv = lax.rsqrt(jnp.mean(centred * centred, axis=-1, keepdims=True) + EPS)
@@ -657,10 +750,10 @@
         sums[1] += sum_rows(first)
 
     def through(first, n, inv):
-        eg = first * gain
+        eg = first * gain_ref[...]
         return (eg - jnp.mean(eg, axis=-1, keepdims=True) - n * jnp.mean(eg * n, axis=-1, keepdims=True)) * inv
 
-    @pl.when(step == attn)
+    @pl.when(step == GLOBALS_AT)
     def _():
         own = pl.ds(block_len, rows - block_len)
         partial = jnp.concatenate([dqkv[r, own] for r in range(row_count)], axis=0)
@@ -672,71 +765,59 @@
             gfirst[:, :, :, pl.ds(r * share, share)] = first[r]
         spread.start(0)
 
-    tiles = attn + 4
-    tile = step - tiles
-
-    @pl.when((tile >= 0) & (tile < 2 * row_count))
-    def _():
-        r, h = lax.rem(tile, row_count), 1 - lax.div(tile, row_count)
-        spot = pl.ds(pl.multiple_of(h * half, half), half)
-        first = nt(dqkv[r, spot], weight_ref[...])
-        n, inv = stats(x_ref[...].astype(jnp.float32))
+    @pl.when(functools.reduce(jnp.logical_or, [step == t for t, _, _ in TILE_AT]))
+    def _():
+        r = jnp.where(step < pairs + 2, 0, 1)
+        h = jnp.where((step == TILE_AT[0][0]) | (step == TILE_AT[2][0]), 1, 0)
+        first = nt(dqkv[r, pl.ds(pl.multiple_of(h * half, half), half)], weight_ref[...])
+        n, inv = stats(jnp.where(h == 0, x_ref[0].astype(jnp.float32), next_x_ref[0].astype(jnp.float32)))
         add_sums(first, n)
         grads[h, r] = (res_ref[...] + through(first, n, inv)).astype(jnp.bfloat16)
 
-    for r in range(row_count):
-
-        @pl.when(tile == r)
+    for t, r, h in TILE_AT:
+
+        @pl.when(step == t)
         def _():
-            home[r].start()
-
-        @pl.when(tile == row_count + r)
-        def _():
-            keep[r].start()
-
-    after = tiles + 2 * row_count
-
-    @pl.when(step == after)
+            (home if h else keep)(r).start()
+
+    @pl.when(step == OWN_AT)
     def _():
         lines = [jnp.sum(sums[n], axis=0, keepdims=True) for n in range(2)]
         value[0] = jnp.concatenate(lines + [vectors_ref[...]])
         small.stage(0)
         own_rows = row_count * share
         at = tuple(place[axis] for axis, _ in SEQ_BITS)
-        n, inv = stats(gx_ref[...].astype(jnp.float32).reshape(own_rows, width))
+        held = pl.ds(pl.multiple_of(share * me, 16), share)
+        n, inv = stats(globals_ref[:, held].astype(jnp.float32).reshape(own_rows, width))
         grad = gres_ref[...].reshape(own_rows, width) + through(gfirst[at].astype(jnp.float32), n, inv)
-        ggrad[at] = grad.astype(jnp.bfloat16).reshape(row_count, share, width)
+        ggrad[(slice(None), *at)] = grad.astype(jnp.bfloat16).reshape(row_count, share, width)
         gather.stage(0)
 
-    @pl.when(step == after + 1)
-    def _():
-        write_big(folds[0], folds[3], inner_o, outer_o)
-        leave = pltpu.make_async_copy(ggrad, ggrad_o, local.at[row_count])
+    @pl.when(step == OWN_AT + 1)
+    def _():
+        leaves = fetch(
+            (folds[0].done, folds[3].done, ggrad, folds[1].done, folds[2].done, value.at[5]),
+            (inner_o, outer_o, ggrad_o, late_o, keys_o, small_o), local, 12 + row_count,
+        )
+        begin(leaves[:2])
         movers = folds + [gather, small]
         for f, n in REAR_END:
             movers[f].stage(n)
-            if (f, n) == (4, 3):
-                leave.start()
-        small_o[...] = value[5]
-        f32 = jnp.float32
-        for c in range(2):
-            spot = pl.ds(c * half_part, half_part)
-            first, second = pl.ds(0, half_part), pl.ds(half_part, half_part)
-            out_o[spot] = folds[1].done[c, first].astype(f32)
-            for j, (fold, lines) in enumerate(((folds[1], second), (folds[2], first), (folds[2], second))):
-                qkv_o[spot, pl.ds(j * width, width)] = fold.done[c, lines].astype(f32)
+        begin(leaves[2:])
         for fold in folds:
             fold.finish()
         gather.finish()
         small.finish()
-        for copy in spread.copies.values():
-            copy.wait_send()
-        for copy in keep + home + [leave]:
+        spread.sent()
+        for r in range(row_count):
+            keep(r).wait()
+            home(r).wait()
+        for copy in leaves:
             copy.wait()
 
 
 def rear(
-    qkv, grad, lse, delta, kaug, tokens, res_grad, global_grad, global_lse, global_delta, own_globals, own_res, normed,
+    qkv, grad, lse, delta, kaug, inputs, next_x, res_grad, global_grad, global_lse, global_delta, own_res, normed,
     globals_in, weight, gain, vectors, outer_ab, outer_c, inner, out, half, count,
 ):
     row_count, rows, cols = qkv.shape
@@ -749,25 +830,25 @@
     scale = (width // HEADS) ** (-0.5)
     attn = row_count * pairs
     f32, bf16 = jnp.float32, jnp.bfloat16
-    row_of = lambda t: jnp.minimum(t, attn - 1) // pairs
-    pair_of = lambda t: jnp.minimum(t, attn - 1) % pairs
+    turn = lambda t: jnp.where(t < pairs, t, jnp.clip(t - 2, pairs, attn - 1))
+    row_of = lambda t: turn(t) // pairs
+    pair_of = lambda t: turn(t) % pairs
     spec = lambda off: pl.BlockSpec((1, rows, LANES), lambda t: (row_of(t), 0, off + pair_of(t)))
     whole = pl.BlockSpec((1, rows, LANES), lambda t: (row_of(t), 0, 0))
 
     def tile_of(t):
-        n = jnp.clip(t - attn - 4, 0, 2 * row_count - 1)
-        return n % row_count * 2 + 1 - n // row_count, 0
-
-    fixed = lambda a: pl.BlockSpec(a.shape, lambda t: (0,) * a.ndim, pipeline_mode=pl.Buffered(1))
+        (a, _, _), (b, _, _), (c, _, _), _ = TILE_AT
+        return jnp.where(t <= a, 1, jnp.where(t <= b, 0, jnp.where(t <= c, 3, 2))), 0
+
     tile = pl.BlockSpec((half, width), tile_of)
     hbm = pl.BlockSpec(memory_space=pl.ANY)
     outs = [
         jax.ShapeDtypeStruct((row_count, block_len, width), bf16),
-        jax.ShapeDtypeStruct((2, 2, 2, row_count, share, width), bf16),
-        jax.ShapeDtypeStruct((part, 4 * width), f32),
-        jax.ShapeDtypeStruct((4 * part, width), f32),
-        jax.ShapeDtypeStruct((part, width), f32),
-        jax.ShapeDtypeStruct((part, 3 * width), f32),
+        jax.ShapeDtypeStruct((row_count, 2, 2, 2, share, width), bf16),
+        jax.ShapeDtypeStruct((2, 2 * part, width), bf16),
+        jax.ShapeDtypeStruct((2, part, width), bf16),
+        jax.ShapeDtypeStruct((2, part, width), bf16),
+        jax.ShapeDtypeStruct((2, 2 * part, width), bf16),
         jax.ShapeDtypeStruct((8, width), f32),
     ]
     folds, sizes = [], []
@@ -780,34 +861,36 @@
     sizes.append(len(refs))
     vmem = pltpu.VMEM
     kinds = 4 + row_count
-    fixeds = (
-        global_grad, global_lse, global_delta, own_globals, own_res, normed, globals_in, weight, gain, vectors,
-        outer_ab, outer_c,
-    )
+    early = (global_grad, global_lse, global_delta)
+    later = (own_res, globals_in, weight, gain, vectors, normed)
     return pl.pallas_call(
         functools.partial(rear_kernel, half, scale, pairs, tuple(sizes)),
-        grid=(attn + 4 + 2 * row_count + 2,),
+        grid=(OWN_AT + 2,),
         in_specs=[spec(0), spec(pairs), spec(2 * pairs)]
         + [pl.BlockSpec((block_len, LANES), lambda t: (row_of(t), pair_of(t)))]
         + [pl.BlockSpec((1, block_len, LANES), lambda t: (row_of(t), 0, 0))]
         + [pl.BlockSpec((block_len, LANES), lambda t: (row_of(t), 0)), whole]
-        + [tile, tile]
-        + [fixed(a) for a in fixeds]
-        + [hbm] * 2,
-        out_specs=[hbm] * 2 + [pl.BlockSpec(memory_space=pltpu.VMEM)] * 5,
+        + [
+            pl.BlockSpec((1, half, width), lambda t: (jnp.where(t <= TILE_AT[1][0], 0, 1), 1, 0)),
+            pl.BlockSpec((1, half, width), lambda t: (jnp.where(t <= TILE_AT[0][0], 0, 1), 0, 0)),
+            tile,
+        ]
+        + [hbm] * 13,
+        out_specs=[hbm] * 7,
         out_shape=outs,
-        scratch_shapes=[
+        scratch_shapes=[vmem(a.shape if a.ndim > 1 else (1, *a.shape), a.dtype) for a in early + later]
+        + [
             vmem((row_count, rows, cols), bf16),
             vmem((2, 2, 2, row_count * share, width), bf16),
             vmem((2, 8, width), f32),
             vmem((3, 2, 2, 2, 2, part // 2, width), bf16),
             vmem((2, row_count, half, width), bf16),
-            vmem((2, 2, 2, row_count, share, width), bf16),
+            vmem((row_count, 2, 2, 2, share, width), bf16),
             vmem((6, 8, width), f32),
             vmem((5, 8, width), f32),
             pltpu.SemaphoreType.DMA((kinds, 5)),
             pltpu.SemaphoreType.DMA((kinds, 5)),
-            pltpu.SemaphoreType.DMA((1 + row_count,)),
+            pltpu.SemaphoreType.DMA((18 + row_count,)),
         ]
         + folds
         + Halve.buffers(row_count * share, width, ("x", "z0", "z1")),
@@ -816,7 +899,7 @@
         ),
         name="rear",
     )(
-        qkv, qkv, qkv, grad, lse, delta, kaug, tokens, res_grad, *fixeds,
+        qkv, qkv, qkv, grad, lse, delta, kaug, inputs, next_x, res_grad, *early, outer_ab, outer_c, *later,
         share_views(inner, count), half_views(out, count),
     )
 
@@ -837,10 +920,11 @@
 
 def mid_kernel(
     half, fold_refs,
-    lengths, x_ref, mixed_ref, cot_ref, gx_ref, gcot_ref, out_w, inner_w, outer_w, bias_ref, gain_ref, shift_ref, heads_ref,
+    lengths, x_ref, next_x_ref, mixed_ref, cot_ref, next_cot_ref, gain_in, shift_in, bias_in, out_in, inner_in, outer_in, gx_in, gcot_in,
     mixed_all, lse_all,
     layer_o, res_o, grad_o, delta_o, gres_o, gout_o, ggrad_o, glse_o, gdelta_o, inner_o, outer_ab_o, outer_c_o, out_o,
     vectors_o,
+    gain_ref, shift_ref, bias_ref, out_w, inner_w, outer_w, gx_ref, gcot_ref, heads_ref,
     hidden, slope, normed, cot, att, proj, residual, outer_src, sums, bias_sums, layers,
     gout, ggrad, glse, gdelta, part_mixed, part_lse, send, recv, local, *scratch,
 ):
@@ -857,6 +941,7 @@
     strips = inner_w.shape[1] // width
     tiles = 2 * row_count
     fold = Fold(place, None, scratch, outer_src, Fold.EARLY)
+    held = pl.ds(pl.multiple_of(share * me, 16), share)
     following = {"seq": lax.rem(me + 1, count)}
     at = tuple(place[axis] for axis, _ in SEQ_BITS)
 
@@ -866,39 +951,53 @@
             (mixed_all.at[r, rows], part_mixed.at[m, r]) if n == 0 else (lse_all.at[r, rows], part_lse.at[m, r])
         )
 
-    part_copies, part_own = [], []
-    for r in range(row_count):
-        for n in range(2):
-            src, dst = parts(me, me, r, n)
-            part_own.append(pltpu.make_async_copy(src, dst, local.at[2 * r + n]))
-            for other in range(1, count):
-                to = lax.rem(me + other, count)
-                src, dst = parts(me, to, r, n)
-                part_copies.append(remote(src, dst, send.at[2 * r + n, other], recv.at[2 * r + n, other], {"seq": to}))
+    def part_copies():
+        copies = []
+        for r in range(row_count):
+            for n in range(2):
+                for other in range(1, count):
+                    to = lax.rem(me + other, count)
+                    src, dst = parts(me, to, r, n)
+                    sems = send.at[2 * r + n, other], recv.at[2 * r + n, other]
+                    copies.append(remote(src, dst, *sems, {"seq": to}))
+        return copies
+
+    def part_own():
+        return [
+            pltpu.make_async_copy(*parts(me, me, r, n), local.at[2 * r + n]) for r in range(row_count) for n in range(2)
+        ]
+
     base = 2 * row_count
     gathers = [
         Gather(place, buf, send.at[base + n], recv.at[base + n]) for n, buf in enumerate((gout, ggrad, glse, gdelta))
     ]
-    leaves = [
-        pltpu.make_async_copy(buf, o, local.at[base + n])
-        for n, (buf, o) in enumerate(((gout, gout_o), (ggrad, ggrad_o), (glse, glse_o), (gdelta, gdelta_o)))
-    ]
-    base += 4
-    home = [
-        remote(layers.at[1, r], layer_o.at[r, pl.ds(0, half)], send.at[base, r], recv.at[base, r], following)
-        for r in range(row_count)
-    ]
-    keep = [
-        pltpu.make_async_copy(layers.at[0, r], layer_o.at[r, pl.ds(half, half)], local.at[base + r]) for r in range(row_count)
-    ]
-    gain, shift = gain_ref[...], shift_ref[...]
+    leaves = lambda: fetch((gout, ggrad, glse, gdelta), (gout_o, ggrad_o, glse_o, gdelta_o), local, base)
+    ends = base + 4
+
+    def home(r):
+        return remote(layers.at[1, r], layer_o.at[r, pl.ds(0, half)], send.at[ends, r], recv.at[ends, r], following)
+
+    def keep(r):
+        return pltpu.make_async_copy(layers.at[0, r], layer_o.at[r, pl.ds(half, half)], local.at[ends + r])
+
+    loads = lambda: fetch(
+        (gain_in, shift_in, bias_in, out_in, inner_in, outer_in, gx_in.at[:, held], gcot_in.at[:, held]),
+        (gain_ref.at[0], shift_ref.at[0], bias_ref.at[0], out_w, inner_w, outer_w, gx_ref, gcot_ref), local, ends + row_count,
+    )
 
     @pl.when(step == 0)
     def _():
+        begin(loads())
         place.greet([{"seq": lax.rem(me + other, count)} for other in range(1, count)])
-        begin(part_own + part_copies)
+        begin(part_own() + part_copies())
+        lane = lax.broadcasted_iota(jnp.int32, (width, LANES), 1)
+        head = lax.div(lax.broadcasted_iota(jnp.int32, (width, LANES), 0), width // HEADS)
+        chosen = jnp.where(lane < 3 * HEADS, lax.rem(lane, HEADS), -1) == head
+        heads_ref[...] = jnp.where(chosen, 1.0, 0.0).astype(bf16)
         sums[...] = jnp.zeros_like(sums)
         bias_sums[...] = jnp.zeros_like(bias_sums)
+        for copy in loads():
+            copy.wait()
 
     def stats(values):
         centred = values - jnp.mean(values, axis=-1, keepdims=True)
@@ -910,7 +1009,7 @@
         total = x.astype(f32) + nn(attended, out_w[...])
         residual[rows] = total
         n, _ = stats(total)
-        second = (n * gain + shift).astype(bf16)
+        second = (n * gain_ref[...] + shift_ref[...]).astype(bf16)
         normed[rows] = second
 
         def run(j, total):
@@ -934,7 +1033,7 @@
 
         second_grad = lax.fori_loop(0, strips, run, jnp.zeros(cotangent.shape, f32))
         n, inv = stats(residual[rows])
-        eg = second_grad * gain
+        eg = second_grad * gain_ref[...]
         through = (eg - jnp.mean(eg, axis=-1, keepdims=True) - n * jnp.mean(eg * n, axis=-1, keepdims=True)) * inv
         sums[0] += sum_rows(second_grad * n)
         sums[1] += sum_rows(second_grad)
@@ -954,8 +1053,9 @@
         owner = lax.rem(me + h, count)
         spot = owner * block_len + (1 - h) * half + lax.broadcasted_iota(jnp.int32, (half, width), 0)
         valid = spot < lengths[r]
-        cot[rows] = jnp.where(valid, cot_ref[...].astype(f32), 0.0).astype(bf16)
-        final = forward(x_ref[...], mixed_ref[0], rows)
+        pick = lambda a, b: jnp.where(h == 0, a[0].astype(f32), b[0].astype(f32))
+        cot[rows] = jnp.where(valid, pick(cot_ref, next_cot_ref), 0.0).astype(bf16)
+        final = forward(pick(x_ref, next_x_ref), mixed_ref[0], rows)
         layers[h, r] = jnp.where(valid, final, 0.0).astype(bf16)
 
     back = step - (tiles + 2 + strips)
@@ -973,25 +1073,25 @@
 
         @pl.when(step == r)
         def _():
-            home[r].start()
+            home(r).start()
 
         @pl.when(step == row_count + r)
         def _():
-            keep[r].start()
+            keep(r).start()
 
     last = pl.ds(tokens, own_rows)
 
     @pl.when(step == tiles)
     def _():
-        for copy in part_own:
+        for copy in part_own():
             copy.wait()
-        for copy in part_copies:
+        for copy in part_copies():
             copy.wait_recv()
         peak = jnp.max(part_lse[...], axis=0)
         shares = jnp.exp(part_lse[...] - peak)
         total = jnp.sum(shares, axis=0)
         lse = peak + jnp.log(total)
-        glse[at] = lse
+        glse[(slice(None), *at)] = lse
         shares = (shares / total).reshape(count * own_rows, LANES)
         lane = lax.broadcasted_iota(jnp.int32, shares.shape, 1)
         shares = jnp.where(lane < HEADS, shares, 0.0)
@@ -1002,7 +1102,7 @@
         mixed = jnp.sum(mixed.reshape(count, own_rows, width), axis=0).astype(bf16)
         cot[last] = gcot_ref[...].reshape(own_rows, width)
         final = forward(gx_ref[...].reshape(own_rows, width), mixed, last)
-        gout[at] = final.astype(bf16).reshape(row_count, share, width)
+        gout[(slice(None), *at)] = final.astype(bf16).reshape(row_count, share, width)
         gathers[0].stage(0)
 
     strip_at = step - (tiles + 1)
@@ -1021,7 +1121,7 @@
             for g in chosen:
                 gathers[g].stage(n)
                 if n == 3:
-                    leaves[g].start()
+                    leaves()[g].start()
 
     for t, n in MID_TICKS.items():
 
@@ -1035,8 +1135,8 @@
     def _():
         res, grad, delta = backward(cot[last], last)
         gres_o[...] = res.reshape(row_count, share, width)
-        ggrad[at] = grad.reshape(row_count, share, width)
-        gdelta[at] = delta.reshape(row_count, share, LANES)
+        ggrad[(slice(None), *at)] = grad.reshape(row_count, share, width)
+        gdelta[(slice(None), *at)] = delta.reshape(row_count, share, LANES)
         for gather in gathers[1:]:
             gather.stage(0)
 
@@ -1058,21 +1158,20 @@
         first, second = fold.held()
         outer_ab_o[...] = fold.own[first]
         outer_c_o[...] = fold.own[second]
-        for copy in fold.core:
-            copy.wait_send()
-        for part in fold.parts:
-            for copy in part.copies.values():
-                copy.wait_send()
+        fold.finish()
         for gather in gathers:
             gather.finish()
-        for copy in part_copies:
+        for copy in part_copies():
             copy.wait_send()
-        for copy in keep + home + leaves:
+        for r in range(row_count):
+            keep(r).wait()
+            home(r).wait()
+        for copy in leaves():
             copy.wait()
 
 
 def mid(
-    lengths, tokens, mixed, lse, cotangent, own_globals, own_cot, out_weight, inner_weight, outer_weight, bias, gain, shift,
+    lengths, inputs, next_x, mixed, lse, cotangent, next_cot, globals_in, global_cot, out_weight, inner_weight, outer_weight, bias, gain, shift,
     half, count,
 ):
     f32, bf16 = jnp.float32, jnp.bfloat16
@@ -1085,8 +1184,6 @@
     part = width // count
     tiles = 2 * row_count
     total = row_count * block_len + own_rows
-    lane, head = jnp.arange(LANES), jnp.arange(width) // (width // HEADS)
-    heads = ((lane[None, :] % HEADS == head[:, None]) & (lane[None, :] < 3 * HEADS)).astype(bf16)
 
     def tile_at(first):
         def place(t):
@@ -1104,11 +1201,12 @@
 
         return pl.BlockSpec((half, cols), index)
 
-    fixed = lambda a: pl.BlockSpec(a.shape, lambda t: (0,) * a.ndim, pipeline_mode=pl.Buffered(1))
+    own_spec = pl.BlockSpec((1, half, width), lambda t: (jnp.clip(t - row_count, 0, row_count - 1), 1, 0))
+    next_spec = pl.BlockSpec((1, half, width), lambda t: (jnp.clip(t, 0, row_count - 1), 0, 0))
     whole = lambda *shape: pl.BlockSpec(shape, lambda t: (0,) * len(shape))
     hbm = pl.BlockSpec(memory_space=pl.ANY)
-    fixeds = (own_globals, own_cot, out_weight, inner_weight, outer_weight, bias[None], gain[None], shift[None], heads)
-    shared = (2, 2, 2, row_count, share)
+    fixeds = (gain, shift, bias, out_weight, inner_weight, outer_weight, globals_in, global_cot)
+    shared = (row_count, 2, 2, 2, share)
     after = 2 * tiles + 2 + strips
     of = jax.ShapeDtypeStruct
     outs = [
@@ -1135,12 +1233,13 @@
         grid=(after + strips + 1,),
         in_specs=[
             pl.BlockSpec(memory_space=pltpu.SMEM),
-            flat(forward_at, width),
+            own_spec,
+            next_spec,
             pl.BlockSpec((1, half, width), lambda t: (*forward_at(t), 0)),
-            flat(forward_at, width),
+            own_spec,
+            next_spec,
         ]
-        + [fixed(a) for a in fixeds]
-        + [hbm] * 2,
+        + [hbm] * (len(fixeds) + 2),
         out_specs=[
             hbm,
             flat(back_at, width),
@@ -1158,7 +1257,11 @@
             whole(2 + strips, width),
         ],
         out_shape=outs,
-        scratch_shapes=[
+        scratch_shapes=[vmem((1, a.shape[0]), f32) for a in fixeds[:3]]
+        + [vmem(a.shape, bf16) for a in fixeds[3:6]]
+        + [vmem((row_count, share, width), bf16)] * 2
+        + [
+            vmem((width, LANES), bf16),
             vmem((total, inner_width), bf16),
             vmem((total, inner_width), bf16),
             vmem((total, width), bf16),
@@ -1178,14 +1281,175 @@
             vmem((count, row_count, share, LANES), f32),
             pltpu.SemaphoreType.DMA((kinds, count)),
             pltpu.SemaphoreType.DMA((kinds, count)),
-            pltpu.SemaphoreType.DMA((kinds + row_count,)),
+            pltpu.SemaphoreType.DMA((kinds + row_count + len(fixeds),)),
         ]
         + fold,
         compiler_params=pltpu.CompilerParams(
             collective_id=10, has_side_effects=True, vmem_limit_bytes=64 * 1024 * 1024
         ),
         name="mid",
-    )(lengths, tokens, mixed, cotangent, *fixeds, mixed, lse)
+    )(lengths, inputs, next_x, mixed, cotangent, next_cot, *fixeds, mixed, lse)
+
+
+def key_marks(me, count, length, half, rows):
+    lane = lax.broadcasted_iota(jnp.int32, (rows, LANES), 1)
+    row = lax.broadcasted_iota(jnp.int32, (rows, LANES), 0)
+    kind = lane - TYPE0
+    side = jnp.where(row < half, 0, 1)
+    owner = lax.rem(me + side, count)
+    position = owner * (2 * half) + jnp.where(row < half, row + half, row - half)
+    apart = (me == count - 1) & (kind < 2) & (kind != side)
+    of_token = jnp.where((position >= length) | apart, NEG, 0.0)
+    of_global = jnp.where((kind == 2) & (me != 0), NEG, 0.0)
+    marks = jnp.where(row < 2 * half, of_token, of_global)
+    return jnp.where((kind >= 0) & (kind < 3), marks, 0.0).astype(jnp.bfloat16)
+
+
+def head_kernel(
+    half, scale, pairs, tq,
+    lengths, inputs, cotangent, globals_in, gain_in, shift_in, weight_in,
+    next_x, next_cot, qkv_o, mixed_o, lse_o, normed_o, kaug_o,
+    gain, shift, weight, xs, qkv, mixed, lse, normed, kaug, send, recv, local,
+):
+    bf16, f32 = jnp.bfloat16, jnp.float32
+    step = pl.program_id(0)
+    me, count = lax.axis_index("seq"), lax.axis_size("seq")
+    row_count, rows, width = xs.shape
+    block_len = 2 * half
+    previous = {"seq": lax.rem(me + count - 1, count)}
+    following = {"seq": lax.rem(me + 1, count)}
+    lower, upper, tail = pl.ds(0, half), pl.ds(half, half), pl.ds(block_len, rows - block_len)
+    turns = [row_count + 1 + r * (pairs + 1) for r in range(row_count)]
+
+    def arrive(r):
+        return remote(inputs.at[r, lower], xs.at[r, upper], send.at[0, r], recv.at[0, r], previous)
+
+    def arrive_cot(r):
+        return remote(cotangent.at[r, lower], next_cot.at[r], send.at[1, r], recv.at[1, r], previous)
+
+    def loads():
+        own = [(inputs.at[r, upper], xs.at[r, lower]) for r in range(row_count)]
+        own += [(globals_in.at[r], xs.at[r, tail]) for r in range(row_count)]
+        own += [(gain_in, gain.at[0]), (shift_in, shift.at[0]), (weight_in, weight)]
+        return fetch(*zip(*own), local)
+
+    def leaves(r):
+        pairs_of = ((qkv, qkv_o), (mixed, mixed_o), (lse, lse_o), (normed, normed_o), (kaug, kaug_o))
+        moved = [(a.at[r], b.at[r]) for a, b in pairs_of] + [(xs.at[r, upper], next_x.at[r])]
+        return fetch(*zip(*moved), local, 16 + 8 * r)
+
+    def project(x):
+        x = x.astype(f32)
+        centred = x - jnp.mean(x, axis=-1, keepdims=True)
+        inv = lax.rsqrt(jnp.mean(centred * centred, axis=-1, keepdims=True) + EPS)
+        n = (centred * inv * gain[...] + shift[...]).astype(bf16)
+        return n, nn(n, weight[...]).astype(bf16)
+
+    @pl.when(step == 0)
+    def _():
+        begin(loads())
+        barrier = pltpu.get_barrier_semaphore()
+        for to in (previous, following):
+            pl.semaphore_signal(barrier, inc=1, device_id=to, device_id_type=MESH_ID)
+        pl.semaphore_wait(barrier, 2)
+        begin([arrive(r) for r in range(row_count)])
+        for r in range(row_count):
+            kaug[r] = key_marks(me, count, lengths[r], half, rows)
+        for copy in loads():
+            copy.wait()
+
+    for r in range(row_count):
+
+        @pl.when(step == turns[r])
+        def _():
+            arrive(r).wait_recv()
+
+    first = turns[0]
+    is_turn = functools.reduce(jnp.logical_or, [step == t for t in turns])
+
+    @pl.when((step < row_count) | is_turn)
+    def _():
+        h = jnp.where(step < row_count, 0, 1)
+        r = jnp.where(step < row_count, step, lax.div(step - first, pairs + 1))
+        spot = pl.ds(pl.multiple_of(h * half, half), half)
+        normed[r, spot], qkv[r, spot] = project(xs[r, spot])
+
+    @pl.when(step == row_count)
+    def _():
+        n, p = project(jnp.concatenate([xs[r, tail] for r in range(row_count)], axis=0))
+        many = rows - block_len
+        for r in range(row_count):
+            normed[r, tail] = n[r * many:(r + 1) * many]
+            qkv[r, tail] = p[r * many:(r + 1) * many]
+
+    @pl.when(step == first + 1)
+    def _():
+        begin([arrive_cot(r) for r in range(row_count)])
+
+    @pl.when((step > first) & jnp.logical_not(is_turn))
+    def _():
+        r, p = lax.div(step - first, pairs + 1), lax.rem(step - first, pairs + 1) - 1
+        lane = lambda j: pl.ds(pl.multiple_of(j * width + p * LANES, LANES), LANES)
+        row = pl.ds(r, 1)
+        attend_kernel(
+            half, scale, tq, p, qkv.at[row, :, lane(0)], qkv.at[row, :, lane(1)], qkv.at[row, :, lane(2)], kaug.at[row],
+            mixed.at[row, :, lane(0)], lse.at[row],
+        )
+
+    for r in range(row_count):
+
+        @pl.when(step == turns[r] + pairs)
+        def _():
+            begin(leaves(r))
+
+    @pl.when(step == turns[-1] + pairs)
+    def _():
+        for r in range(row_count):
+            for copy in leaves(r):
+                copy.wait()
+            arrive(r).wait_send()
+            arrive_cot(r).wait()
+
+
+def head(lengths, inputs, cotangent, globals_in, gain, shift, weight, tq):
+    bf16, f32 = jnp.bfloat16, jnp.float32
+    row_count, block_len, width = inputs.shape
+    half = block_len // 2
+    rows = block_len + globals_in.shape[1]
+    pairs = width // LANES
+    scale = (width // HEADS) ** (-0.5)
+    hbm = pl.BlockSpec(memory_space=pl.ANY)
+    of, vmem = jax.ShapeDtypeStruct, pltpu.VMEM
+    results = [
+        ((row_count, rows, 3 * width), bf16),
+        ((row_count, rows, width), bf16),
+        ((row_count, rows, LANES), f32),
+        ((row_count, rows, width), bf16),
+        ((row_count, rows, LANES), bf16),
+    ]
+    return pl.pallas_call(
+        functools.partial(head_kernel, half, scale, pairs, tq),
+        grid=(row_count + 1 + row_count * (pairs + 1),),
+        in_specs=[pl.BlockSpec(memory_space=pltpu.SMEM)] + [hbm] * 6,
+        out_specs=[hbm] * 7,
+        out_shape=[of((row_count, half, width), bf16)] * 2 + [of(*r) for r in results],
+        scratch_shapes=[
+            vmem((1, width), f32),
+            vmem((1, width), f32),
+            vmem(weight.shape, bf16),
+            vmem((row_count, rows, width), bf16),
+        ]
+        + [vmem(*r) for r in results]
+        + [
+            pltpu.SemaphoreType.DMA((2, row_count)),
+            pltpu.SemaphoreType.DMA((2, row_count)),
+            pltpu.SemaphoreType.DMA((16 + 8 * row_count,)),
+        ],
+        compiler_params=pltpu.CompilerParams(
+            collective_id=11, has_side_effects=True, vmem_limit_bytes=60 * 1024 * 1024
+        ),
+        name="head",
+    )(lengths, inputs, cotangent, globals_in, gain, shift, weight)
 
 
 def wgrad_kernel(a_ref, b_ref, o_ref):
@@ -1294,6 +1558,33 @@
     share = global_count // count
     own_rows = row_count * share
 
+    if count == 8 and lax.axis_size("batch") == 4:
+        next_x, next_cot, qkv, mixed, lse, normed, kaug = head(
+            lengths, inputs, output_cotangent, global_inputs, first_gain, first_shift, qkv_weight, 320
+        )
+        (
+            layer_output, residual_grad, block_grad, block_delta, own_res, global_out, global_grad, global_lse, global_delta,
+            inner_wgrad, outer_ab, outer_c, out_grad, vectors,
+        ) = mid(
+            lengths, inputs, next_x, mixed, lse, output_cotangent, next_cot, global_inputs, global_cotangent, out_weight, inner_weight,
+            outer_weight, inner_bias, second_gain, second_shift, half, count,
+        )
+        input_out, global_grad, *reduced = rear(
+            qkv, block_grad, lse, block_delta, kaug, inputs, next_x, residual_grad, global_grad, global_lse, global_delta,
+            own_res, normed, global_inputs, qkv_weight, first_gain, vectors, outer_ab, outer_c, inner_wgrad,
+            out_grad, half, count,
+        )
+        joined = lambda a: a.reshape(row_count, global_count, width)
+        inner_out, outer_out, out_out, qkv_out, *lines, layer_output, input_out, global_out, global_grad = finish(
+            *reduced, layer_output, input_out, joined(global_out), joined(global_grad)
+        )
+        fg, fs, sg, ss, bias = (line.reshape(-1) for line in lines)
+        return (
+            layer_output, global_out, input_out, global_grad, fg, fs, qkv_out, out_out, sg, ss, inner_out, bias, outer_out,
+        )
+
+    own_globals = lax.dynamic_slice_in_dim(global_inputs, me * share, share, axis=1)
+    own_global_cot = lax.dynamic_slice_in_dim(global_cotangent, me * share, share, axis=1)
     next_inputs = lax.ppermute(inputs[:, :half], "seq", back)
     next_cotangent = lax.ppermute(output_cotangent[:, :half], "seq", back)
     block = jnp.concatenate([inputs[:, half:], next_inputs], axis=1)
@@ -1317,31 +1608,8 @@
     qkv = qkv.reshape(row_count, rows, 3 * width)
 
     mixed, lse = attend(qkv, kaug, half)
-    own_globals = lax.dynamic_slice_in_dim(global_inputs, me * share, share, axis=1)
-    own_global_cot = lax.dynamic_slice_in_dim(global_cotangent, me * share, share, axis=1)
     tokens_in = block.reshape(token_rows, width)
     cot_block = jnp.concatenate([output_cotangent[:, half:], next_cotangent], axis=1)
-    if count == 8 and lax.axis_size("batch") == 4:
-        (
-            layer_output, residual_grad, block_grad, block_delta, own_res, global_out, global_grad, global_lse, global_delta,
-            inner_wgrad, outer_ab, outer_c, out_grad, vectors,
-        ) = mid(
-            lengths, tokens_in, mixed, lse, cot_block.reshape(token_rows, width), own_globals, own_global_cot, out_weight,
-            inner_weight, outer_weight, inner_bias, second_gain, second_shift, half, count,
-        )
-        input_out, global_grad, inner_out, outer_out, out_out, qkv_out, small = rear(
-            qkv, block_grad, lse, block_delta, kaug, tokens_in, residual_grad, global_grad, global_lse, global_delta,
-            own_globals, own_res, normed, global_inputs, qkv_weight, first_gain[None], vectors, outer_ab, outer_c, inner_wgrad,
-            out_grad, half, count,
-        )
-        cut = lambda a: lax.dynamic_slice_in_dim(a, me * (a.shape[0] // count), a.shape[0] // count)
-        vectors_out = [cut(small[n]) for n in range(4)] + [cut(small[4:].reshape(-1))]
-        joined = lambda a: join_rows(a.reshape(count, own_rows, width), row_count)
-        return (
-            layer_output, joined(global_out), input_out, joined(global_grad), vectors_out[0], vectors_out[1], qkv_out,
-            out_out, vectors_out[2], vectors_out[3], inner_out, vectors_out[4], outer_out,
-        )
-
     part_mixed, part_lse = spread(
         [split_rows(mixed[:, block_len:], count), split_rows(lse[:, block_len:], count)], count, False, 0
     )

time: 308 us -> 266 us (0.86)
  local copies, waits for them, and re-layouts: 25.7 us -> 0 us
  Pallas kernels: 246 us -> 262 us
  waiting for transfers between devices: 12 us -> 0 us
  other arithmetic: 10.4 us -> 1.23 us
  matrix products: 6.54 us -> 0 us
  starting transfers between devices: 6.51 us -> 0 us
    pallas_call x1 -> x2, Pallas kernels: 27.9 us -> 55.1 us  [the longest x1 48.7 us: head(): pl.pallas_call(functools.partial(head_kernel, half, scale, pairs, tq), gr...]
    ppermute x2 -> x0, waiting for transfers between devices: 12 us -> none  [the longest x1 12 us: body(): next_inputs = lax.ppermute(inputs[:, :half], 'seq', back)]
    unnamed x46 -> x0, local copies, waits for them, and re-layouts: 10.7 us -> none
    pallas_call x1, Pallas kernels: 119 us -> 110 us  [rear(): pl.pallas_call(functools.partial(rear_kernel, half, scale, pairs, tuple(s...]
    dot_general x1 -> x0, matrix products: 6.54 us -> none  [nn(): return jnp.dot(a, b, preferred_element_type=jnp.float32)]
    ppermute x2 -> x0, starting transfers between devices: 6.51 us -> none  [the longest x1 5.98 us: body(): next_inputs = lax.ppermute(inputs[:, :half], 'seq', back)]
    slice x4 -> x0, local copies, waits for them, and re-layouts: 5.16 us -> none  [the longest x1 2.49 us: body(): block = jnp.concatenate([inputs[:, half:], next_inputs], axis=1)]
    convert_element_type x3 -> x0, other arithmetic: 5.04 us -> none  [the longest x2 4.19 us: body(): normed = (n_first * first_gain + first_shift).astype(bf16)]
  transfers between devices with their start and end apart: 2 -> 0, of which waited for: 1 -> 0; matrix products, arithmetic and copies ran while one was open for 5% -> 0% of each run, Pallas kernels for 9% -> 0%
where the time goes in v3:
time: 266 us; the launch traced here: 264 us
  Pallas kernels  262 us (98%)
    pallas_call x1, Pallas kernels, rear(): pl.pallas_call(functools.partial(rear_kernel, half, scale, pairs, tuple(s...  110 us
    pallas_call x1, Pallas kernels, mid(): pl.pallas_call(functools.partial(mid_kernel, half, len(fold)), grid=(afte...  96.7 us
    pallas_call x1, Pallas kernels, head(): pl.pallas_call(functools.partial(head_kernel, half, scale, pairs, tq), gr...  48.7 us
    pallas_call x1, Pallas kernels, finish(): pl.pallas_call(finish_kernel, in_specs=[vmem] * 9, out_specs=[vmem] * 9 +...  6.37 us

profile of v3, /device:TPU:0, one launch (start us, length us, event | category | flops | bytes accessed | tf_op | source)
XLA Modules:
  0.0 263.8 jit_solution(10955051713352580880)
XLA Ops:
  0.6 48.7 %head.1 = (bf16[2,256,768]{2,1,0:T(8,128)(2,1)}, bf16[2,256,768]{2,1,0:T(8,128)(2,1)}, bf16[2,640,2304]{2,1,0:T(8,128)(2,1)}, bf16[2,640,768]{2,1,0:T(8,128)(2,1...) custom-call(s32[2]{0:T(128)} %lengths.3, bf16[2,512,768]{2,1,0:T(8,128)(2,1)} %x_ref.3, ...), custom_call_target="tpu_custom_call" | custom-call | tf_op jit(solution)/shard_map/head/pallas_call | solution.py:1430
  49.3 96.7 %mid.1 = (bf16[2,512,768]{2,1,0:T(8,128)(2,1)}, f32[1024,768]{1,0:T(8,128)}, bf16[1024,768]{1,0:T(8,128)(2,1)}, f32[1024,128]{1,0:T(8,128)}, f32[2,16,768]{2,1,0...) custom-call(s32[2]{0:T(128)} %lengths.3, ...), custom_call_target="tpu_custom_call" | custom-call | tf_op jit(solution)/shard_map/mid/pallas_call | solution.py:1231
  146.0 110.2 %rear.1 = (bf16[2,512,768]{2,1,0:T(8,128)(2,1)}, bf16[2,2,2,2,16,768]{5,4,3,2,1,0:T(8,128)(2,1)}, bf16[2,192,768]{2,1,0:T(8,128)(2,1)}, bf16[2,96,768]{2,1,0:T(8...) custom-call(bf16[2,640,2304]{2,1,0:T(8,128)(2,1)} %get-tuple-element.54.q_ref.k_ref.v_ref, ...), custom_call_target="tpu_custom_call" | custom-call | tf_op jit(solution)/shard_map/rear/pallas_call | solution.py:866
  256.2 6.4 %finish.1 = (f32[96,3072]{1,0:T(8,128)}, f32[384,768]{1,0:T(8,128)}, f32[96,768]{1,0:T(8,128)}, f32[96,2304]{1,0:T(8,128)}, f32[1,96]{1,0:T(1,128)}, /*index=5*/...) custom-call(bf16[2,192,768]{2,1,0:T(8,128)(2,1)} %get-tuple-element., ...), custom_call_target="tpu_custom_call" | custom-call | tf_op jit(solution)/shard_map/finish/pallas_call | solution.py:579
  262.6 1.2 reduce

commit v4 on v3

--- a/solution.py
+++ b/solution.py
@@ -44,6 +44,7 @@
     for sel in (low_all, jnp.logical_not(low_all)):
         kx.append(jnp.concatenate([jnp.where(sel, k, zero), kaug], axis=1))
         vx.append(jnp.concatenate([jnp.where(sel, v, zero), jnp.where(sel, one, zero)], axis=1))
+    vx = jnp.concatenate(vx, axis=0)
     for start in range(0, rows, tq):
         lane = lax.broadcasted_iota(jnp.int32, (tq, LANES), 1)
         row = lax.broadcasted_iota(jnp.int32, (tq, LANES), 0) + start
@@ -51,15 +52,13 @@
         qaug = jnp.where(type_marks(rows, half, lane, row), one, zero)
         q = (q_ref[0, start:start + tq].astype(jnp.float32) * scale).astype(jnp.bfloat16)
         qx = jnp.concatenate([q, qaug], axis=1)
-        acc = None
-        peaks = []
+        probs, peaks = [], []
         for a in (0, 1):
             s = nt(qx, kx[a])
             peak = jnp.max(s, axis=1, keepdims=True)
-            p = jnp.exp(s - peak).astype(jnp.bfloat16)
-            part = nn(p, vx[a])
-            acc = part if acc is None else acc + part
+            probs.append(jnp.exp(s - peak).astype(jnp.bfloat16))
             peaks.append(peak)
+        acc = nn(jnp.concatenate(probs, axis=1), vx)
         total = acc[:, LANES:]
         o_ref[0, start:start + tq] = (acc[:, :LANES] / total).astype(jnp.bfloat16)
         lse = jnp.where(low, peaks[0], peaks[1]) + jnp.log(total)
@@ -119,8 +118,8 @@
     qx = jnp.concatenate([q, qaug], axis=1)
     gx = jnp.concatenate([g, gaug], axis=1)
     sels = (low, jnp.logical_not(low))
-    qh = [jnp.where(sel, q, zero) for sel in sels]
-    gh = [jnp.where(sel, g, zero) for sel in sels]
+    qh = jnp.concatenate([jnp.where(sel, q, zero) for sel in sels], axis=0)
+    gh = jnp.concatenate([jnp.where(sel, g, zero) for sel in sels], axis=0)
     dq = None
     for start in range(0, rows, tk):
         lane_k = lax.broadcasted_iota(jnp.int32, (tk, LANES), 1)
@@ -130,22 +129,19 @@
         k = k_ref[0, start:start + tk]
         v = v_ref[0, start:start + tk]
         kaug = kaug_ref[0, start:start + tk]
-        dk = dv = None
+        probs, grads, keys = [], [], []
         for a, sel in ((0, low_k), (1, jnp.logical_not(low_k))):
             marks = inside & (head == 2 * pair + a)
-            kh = jnp.where(sel, k, zero)
-            kx = jnp.concatenate([kh, jnp.where(marks, -one, kaug)], axis=1)
+            keys.append(jnp.where(sel, k, zero))
+            kx = jnp.concatenate([keys[a], jnp.where(marks, -one, kaug)], axis=1)
             vx = jnp.concatenate([jnp.where(sel, v, zero), jnp.where(marks, -one, zero)], axis=1)
             p = jnp.exp(nt(kx, qx))
-            ds = (p * nt(vx, gx)).astype(jnp.bfloat16)
-            part_v = nn(p.astype(jnp.bfloat16), gh[a])
-            part_k = nn(ds, qh[a])
-            part_q = tn(ds, kh)
-            dv = part_v if dv is None else dv + part_v
-            dk = part_k if dk is None else dk + part_k
-            dq = part_q if dq is None else dq + part_q
-        dk_ref[0, start:start + tk] = dk.astype(jnp.bfloat16)
-        dv_ref[0, start:start + tk] = dv.astype(jnp.bfloat16)
+            grads.append((p * nt(vx, gx)).astype(jnp.bfloat16))
+            probs.append(p.astype(jnp.bfloat16))
+        dv_ref[0, start:start + tk] = nn(jnp.concatenate(probs, axis=1), gh).astype(jnp.bfloat16)
+        dk_ref[0, start:start + tk] = nn(jnp.concatenate(grads, axis=1), qh).astype(jnp.bfloat16)
+        part = tn(jnp.concatenate(grads, axis=0), jnp.concatenate(keys, axis=0))
+        dq = part if dq is None else dq + part
     dq_ref[0] = (dq * scale).astype(jnp.bfloat16)
 
 
@@ -356,8 +352,8 @@
 
 PARTS = (
     ((0, 256), ("x", "y", "z0", "z1")),
-    ((256, 256), ("y", "x", "z0", "z1")),
-    ((512, 256), ("z0", "z1", "x", "y")),
+    ((256, 384), ("y", "x", "z0", "z1")),
+    ((640, 128), ("z0", "z1", "x", "y")),
 )
 
 
@@ -532,7 +528,7 @@
 
 
 def finish_kernel(
-    inner, late, keys, outer, small, layer, igrad, gout, ggrad,
+    inner, out, queries, keys, outer, small, layer, igrad, gout, ggrad,
     inner_o, outer_o, out_o, qkv_o, fg_o, fs_o, sg_o, ss_o, bias_o, layer_o, igrad_o, gout_o, ggrad_o, sems,
 ):
     f32 = jnp.float32
@@ -549,8 +545,8 @@
         outer_o[pl.ds(c * half, half)] = outer[c].astype(f32)
         spot = pl.ds(c * part // 2, part // 2)
         first, second = pl.ds(0, part // 2), pl.ds(part // 2, part // 2)
-        out_o[spot] = late[c, first].astype(f32)
-        for j, (ref, lines) in enumerate(((late, second), (keys, first), (keys, second))):
+        out_o[spot] = out[c, first].astype(f32)
+        for j, (ref, lines) in enumerate(((queries, first), (keys, first), (keys, second))):
             qkv_o[spot, pl.ds(j * width, width)] = ref[c, lines].astype(f32)
     values = small[...]
     turned = pltpu.roll(values, lax.rem(width - part * me, width), 1)
@@ -568,9 +564,9 @@
         copy.wait()
 
 
-def finish(inner, late, keys, outer, small, layer, igrad, gout, ggrad):
+def finish(inner, out, queries, keys, outer, small, layer, igrad, gout, ggrad):
     width = small.shape[1]
-    part = late.shape[1]
+    part = keys.shape[1]
     bias = 2 * outer.shape[1]
     vmem, hbm = pl.BlockSpec(memory_space=pltpu.VMEM), pl.BlockSpec(memory_space=pl.ANY)
     shapes = [(part, 2 * inner.shape[1] // part * width), (bias, width), (part, width), (part, 3 * width)]
@@ -578,14 +574,14 @@
     moved = [layer, igrad, gout, ggrad]
     return pl.pallas_call(
         finish_kernel,
-        in_specs=[vmem] * 9,
+        in_specs=[vmem] * 10,
         out_specs=[vmem] * 9 + [hbm] * 4,
         out_shape=[jax.ShapeDtypeStruct(s, jnp.float32) for s in shapes]
         + [jax.ShapeDtypeStruct(a.shape, a.dtype) for a in moved],
         scratch_shapes=[pltpu.SemaphoreType.DMA((4,))],
         compiler_params=pltpu.CompilerParams(vmem_limit_bytes=60 * 1024 * 1024),
         name="finish",
-    )(inner, late, keys, outer, small, *moved)
+    )(inner, out, queries, keys, outer, small, *moved)
 
 
 def begin(copies):
@@ -608,27 +604,27 @@
 
 
 TILE_AT = ((6, 0, 1), (7, 0, 0), (15, 1, 1), (19, 1, 0))
-GLOBALS_AT, STRIPS_AT, OWN_AT = 14, 16, 20
+GLOBALS_AT, STRIPS_AT, LAST = 14, 16, 20
 REAR_TICKS = {
-    0: ((0, 0),),
-    2: ((0, 1),),
-    3: ((3, 4),),
-    5: ((3, 5),),
-    6: ((0, 2),),
-    7: ((3, 6),),
-    8: ((3, 7),),
-    11: ((0, 3),),
-    14: ((0, 4),),
-    16: ((0, 5),),
-    17: ((1, 0),),
-    18: ((0, 6),),
-    19: ((1, 1), (2, 0), (0, 7)),
+    0: ((0, 0), (4, 0)),
+    3: ((0, 1),),
+    4: ((3, 4), (4, 1)),
+    8: ((3, 5),),
+    9: ((0, 2), (4, 2)),
+    10: ((3, 6),),
+    12: ((3, 7), (4, 3)),
+    13: ((0, 3),),
+    15: ((4, 4),),
+    17: ((0, 4), (1, 0)),
+    18: ((4, 5),),
+    19: ((0, 5), (1, 1), (2, 0)),
 }
 REAR_END = (
-    (2, 1), (5, 1), (1, 2), (4, 1), (2, 2), (1, 3), (5, 2), (4, 2), (2, 3), (5, 3), (1, 4), (4, 3), (5, 4), (2, 4), (5, 5), (1, 5), (2, 5), (1, 6),
-    (2, 6), (1, 7), (2, 7),
+    (7, 0), (5, 1), (2, 1), (7, 1), (1, 2), (4, 6), (0, 6), (5, 2), (6, 0), (2, 2), (7, 2), (1, 3), (0, 7), (4, 7), (6, 1),
+    (2, 3), (7, 3), (1, 4), (6, 2), (2, 4), (7, 4), (1, 5), (6, 3), (2, 5), (7, 5), (1, 6), (2, 6), (1, 7), (2, 7),
 )
-SPREAD_TICKS = {17: 0, 18: 1, 20: 2}
+SPREAD_AT = 18
+LONE = 64
 
 
 def rear_kernel(
@@ -636,7 +632,7 @@
     q_ref, k_ref, v_ref, g_ref, lse_ref, delta_ref, kaug_ref,
     x_ref, next_x_ref, res_ref, gg_in, glse_in, gdelta_in, outer_ab, outer_c, gres_in, globals_in, weight_in, gain_in, vectors_in,
     normed_in, inner, out,
-    igrad_o, ggrad_o, inner_o, late_o, keys_o, outer_o, small_o,
+    igrad_o, ggrad_o, inner_o, out_o, queries_o, keys_o, outer_o, small_o,
     gg_ref, glse_ref, gdelta_ref, gres_ref, globals_ref, weight_ref, gain_ref, vectors_ref, normed_ref,
     dqkv, gfirst, sums, qkv_src, grads, ggrad, value, got,
     send, recv, local, *scratch,
@@ -655,7 +651,7 @@
     half_part = part_rows // 2
     sources = (
         [(lambda c, j=j: inner.at[c * strips + j], part_rows) for j in range(strips)],
-        [(lambda c: out.at[:, :, :, c], half_part), (lambda c: qkv_src.at[0, :, :, :, c], half_part)],
+        [(lambda c: qkv_src.at[0, :, :, :, c], half_part)],
         [(lambda c, j=j: qkv_src.at[j, :, :, :, c], half_part) for j in (1, 2)],
     )
     folds, at = [], 0
@@ -664,6 +660,8 @@
         at += size
     folds.append(Fold(place, (), scratch[at:at + fold_refs[3]], None, Fold.LATE))
     at += fold_refs[3]
+    folds.append(Fold(place, [(lambda c: out.at[:, :, :, c], half_part)], scratch[at:at + fold_refs[4]]))
+    at += fold_refs[4]
     spread = Halve(place, gfirst, (0, width), ("x", "z0", "z1"), scratch[at:], send.at[0], recv.at[0], 0)
     gather = Gather(place, ggrad, send.at[row_count], recv.at[row_count])
     small = Sum(place, value, got, send.at[row_count + 1], recv.at[row_count + 1])
@@ -711,13 +709,14 @@
             *(dqkv.at[pl.ds(r, 1), :, spot] for spot in spots),
         )
 
-    for t, n in SPREAD_TICKS.items():
-
-        @pl.when(step == t)
-        def _():
-            spread.finish(n)
-            if n < 2:
-                spread.start(n + 1)
+    def move_spread(n):
+        spread.finish(n)
+        if n < 2:
+            spread.start(n + 1)
+
+    @pl.when(step == SPREAD_AT)
+    def _():
+        move_spread(0)
 
     @pl.when(step == TILE_AT[0][0])
     def _():
@@ -780,30 +779,37 @@
         def _():
             (home if h else keep)(r).start()
 
-    @pl.when(step == OWN_AT)
-    def _():
-        lines = [jnp.sum(sums[n], axis=0, keepdims=True) for n in range(2)]
-        value[0] = jnp.concatenate(lines + [vectors_ref[...]])
-        small.stage(0)
+    def own_globals():
         own_rows = row_count * share
         at = tuple(place[axis] for axis, _ in SEQ_BITS)
         held = pl.ds(pl.multiple_of(share * me, 16), share)
         n, inv = stats(globals_ref[:, held].astype(jnp.float32).reshape(own_rows, width))
         grad = gres_ref[...].reshape(own_rows, width) + through(gfirst[at].astype(jnp.float32), n, inv)
         ggrad[(slice(None), *at)] = grad.astype(jnp.bfloat16).reshape(row_count, share, width)
-        gather.stage(0)
-
-    @pl.when(step == OWN_AT + 1)
-    def _():
+
+    @pl.when(step == LAST)
+    def _():
+        lines = [jnp.sum(sums[n], axis=0, keepdims=True) for n in range(2)]
+        value[0] = jnp.concatenate(lines + [vectors_ref[...]])
         leaves = fetch(
-            (folds[0].done, folds[3].done, ggrad, folds[1].done, folds[2].done, value.at[5]),
-            (inner_o, outer_o, ggrad_o, late_o, keys_o, small_o), local, 12 + row_count,
+            (folds[0].done, folds[4].done, folds[1].done, folds[2].done, folds[3].done, value.at[5], ggrad),
+            (inner_o, out_o, queries_o, keys_o, outer_o, small_o, ggrad_o), local, 12 + row_count,
         )
-        begin(leaves[:2])
-        movers = folds + [gather, small]
+        ready = {(0, 7): 0, (4, 7): 1, (1, 7): 2, (2, 7): 3, (3, 7): 4, (7, 5): 5, (6, 3): 6}
+        leaves[4].start()
         for f, n in REAR_END:
-            movers[f].stage(n)
-        begin(leaves[2:])
+            if f == 5:
+                move_spread(n)
+                if n == 2:
+                    own_globals()
+            elif f == 6:
+                gather.stage(n)
+            elif f == 7:
+                small.stage(n)
+            else:
+                folds[f].stage(n)
+            if (f, n) in ready:
+                leaves[ready[f, n]].start()
         for fold in folds:
             fold.finish()
         gather.finish()
@@ -846,26 +852,27 @@
         jax.ShapeDtypeStruct((row_count, block_len, width), bf16),
         jax.ShapeDtypeStruct((row_count, 2, 2, 2, share, width), bf16),
         jax.ShapeDtypeStruct((2, 2 * part, width), bf16),
-        jax.ShapeDtypeStruct((2, part, width), bf16),
+        jax.ShapeDtypeStruct((2, LONE, width), bf16),
+        jax.ShapeDtypeStruct((2, LONE, width), bf16),
         jax.ShapeDtypeStruct((2, part, width), bf16),
         jax.ShapeDtypeStruct((2, 2 * part, width), bf16),
         jax.ShapeDtypeStruct((8, width), f32),
     ]
     folds, sizes = [], []
-    for size, pieces in ((2 * part, 2), (part, 2), (part, 2)):
+    for size, pieces in ((2 * part, 2), (LONE, 1), (part, 2)):
         refs = Fold.scratch(size, width, pieces)
         folds += refs
         sizes.append(len(refs))
-    refs = Fold.scratch(2 * part, width, 0, False, Fold.LATE)
-    folds += refs
-    sizes.append(len(refs))
+    for refs in (Fold.scratch(2 * part, width, 0, False, Fold.LATE), Fold.scratch(LONE, width, 1)):
+        folds += refs
+        sizes.append(len(refs))
     vmem = pltpu.VMEM
     kinds = 4 + row_count
     early = (global_grad, global_lse, global_delta)
     later = (own_res, globals_in, weight, gain, vectors, normed)
     return pl.pallas_call(
         functools.partial(rear_kernel, half, scale, pairs, tuple(sizes)),
-        grid=(OWN_AT + 2,),
+        grid=(LAST + 1,),
         in_specs=[spec(0), spec(pairs), spec(2 * pairs)]
         + [pl.BlockSpec((block_len, LANES), lambda t: (row_of(t), pair_of(t)))]
         + [pl.BlockSpec((1, block_len, LANES), lambda t: (row_of(t), 0, 0))]
@@ -876,7 +883,7 @@
             tile,
         ]
         + [hbm] * 13,
-        out_specs=[hbm] * 7,
+        out_specs=[hbm] * 8,
         out_shape=outs,
         scratch_shapes=[vmem(a.shape if a.ndim > 1 else (1, *a.shape), a.dtype) for a in early + later]
         + [
@@ -890,7 +897,7 @@
             vmem((5, 8, width), f32),
             pltpu.SemaphoreType.DMA((kinds, 5)),
             pltpu.SemaphoreType.DMA((kinds, 5)),
-            pltpu.SemaphoreType.DMA((18 + row_count,)),
+            pltpu.SemaphoreType.DMA((20 + row_count,)),
         ]
         + folds
         + Halve.buffers(row_count * share, width, ("x", "z0", "z1")),
@@ -1004,7 +1011,7 @@
         inv = lax.rsqrt(jnp.mean(centred * centred, axis=-1, keepdims=True) + EPS)
         return centred * inv, inv
 
-    def forward(x, attended, rows):
+    def forward(x, attended, rows, unroll=True):
         att[rows] = attended
         total = x.astype(f32) + nn(attended, out_w[...])
         residual[rows] = total
@@ -1021,9 +1028,9 @@
             slope[rows, strip] = (cdf + inner * bell * ((0.5 / math.pi) ** 0.5)).astype(bf16)
             return total + nn(active, outer_w[strip, :])
 
-        return lax.fori_loop(0, strips, run, total)
-
-    def backward(cotangent, rows):
+        return lax.fori_loop(0, strips, run, total, unroll=unroll)
+
+    def backward(cotangent, rows, unroll=True):
         def run(j, total):
             strip = pl.ds(pl.multiple_of(j * width, width), width)
             grad = (nt(cotangent, outer_w[strip, :]) * slope[rows, strip].astype(f32)).astype(bf16)
@@ -1031,7 +1038,7 @@
             bias_sums[j] += sum_rows(grad.astype(f32))
             return total + nt(grad, inner_w[:, strip])
 
-        second_grad = lax.fori_loop(0, strips, run, jnp.zeros(cotangent.shape, f32))
+        second_grad = lax.fori_loop(0, strips, run, jnp.zeros(cotangent.shape, f32), unroll=unroll)
         n, inv = stats(residual[rows])
         eg = second_grad * gain_ref[...]
         through = (eg - jnp.mean(eg, axis=-1, keepdims=True) - n * jnp.mean(eg * n, axis=-1, keepdims=True)) * inv
@@ -1101,7 +1108,7 @@
         mixed = wide * part_mixed[...].reshape(count * own_rows, width).astype(f32)
         mixed = jnp.sum(mixed.reshape(count, own_rows, width), axis=0).astype(bf16)
         cot[last] = gcot_ref[...].reshape(own_rows, width)
-        final = forward(gx_ref[...].reshape(own_rows, width), mixed, last)
+        final = forward(gx_ref[...].reshape(own_rows, width), mixed, last, False)
         gout[(slice(None), *at)] = final.astype(bf16).reshape(row_count, share, width)
         gathers[0].stage(0)
 
@@ -1133,7 +1140,7 @@
 
     @pl.when(step == tiles + 1 + strips)
     def _():
-        res, grad, delta = backward(cot[last], last)
+        res, grad, delta = backward(cot[last], last, False)
         gres_o[...] = res.reshape(row_count, share, width)
         ggrad[(slice(None), *at)] = grad.reshape(row_count, share, width)
         gdelta[(slice(None), *at)] = delta.reshape(row_count, share, LANES)
@@ -1220,8 +1227,8 @@
         of((*shared, LANES), f32),
         of((*shared, LANES), f32),
         of((strips, width, width), bf16),
-        of((2, 2, strips * part // 4, 512), bf16),
-        of((2, strips * part // 2, 256), bf16),
+        of((2, 2, strips * part // 4, 640), bf16),
+        of((2, strips * part // 2, 128), bf16),
         of((width, width), bf16),
         of((2 + strips, width), f32),
     ]
@@ -1352,7 +1359,7 @@
         for to in (previous, following):
             pl.semaphore_signal(barrier, inc=1, device_id=to, device_id_type=MESH_ID)
         pl.semaphore_wait(barrier, 2)
-        begin([arrive(r) for r in range(row_count)])
+        arrive(0).start()
         for r in range(row_count):
             kaug[r] = key_marks(me, count, lengths[r], half, rows)
         for copy in loads():
@@ -1363,6 +1370,8 @@
         @pl.when(step == turns[r])
         def _():
             arrive(r).wait_recv()
+            if r + 1 < row_count:
+                arrive(r + 1).start()
 
     first = turns[0]
     is_turn = functools.reduce(jnp.logical_or, [step == t for t in turns])
@@ -1382,7 +1391,7 @@
             normed[r, tail] = n[r * many:(r + 1) * many]
             qkv[r, tail] = p[r * many:(r + 1) * many]
 
-    @pl.when(step == first + 1)
+    @pl.when(step == first + 4)
     def _():
         begin([arrive_cot(r) for r in range(row_count)])
 

time: 266 us -> 247 us (0.929)
  Pallas kernels: 262 us -> 243 us
    pallas_call x1, Pallas kernels: 110 us -> 102 us  [rear(): pl.pallas_call(functools.partial(rear_kernel, half, scale, pairs, tuple(s...]
    pallas_call x1, Pallas kernels: 48.7 us -> 42.7 us  [head(): pl.pallas_call(functools.partial(head_kernel, half, scale, pairs, tq), gr...]
    pallas_call x1, Pallas kernels: 96.7 us -> 91.7 us  [mid(): pl.pallas_call(functools.partial(mid_kernel, half, len(fold)), grid=(afte...]
where the time goes in v4:
time: 247 us; the launch traced here: 245 us
  Pallas kernels  243 us (98%)
    pallas_call x1, Pallas kernels, rear(): pl.pallas_call(functools.partial(rear_kernel, half, scale, pairs, tuple(s...  102 us
    pallas_call x1, Pallas kernels, mid(): pl.pallas_call(functools.partial(mid_kernel, half, len(fold)), grid=(afte...  91.7 us
    pallas_call x1, Pallas kernels, head(): pl.pallas_call(functools.partial(head_kernel, half, scale, pairs, tq), gr...  42.7 us
    pallas_call x1, Pallas kernels, finish(): pl.pallas_call(finish_kernel, in_specs=[vmem] * 10, out_specs=[vmem] * 9...  6.46 us

profile of v4, /device:TPU:0, one launch (start us, length us, event | category | flops | bytes accessed | tf_op | source)
XLA Modules:
  0.0 244.8 jit_solution(15497586728364773441)
XLA Ops:
  0.6 42.7 %head.1 = (bf16[2,256,768]{2,1,0:T(8,128)(2,1)}, bf16[2,256,768]{2,1,0:T(8,128)(2,1)}, bf16[2,640,2304]{2,1,0:T(8,128)(2,1)}, bf16[2,640,768]{2,1,0:T(8,128)(2,1...) custom-call(s32[2]{0:T(128)} %lengths.3, bf16[2,512,768]{2,1,0:T(8,128)(2,1)} %x_ref.3, ...), custom_call_target="tpu_custom_call" | custom-call | tf_op jit(solution)/shard_map/head/pallas_call | solution.py:1439
  43.3 91.7 %mid.1 = (bf16[2,512,768]{2,1,0:T(8,128)(2,1)}, f32[1024,768]{1,0:T(8,128)}, bf16[1024,768]{1,0:T(8,128)(2,1)}, f32[1024,128]{1,0:T(8,128)}, f32[2,16,768]{2,1,0...) custom-call(s32[2]{0:T(128)} %lengths.3, ...), custom_call_target="tpu_custom_call" | custom-call | tf_op jit(solution)/shard_map/mid/pallas_call | solution.py:1238
  135.0 102.1 %rear.1 = (bf16[2,512,768]{2,1,0:T(8,128)(2,1)}, bf16[2,2,2,2,16,768]{5,4,3,2,1,0:T(8,128)(2,1)}, bf16[2,192,768]{2,1,0:T(8,128)(2,1)}, bf16[2,64,768]{2,1,0:T(8...) custom-call(bf16[2,640,2304]{2,1,0:T(8,128)(2,1)} %get-tuple-element, ...), custom_call_target="tpu_custom_call" | custom-call | tf_op jit(solution)/shard_map/rear/pallas_call | solution.py:873
  237.1 6.5 %finish.1 = (f32[96,3072]{1,0:T(8,128)}, f32[384,768]{1,0:T(8,128)}, f32[96,768]{1,0:T(8,128)}, f32[96,2304]{1,0:T(8,128)}, f32[1,96]{1,0:T(1,128)}, /*index=5*/...) custom-call(bf16[2,192,768]{2,1,0:T(8,128)(2,1)} %get-tuple-element., ...), custom_call_target="tpu_custom_call" | custom-call | tf_op jit(solution)/shard_map/finish/pallas_call | solution.py:575
  243.6 1.3 reduce

commit v5 on v4

--- a/solution.py
+++ b/solution.py
@@ -528,17 +528,25 @@
 
 
 def finish_kernel(
-    inner, out, queries, keys, outer, small, layer, igrad, gout, ggrad,
-    inner_o, outer_o, out_o, qkv_o, fg_o, fs_o, sg_o, ss_o, bias_o, layer_o, igrad_o, gout_o, ggrad_o, sems,
+    inner_in, out_in, queries_in, keys_in, outer_in, small_in, layer, igrad, gout, ggrad,
+    inner_o, outer_o, out_o, qkv_o, fg_o, fs_o, sg_o, ss_o, bias_o, layer_o, igrad_o, gout_o, ggrad_o,
+    inner, out, queries, keys, outer, small, *scratch,
 ):
+    *held, sems = scratch
     f32 = jnp.float32
     me = lax.axis_index("seq")
-    copies = fetch((layer, igrad, gout, ggrad), (layer_o, igrad_o, gout_o, ggrad_o), sems)
-    begin(copies)
+    moved = (layer, igrad, gout, ggrad)
+    own = fetch(
+        (inner_in, out_in, queries_in, keys_in, outer_in, small_in), (inner, out, queries, keys, outer, small), sems
+    )
+    into, away = fetch(moved, held, sems, 6), fetch(held, (layer_o, igrad_o, gout_o, ggrad_o), sems, 10)
+    begin(own + into)
     width = outer_o.shape[1]
     part = inner_o.shape[0]
-    strips = inner.shape[1] // part
+    strips = inner_o.shape[1] // width // 2
     half = outer.shape[1]
+    for copy in own:
+        copy.wait()
     for c in range(2):
         for j in range(strips):
             inner_o[:, pl.ds((c * strips + j) * width, width)] = inner[c, pl.ds(j * part, part)].astype(f32)
@@ -548,19 +556,22 @@
         out_o[spot] = out[c, first].astype(f32)
         for j, (ref, lines) in enumerate(((queries, first), (keys, first), (keys, second))):
             qkv_o[spot, pl.ds(j * width, width)] = ref[c, lines].astype(f32)
+    for copy, onward in zip(into, away):
+        copy.wait()
+        onward.start()
     values = small[...]
     turned = pltpu.roll(values, lax.rem(width - part * me, width), 1)
     for n, ref in enumerate((fg_o, fs_o, sg_o, ss_o)):
-        ref[...] = turned[n:n + 1, :part]
-    wide = bias_o.shape[1]
+        ref[...] = turned[n, :part]
+    wide = bias_o.shape[0]
     per = width // wide
     row = small[pl.ds(4 + lax.div(me, per), 1)]
-    spots = [row[:, n * wide:(n + 1) * wide] for n in range(per)]
+    spots = [row[0, n * wide:(n + 1) * wide] for n in range(per)]
     chosen = spots[0]
     for n in range(1, per):
         chosen = jnp.where(lax.rem(me, per) == n, spots[n], chosen)
     bias_o[...] = chosen
-    for copy in copies:
+    for copy in away:
         copy.wait()
 
 
@@ -569,19 +580,18 @@
     part = keys.shape[1]
     bias = 2 * outer.shape[1]
     vmem, hbm = pl.BlockSpec(memory_space=pltpu.VMEM), pl.BlockSpec(memory_space=pl.ANY)
-    shapes = [(part, 2 * inner.shape[1] // part * width), (bias, width), (part, width), (part, 3 * width)]
-    shapes += [(1, part)] * 4 + [(1, bias)]
-    moved = [layer, igrad, gout, ggrad]
+    shapes = [(part, 4 * width), (bias, width), (part, width), (part, 3 * width)] + [(part,)] * 4 + [(bias,)]
+    own, moved = [inner, out, queries, keys, outer, small], [layer, igrad, gout, ggrad]
     return pl.pallas_call(
         finish_kernel,
-        in_specs=[vmem] * 10,
+        in_specs=[hbm] * 10,
         out_specs=[vmem] * 9 + [hbm] * 4,
         out_shape=[jax.ShapeDtypeStruct(s, jnp.float32) for s in shapes]
         + [jax.ShapeDtypeStruct(a.shape, a.dtype) for a in moved],
-        scratch_shapes=[pltpu.SemaphoreType.DMA((4,))],
+        scratch_shapes=[pltpu.VMEM(a.shape, a.dtype) for a in own + moved] + [pltpu.SemaphoreType.DMA((14,))],
         compiler_params=pltpu.CompilerParams(vmem_limit_bytes=60 * 1024 * 1024),
         name="finish",
-    )(inner, out, queries, keys, outer, small, *moved)
+    )(*own, *moved)
 
 
 def begin(copies):
@@ -921,8 +931,9 @@
     return jnp.where(v < 0, tail, 1.0 - tail), bell
 
 
-MID_TICKS = {9: 0, 11: 1, 14: 2}
-MID_GATHERS = {6: (0, 1), 8: (0, 2), 10: (0, 3), 11: (1, 1), 12: (1, 2), 13: (1, 3)}
+STRIPS_FROM, BACK_FROM = 4, 8
+MID_TICKS = {8: 0, 9: 1, 13: 2}
+MID_GATHERS = {6: (0, 1), 8: (0, 2), 11: (0, 3), 10: (1, 1), 12: (1, 2), 15: (1, 3)}
 
 
 def mid_kernel(
@@ -1053,42 +1064,39 @@
         rest = (product - top.astype(f32)).astype(bf16)
         return res, grad, nn(top, heads_ref[...]) + nn(rest, heads_ref[...])
 
-    @pl.when(step < tiles)
-    def _():
-        r, h = lax.rem(step, row_count), 1 - lax.div(step, row_count)
-        rows = pl.ds(pl.multiple_of((2 * r + h) * half, half), half)
+    def turn(n):
+        return lax.div(n, 2), jnp.where(n == 0, 1, 0)
+
+    def is_valid(r, h):
         owner = lax.rem(me + h, count)
         spot = owner * block_len + (1 - h) * half + lax.broadcasted_iota(jnp.int32, (half, width), 0)
-        valid = spot < lengths[r]
+        return spot < lengths[r]
+
+    @pl.when(step < tiles - 1)
+    def _():
+        r, h = turn(step)
+        rows = pl.ds(pl.multiple_of((2 * r + h) * half, half), half)
+        valid = is_valid(r, h)
         pick = lambda a, b: jnp.where(h == 0, a[0].astype(f32), b[0].astype(f32))
         cot[rows] = jnp.where(valid, pick(cot_ref, next_cot_ref), 0.0).astype(bf16)
         final = forward(pick(x_ref, next_x_ref), mixed_ref[0], rows)
         layers[h, r] = jnp.where(valid, final, 0.0).astype(bf16)
 
-    back = step - (tiles + 2 + strips)
-
-    @pl.when((back >= 0) & (back < tiles))
-    def _():
-        r, h = lax.rem(back, row_count), 1 - lax.div(back, row_count)
+    back = step - (BACK_FROM + 1)
+
+    @pl.when((back >= 0) & (back < tiles - 1))
+    def _():
+        r, h = turn(back)
         rows = pl.ds(pl.multiple_of((2 * r + h) * half, half), half)
         res, grad, delta = backward(cot[rows], rows)
         res_o[...] = res
         grad_o[...] = grad
         delta_o[...] = delta
 
-    for r in range(row_count):
-
-        @pl.when(step == r)
-        def _():
-            home(r).start()
-
-        @pl.when(step == row_count + r)
-        def _():
-            keep(r).start()
-
-    last = pl.ds(tokens, own_rows)
-
-    @pl.when(step == tiles)
+    last_row = row_count - 1
+    joint = pl.ds(tokens - half, half + own_rows)
+
+    @pl.when(step == tiles - 1)
     def _():
         for copy in part_own():
             copy.wait()
@@ -1107,12 +1115,26 @@
         wide = nt(top, heads_ref[...]) + nt(rest, heads_ref[...])
         mixed = wide * part_mixed[...].reshape(count * own_rows, width).astype(f32)
         mixed = jnp.sum(mixed.reshape(count, own_rows, width), axis=0).astype(bf16)
-        cot[last] = gcot_ref[...].reshape(own_rows, width)
-        final = forward(gx_ref[...].reshape(own_rows, width), mixed, last, False)
-        gout[(slice(None), *at)] = final.astype(bf16).reshape(row_count, share, width)
+        valid = is_valid(last_row, 1)
+        local_cot = jnp.where(valid, next_cot_ref[0].astype(f32), 0.0).astype(bf16)
+        cot[joint] = jnp.concatenate([local_cot, gcot_ref[...].reshape(own_rows, width)], axis=0)
+        x = jnp.concatenate([next_x_ref[0], gx_ref[...].reshape(own_rows, width)], axis=0)
+        final = forward(x, jnp.concatenate([mixed_ref[0], mixed], axis=0), joint, False)
+        layers[1, last_row] = jnp.where(valid, final[:half], 0.0).astype(bf16)
+        gout[(slice(None), *at)] = final[half:].astype(bf16).reshape(row_count, share, width)
         gathers[0].stage(0)
 
-    strip_at = step - (tiles + 1)
+    @pl.when(step == 0)
+    def _():
+        home(0).start()
+
+    for t, h, r in ((1, 0, 0), (2, 0, 1), (3, 1, 1)):
+
+        @pl.when(step == t)
+        def _():
+            (home if h else keep)(r).start()
+
+    strip_at = step - STRIPS_FROM
 
     @pl.when((strip_at >= 0) & (strip_at < strips))
     def _():
@@ -1136,25 +1158,26 @@
         def _():
             fold.stage(n)
 
-    after = 2 * tiles + 1 + strips
-
-    @pl.when(step == tiles + 1 + strips)
-    def _():
-        res, grad, delta = backward(cot[last], last, False)
-        gres_o[...] = res.reshape(row_count, share, width)
-        ggrad[(slice(None), *at)] = grad.reshape(row_count, share, width)
-        gdelta[(slice(None), *at)] = delta.reshape(row_count, share, LANES)
+    after = BACK_FROM + tiles
+
+    @pl.when(step == BACK_FROM)
+    def _():
+        res, grad, delta = backward(cot[joint], joint, False)
+        res_o[...], gres_o[...] = res[:half], res[half:].reshape(row_count, share, width)
+        grad_o[...], delta_o[...] = grad[:half], delta[:half]
+        ggrad[(slice(None), *at)] = grad[half:].reshape(row_count, share, width)
+        gdelta[(slice(None), *at)] = delta[half:].reshape(row_count, share, LANES)
         for gather in gathers[1:]:
             gather.stage(0)
 
-    inner_at = step - (after + 1)
+    inner_at = step - after
 
     @pl.when((inner_at >= 0) & (inner_at < strips))
     def _():
         strip = pl.ds(pl.multiple_of(inner_at * width, width), width)
         inner_o[0] = tn(normed[...], slope[:, strip]).astype(bf16)
 
-    @pl.when(step == after + 1 + strips)
+    @pl.when(step == after + strips)
     def _():
         out_o[...] = tn(att[...], proj[...]).astype(bf16)
         lines = [jnp.sum(sums[n], axis=0, keepdims=True) for n in range(2)]
@@ -1192,29 +1215,20 @@
     tiles = 2 * row_count
     total = row_count * block_len + own_rows
 
-    def tile_at(first):
-        def place(t):
-            n = jnp.clip(t - first, 0, tiles - 1)
-            return n % row_count, 1 - n // row_count
-
-        return place
-
-    forward_at, back_at = tile_at(0), tile_at(tiles + 2 + strips)
-
-    def flat(where, cols):
+    def flat(cols):
         def index(t):
-            r, h = where(t)
-            return 2 * r + h, 0
+            n = t - BACK_FROM
+            return jnp.where(n <= 0, 3, jnp.where(n == 1, 1, jnp.where(n == 2, 0, 2))), 0
 
         return pl.BlockSpec((half, cols), index)
 
-    own_spec = pl.BlockSpec((1, half, width), lambda t: (jnp.clip(t - row_count, 0, row_count - 1), 1, 0))
-    next_spec = pl.BlockSpec((1, half, width), lambda t: (jnp.clip(t, 0, row_count - 1), 0, 0))
+    own_spec = pl.BlockSpec((1, half, width), lambda t: (jnp.where(t <= 1, 0, 1), 1, 0))
+    next_spec = pl.BlockSpec((1, half, width), lambda t: (jnp.where(t <= 0, 0, 1), 0, 0))
     whole = lambda *shape: pl.BlockSpec(shape, lambda t: (0,) * len(shape))
     hbm = pl.BlockSpec(memory_space=pl.ANY)
     fixeds = (gain, shift, bias, out_weight, inner_weight, outer_weight, globals_in, global_cot)
     shared = (row_count, 2, 2, 2, share)
-    after = 2 * tiles + 2 + strips
+    after = BACK_FROM + tiles
     of = jax.ShapeDtypeStruct
     outs = [
         of((row_count, block_len, width), bf16),
@@ -1242,16 +1256,16 @@
             pl.BlockSpec(memory_space=pltpu.SMEM),
             own_spec,
             next_spec,
-            pl.BlockSpec((1, half, width), lambda t: (*forward_at(t), 0)),
+            pl.BlockSpec((1, half, width), lambda t: (jnp.where(t <= 1, 0, 1), jnp.where((t == 0) | (t >= 3), 1, 0), 0)),
             own_spec,
             next_spec,
         ]
         + [hbm] * (len(fixeds) + 2),
         out_specs=[
             hbm,
-            flat(back_at, width),
-            flat(back_at, width),
-            flat(back_at, LANES),
+            flat(width),
+            flat(width),
+            flat(LANES),
             whole(row_count, share, width),
             hbm,
             hbm,
@@ -1587,7 +1601,7 @@
         inner_out, outer_out, out_out, qkv_out, *lines, layer_output, input_out, global_out, global_grad = finish(
             *reduced, layer_output, input_out, joined(global_out), joined(global_grad)
         )
-        fg, fs, sg, ss, bias = (line.reshape(-1) for line in lines)
+        fg, fs, sg, ss, bias = lines
         return (
             layer_output, global_out, input_out, global_grad, fg, fs, qkv_out, out_out, sg, ss, inner_out, bias, outer_out,
         )

time: 247 us -> 235 us (0.951)
  Pallas kernels: 243 us -> 232 us
    pallas_call x1, Pallas kernels: 91.7 us -> 83.7 us  [mid(): pl.pallas_call(functools.partial(mid_kernel, half, len(fold)), grid=(afte...]
where the time goes in v5:
time: 235 us; the launch traced here: 233 us
  Pallas kernels  232 us (99%)
    pallas_call x1, Pallas kernels, rear(): pl.pallas_call(functools.partial(rear_kernel, half, scale, pairs, tuple(s...  100 us
    pallas_call x1, Pallas kernels, mid(): pl.pallas_call(functools.partial(mid_kernel, half, len(fold)), grid=(afte...  83.7 us
    pallas_call x1, Pallas kernels, head(): pl.pallas_call(functools.partial(head_kernel, half, scale, pairs, tq), gr...  42.7 us
    pallas_call x1, Pallas kernels, finish(): pl.pallas_call(finish_kernel, in_specs=[hbm] * 10, out_specs=[vmem] * 9 +...  5.84 us

profile of v5, /device:TPU:0, one launch (start us, length us, event | category | flops | bytes accessed | tf_op | source)
XLA Modules:
  0.0 233.3 jit_solution(15404244312413194204)
XLA Ops:
  0.6 42.7 %head.1 = (bf16[2,256,768]{2,1,0:T(8,128)(2,1)}, bf16[2,256,768]{2,1,0:T(8,128)(2,1)}, bf16[2,640,2304]{2,1,0:T(8,128)(2,1)}, bf16[2,640,768]{2,1,0:T(8,128)(2,1...) custom-call(s32[2]{0:T(128)} %lengths.3, bf16[2,512,768]{2,1,0:T(8,128)(2,1)} %x_ref.3, ...), custom_call_target="tpu_custom_call" | custom-call | tf_op jit(solution)/shard_map/head/pallas_call | solution.py:1453
  43.3 83.7 %mid.1 = (bf16[2,512,768]{2,1,0:T(8,128)(2,1)}, f32[1024,768]{1,0:T(8,128)}, bf16[1024,768]{1,0:T(8,128)(2,1)}, f32[1024,128]{1,0:T(8,128)}, f32[2,16,768]{2,1,0...) custom-call(s32[2]{0:T(128)} %lengths.3, ...), custom_call_target="tpu_custom_call" | custom-call | tf_op jit(solution)/shard_map/mid/pallas_call | solution.py:1252
  127.0 100.3 %rear.1 = (bf16[2,512,768]{2,1,0:T(8,128)(2,1)}, bf16[2,2,2,2,16,768]{5,4,3,2,1,0:T(8,128)(2,1)}, bf16[2,192,768]{2,1,0:T(8,128)(2,1)}, bf16[2,64,768]{2,1,0:T(8...) custom-call(bf16[2,640,2304]{2,1,0:T(8,128)(2,1)} %get-tuple-element, ...), custom_call_target="tpu_custom_call" | custom-call | tf_op jit(solution)/shard_map/rear/pallas_call | solution.py:883
  227.3 5.8 %finish.1 = (f32[96,3072]{1,0:T(8,128)}, f32[384,768]{1,0:T(8,128)}, f32[96,768]{1,0:T(8,128)}, f32[96,2304]{1,0:T(8,128)}, f32[96]{0:T(128)}, /*index=5*/f32[96...) custom-call(bf16[2,192,768]{2,1,0:T(8,128)(2,1)} %get-tuple-element., ...), custom_call_target="tpu_custom_call" | custom-call | tf_op jit(solution)/shard_map/finish/pallas_call | solution.py:585

commit v6 on v5

--- a/solution.py
+++ b/solution.py
@@ -528,17 +528,15 @@
 
 
 def finish_kernel(
-    inner_in, out_in, queries_in, keys_in, outer_in, small_in, layer, igrad, gout, ggrad,
+    inner_in, late_in, keys_in, outer_in, small_in, layer, igrad, gout, ggrad,
     inner_o, outer_o, out_o, qkv_o, fg_o, fs_o, sg_o, ss_o, bias_o, layer_o, igrad_o, gout_o, ggrad_o,
-    inner, out, queries, keys, outer, small, *scratch,
+    inner, late, keys, outer, small, *scratch,
 ):
     *held, sems = scratch
     f32 = jnp.float32
     me = lax.axis_index("seq")
     moved = (layer, igrad, gout, ggrad)
-    own = fetch(
-        (inner_in, out_in, queries_in, keys_in, outer_in, small_in), (inner, out, queries, keys, outer, small), sems
-    )
+    own = fetch((inner_in, late_in, keys_in, outer_in, small_in), (inner, late, keys, outer, small), sems)
     into, away = fetch(moved, held, sems, 6), fetch(held, (layer_o, igrad_o, gout_o, ggrad_o), sems, 10)
     begin(own + into)
     width = outer_o.shape[1]
@@ -553,8 +551,8 @@
         outer_o[pl.ds(c * half, half)] = outer[c].astype(f32)
         spot = pl.ds(c * part // 2, part // 2)
         first, second = pl.ds(0, part // 2), pl.ds(part // 2, part // 2)
-        out_o[spot] = out[c, first].astype(f32)
-        for j, (ref, lines) in enumerate(((queries, first), (keys, first), (keys, second))):
+        out_o[spot] = late[c, first].astype(f32)
+        for j, (ref, lines) in enumerate(((late, second), (keys, first), (keys, second))):
             qkv_o[spot, pl.ds(j * width, width)] = ref[c, lines].astype(f32)
     for copy, onward in zip(into, away):
         copy.wait()
@@ -575,16 +573,16 @@
         copy.wait()
 
 
-def finish(inner, out, queries, keys, outer, small, layer, igrad, gout, ggrad):
+def finish(inner, late, keys, outer, small, layer, igrad, gout, ggrad):
     width = small.shape[1]
     part = keys.shape[1]
     bias = 2 * outer.shape[1]
     vmem, hbm = pl.BlockSpec(memory_space=pltpu.VMEM), pl.BlockSpec(memory_space=pl.ANY)
     shapes = [(part, 4 * width), (bias, width), (part, width), (part, 3 * width)] + [(part,)] * 4 + [(bias,)]
-    own, moved = [inner, out, queries, keys, outer, small], [layer, igrad, gout, ggrad]
+    own, moved = [inner, late, keys, outer, small], [layer, igrad, gout, ggrad]
     return pl.pallas_call(
         finish_kernel,
-        in_specs=[hbm] * 10,
+        in_specs=[hbm] * 9,
         out_specs=[vmem] * 9 + [hbm] * 4,
         out_shape=[jax.ShapeDtypeStruct(s, jnp.float32) for s in shapes]
         + [jax.ShapeDtypeStruct(a.shape, a.dtype) for a in moved],
@@ -613,28 +611,25 @@
                 folds[f].stage(n)
 
 
-TILE_AT = ((6, 0, 1), (7, 0, 0), (15, 1, 1), (19, 1, 0))
-GLOBALS_AT, STRIPS_AT, LAST = 14, 16, 20
+TILE_AT = ((6, 0, 1), (7, 0, 0), (18, 1, 1), (19, 1, 0))
+STRIPS_AT, GLOBALS_AT, LAST = 15, 14, 20
 REAR_TICKS = {
-    0: ((0, 0), (4, 0)),
+    0: ((0, 0),),
     3: ((0, 1),),
-    4: ((3, 4), (4, 1)),
+    4: ((3, 4),),
     8: ((3, 5),),
-    9: ((0, 2), (4, 2)),
+    9: ((0, 2),),
     10: ((3, 6),),
-    12: ((3, 7), (4, 3)),
+    12: ((3, 7),),
     13: ((0, 3),),
-    15: ((4, 4),),
-    17: ((0, 4), (1, 0)),
-    18: ((4, 5),),
-    19: ((0, 5), (1, 1), (2, 0)),
+    16: ((1, 0),),
+    18: ((0, 4), (2, 0), (1, 1)),
+    19: ((0, 5),),
 }
 REAR_END = (
-    (7, 0), (5, 1), (2, 1), (7, 1), (1, 2), (4, 6), (0, 6), (5, 2), (6, 0), (2, 2), (7, 2), (1, 3), (0, 7), (4, 7), (6, 1),
-    (2, 3), (7, 3), (1, 4), (6, 2), (2, 4), (7, 4), (1, 5), (6, 3), (2, 5), (7, 5), (1, 6), (2, 6), (1, 7), (2, 7),
+    (7, 0), (2, 1), (5, 0), (1, 2), (7, 1), (5, 1), (2, 2), (0, 6), (1, 3), (7, 2), (5, 2), (6, 0), (2, 3), (0, 7), (1, 4),
+    (7, 3), (6, 1), (2, 4), (1, 5), (7, 4), (6, 2), (2, 5), (1, 6), (7, 5), (6, 3), (2, 6), (1, 7), (2, 7),
 )
-SPREAD_AT = 18
-LONE = 64
 
 
 def rear_kernel(
@@ -642,7 +637,7 @@
     q_ref, k_ref, v_ref, g_ref, lse_ref, delta_ref, kaug_ref,
     x_ref, next_x_ref, res_ref, gg_in, glse_in, gdelta_in, outer_ab, outer_c, gres_in, globals_in, weight_in, gain_in, vectors_in,
     normed_in, inner, out,
-    igrad_o, ggrad_o, inner_o, out_o, queries_o, keys_o, outer_o, small_o,
+    igrad_o, ggrad_o, inner_o, late_o, keys_o, outer_o, small_o,
     gg_ref, glse_ref, gdelta_ref, gres_ref, globals_ref, weight_ref, gain_ref, vectors_ref, normed_ref,
     dqkv, gfirst, sums, qkv_src, grads, ggrad, value, got,
     send, recv, local, *scratch,
@@ -661,7 +656,7 @@
     half_part = part_rows // 2
     sources = (
         [(lambda c, j=j: inner.at[c * strips + j], part_rows) for j in range(strips)],
-        [(lambda c: qkv_src.at[0, :, :, :, c], half_part)],
+        [(lambda c: out.at[:, :, :, c], half_part), (lambda c: qkv_src.at[0, :, :, :, c], half_part)],
         [(lambda c, j=j: qkv_src.at[j, :, :, :, c], half_part) for j in (1, 2)],
     )
     folds, at = [], 0
@@ -670,8 +665,6 @@
         at += size
     folds.append(Fold(place, (), scratch[at:at + fold_refs[3]], None, Fold.LATE))
     at += fold_refs[3]
-    folds.append(Fold(place, [(lambda c: out.at[:, :, :, c], half_part)], scratch[at:at + fold_refs[4]]))
-    at += fold_refs[4]
     spread = Halve(place, gfirst, (0, width), ("x", "z0", "z1"), scratch[at:], send.at[0], recv.at[0], 0)
     gather = Gather(place, ggrad, send.at[row_count], recv.at[row_count])
     small = Sum(place, value, got, send.at[row_count + 1], recv.at[row_count + 1])
@@ -724,10 +717,6 @@
         if n < 2:
             spread.start(n + 1)
 
-    @pl.when(step == SPREAD_AT)
-    def _():
-        move_spread(0)
-
     @pl.when(step == TILE_AT[0][0])
     def _():
         for copy in later():
@@ -802,11 +791,11 @@
         lines = [jnp.sum(sums[n], axis=0, keepdims=True) for n in range(2)]
         value[0] = jnp.concatenate(lines + [vectors_ref[...]])
         leaves = fetch(
-            (folds[0].done, folds[4].done, folds[1].done, folds[2].done, folds[3].done, value.at[5], ggrad),
-            (inner_o, out_o, queries_o, keys_o, outer_o, small_o, ggrad_o), local, 12 + row_count,
+            (folds[0].done, folds[1].done, folds[2].done, folds[3].done, value.at[5], ggrad),
+            (inner_o, late_o, keys_o, outer_o, small_o, ggrad_o), local, 12 + row_count,
         )
-        ready = {(0, 7): 0, (4, 7): 1, (1, 7): 2, (2, 7): 3, (3, 7): 4, (7, 5): 5, (6, 3): 6}
-        leaves[4].start()
+        ready = {(0, 7): 0, (1, 7): 1, (2, 7): 2, (7, 5): 4, (6, 3): 5}
+        leaves[3].start()
         for f, n in REAR_END:
             if f == 5:
                 move_spread(n)
@@ -862,20 +851,19 @@
         jax.ShapeDtypeStruct((row_count, block_len, width), bf16),
         jax.ShapeDtypeStruct((row_count, 2, 2, 2, share, width), bf16),
         jax.ShapeDtypeStruct((2, 2 * part, width), bf16),
-        jax.ShapeDtypeStruct((2, LONE, width), bf16),
-        jax.ShapeDtypeStruct((2, LONE, width), bf16),
+        jax.ShapeDtypeStruct((2, part, width), bf16),
         jax.ShapeDtypeStruct((2, part, width), bf16),
         jax.ShapeDtypeStruct((2, 2 * part, width), bf16),
         jax.ShapeDtypeStruct((8, width), f32),
     ]
     folds, sizes = [], []
-    for size, pieces in ((2 * part, 2), (LONE, 1), (part, 2)):
+    for size, pieces in ((2 * part, 2), (part, 2), (part, 2)):
         refs = Fold.scratch(size, width, pieces)
         folds += refs
         sizes.append(len(refs))
-    for refs in (Fold.scratch(2 * part, width, 0, False, Fold.LATE), Fold.scratch(LONE, width, 1)):
-        folds += refs
-        sizes.append(len(refs))
+    refs = Fold.scratch(2 * part, width, 0, False, Fold.LATE)
+    folds += refs
+    sizes.append(len(refs))
     vmem = pltpu.VMEM
     kinds = 4 + row_count
     early = (global_grad, global_lse, global_delta)
@@ -893,7 +881,7 @@
             tile,
         ]
         + [hbm] * 13,
-        out_specs=[hbm] * 8,
+        out_specs=[hbm] * 7,
         out_shape=outs,
         scratch_shapes=[vmem(a.shape if a.ndim > 1 else (1, *a.shape), a.dtype) for a in early + later]
         + [

time: 235 us -> 230 us (0.979)
  Pallas kernels: 232 us -> 229 us
    pallas_call x1, Pallas kernels: 100 us -> 96.4 us  [rear(): pl.pallas_call(functools.partial(rear_kernel, half, scale, pairs, tuple(s...]
where the time goes in v6:
time: 230 us; the launch traced here: 229 us
  Pallas kernels  229 us (100%)
    pallas_call x1, Pallas kernels, rear(): pl.pallas_call(functools.partial(rear_kernel, half, scale, pairs, tuple(s...  96.4 us
    pallas_call x1, Pallas kernels, mid(): pl.pallas_call(functools.partial(mid_kernel, half, len(fold)), grid=(afte...  83.6 us
    pallas_call x1, Pallas kernels, head(): pl.pallas_call(functools.partial(head_kernel, half, scale, pairs, tq), gr...  42.8 us
    pallas_call x1, Pallas kernels, finish(): pl.pallas_call(finish_kernel, in_specs=[hbm] * 9, out_specs=[vmem] * 9 +...  5.81 us

profile of v6, /device:TPU:0, one launch (start us, length us, event | category | flops | bytes accessed | tf_op | source)
XLA Modules:
  0.0 229.4 jit_solution(8234459663164805350)
XLA Ops:
  0.6 42.8 %head.1 = (bf16[2,256,768]{2,1,0:T(8,128)(2,1)}, bf16[2,256,768]{2,1,0:T(8,128)(2,1)}, bf16[2,640,2304]{2,1,0:T(8,128)(2,1)}, bf16[2,640,768]{2,1,0:T(8,128)(2,1...) custom-call(s32[2]{0:T(128)} %lengths.3, bf16[2,512,768]{2,1,0:T(8,128)(2,1)} %x_ref.3, ...), custom_call_target="tpu_custom_call" | custom-call | tf_op jit(solution)/shard_map/head/pallas_call | solution.py:1441
  43.4 83.6 %mid.1 = (bf16[2,512,768]{2,1,0:T(8,128)(2,1)}, f32[1024,768]{1,0:T(8,128)}, bf16[1024,768]{1,0:T(8,128)(2,1)}, f32[1024,128]{1,0:T(8,128)}, f32[2,16,768]{2,1,0...) custom-call(s32[2]{0:T(128)} %lengths.3, ...), custom_call_target="tpu_custom_call" | custom-call | tf_op jit(solution)/shard_map/mid/pallas_call | solution.py:1240
  127.1 96.4 %rear.1 = (bf16[2,512,768]{2,1,0:T(8,128)(2,1)}, bf16[2,2,2,2,16,768]{5,4,3,2,1,0:T(8,128)(2,1)}, bf16[2,192,768]{2,1,0:T(8,128)(2,1)}, bf16[2,96,768]{2,1,0:T(8...) custom-call(bf16[2,640,2304]{2,1,0:T(8,128)(2,1)} %get-tuple-element.54.q_ref.k_ref.v_ref, ...), custom_call_target="tpu_custom_call" | custom-call | tf_op jit(solution)/shard_map/rear/pallas_call | solution.py:871
  223.4 5.8 %finish.1 = (f32[96,3072]{1,0:T(8,128)}, f32[384,768]{1,0:T(8,128)}, f32[96,768]{1,0:T(8,128)}, f32[96,2304]{1,0:T(8,128)}, f32[96]{0:T(128)}, /*index=5*/f32[96...) custom-call(bf16[2,192,768]{2,1,0:T(8,128)(2,1)} %get-tuple-element., ...), custom_call_target="tpu_custom_call" | custom-call | tf_op jit(solution)/shard_map/finish/pallas_call | solution.py:583
